TPU v7x, 32 devices: a whole 2x2x4 slice. The times are simulated.
32 devices in a mesh: dp: 8 (over y, x, core), tensor: 4 (over z).
Axes of the slice: x: 2, y: 2, z: 4, core: 2. Of those that a mesh axis runs over, the one named last changes fastest.
Arguments:
- tokens: bfloat16 [8192, 1024], P(('dp', 'tensor')), may hold values from -6 to 6
- cotangent: bfloat16 [8192, 1024], P(('dp', 'tensor')), may hold values from -6 to 6
- doc_lengths: int32 [8, 8], P('dp'), may hold values from 1 to 832, 1024 in all within a row
- query_weight: bfloat16 [1024, 1024], P('dp', 'tensor'), may hold values from -0.1875 to 0.1875
- key_weight: bfloat16 [1024, 1024], P('dp', 'tensor'), may hold values from -0.1875 to 0.1875
- value_weight: bfloat16 [1024, 1024], P('dp', 'tensor'), may hold values from -0.1875 to 0.1875
- output_weight: bfloat16 [1024, 1024], P('tensor', 'dp'), may hold values from -3 to 3
- inner_weight: bfloat16 [1024, 4096], P('dp', 'tensor'), may hold values from -0.1875 to 0.1875
- outer_weight: bfloat16 [4096, 1024], P('tensor', 'dp'), may hold values from -0.09375 to 0.09375
- query_offset: bfloat16 [1024], P(('tensor', 'dp')), may hold values from -3 to 3
- value_offset: bfloat16 [1024], P(('tensor', 'dp')), may hold values from -3 to 3
- inner_offset: bfloat16 [4096], P(('tensor', 'dp')), may hold values from -3 to 3
- output_offset: bfloat16 [1024], P(('dp', 'tensor')), may hold values from -3 to 3
- outer_offset: bfloat16 [1024], P(('dp', 'tensor')), may hold values from -3 to 3
- first_gain: bfloat16 [1024], P(('dp', 'tensor')), may hold values from 0.25 to 1.75
- first_shift: bfloat16 [1024], P(('dp', 'tensor')), may hold values from -3 to 3
- second_gain: bfloat16 [1024], P(('dp', 'tensor')), may hold values from 0.25 to 1.75
- second_shift: bfloat16 [1024], P(('dp', 'tensor')), may hold values from -3 to 3
Outputs:
- layer_out: bfloat16 [8192, 1024], P(('dp', 'tensor'))
- tokens_grad: float32 [8192, 1024], P(('dp', 'tensor'))
- query_grad: float32 [1024, 1024], P('dp', 'tensor')
- key_grad: float32 [1024, 1024], P('dp', 'tensor')
- value_grad: float32 [1024, 1024], P('dp', 'tensor')
- output_grad: float32 [1024, 1024], P('tensor', 'dp')
- inner_grad: float32 [1024, 4096], P('dp', 'tensor')
- outer_grad: float32 [4096, 1024], P('tensor', 'dp')
- offset_query: float32 [1024], P(('tensor', 'dp'))
- offset_value: float32 [1024], P(('tensor', 'dp'))
- offset_inner: float32 [4096], P(('tensor', 'dp'))
- offset_output: float32 [1024], P(('dp', 'tensor'))
- offset_outer: float32 [1024], P(('dp', 'tensor'))
- gain_first: float32 [1024], P(('dp', 'tensor'))
- shift_first: float32 [1024], P(('dp', 'tensor'))
- gain_second: float32 [1024], P(('dp', 'tensor'))
- shift_second: float32 [1024], P(('dp', 'tensor'))
Inputs may be any that keep to these rules, and one draw needn't show every extreme that they name: `doc_lengths`: row s lists, in order, the lengths of the 8 documents packed into sequence s; they sum to 1024, and the longest has exactly 832 tokens.
All inputs are finite; a program needn't handle non-finite values.
Results may differ from a plain program's by a relative error of at most 0.018.
Values may be sent and summed in bfloat16 or wider, within the bound.
No kernel may reach another device: no remote copies, remote signals or barrier semaphores. Data moves between devices by JAX's collectives and lax.ppermute only.
A program may use at most 128 MiB of HBM per device.

v0:
```python
import jax
import jax.numpy as jnp
from jax import lax
from jax.sharding import PartitionSpec as P

HEAD_DIM = 64
LENGTH = 1024


def norm_rows(value, gain, shift):
    centered = value - jnp.mean(value, -1, keepdims=True)
    scale = lax.rsqrt(jnp.mean(centered * centered, -1, keepdims=True) + 1e-05)
    normed = centered * scale
    return (normed * gain + shift, normed, scale)


def norm_back(grad, normed, scale, gain):
    scaled = grad * gain
    return scale * (
        scaled
        - jnp.mean(scaled, -1, keepdims=True)
        - normed * jnp.mean(scaled * normed, -1, keepdims=True)
    )


def gelu_slope(inner):
    return (
        0.5 * (1.0 + lax.erf(inner * 0.7071067811865476))
        + inner * jnp.exp(-0.5 * inner * inner) * 0.3989422804014327
    )


def segment_ids(doc_lengths):
    bounds = jnp.cumsum(doc_lengths, axis=1)
    places = jnp.arange(LENGTH, dtype=jnp.int32)
    return jnp.sum((places[None, :, None] >= bounds[:, None, :]).astype(jnp.int32), -1)


def masked_scores(block_rows, keys, own, segment):
    scores = (
        jnp.einsum("qhd,khd->hqk", block_rows, keys, preferred_element_type=jnp.float32) * 0.125
    )
    same = (own[:, None] == segment[None, :])[None]
    return jnp.where(same, scores, -1e30)


def attend_sequence(queries, keys, values, segment, block):
    count = LENGTH // block

    def one_block(index):
        start = index * block
        block_rows = lax.dynamic_slice_in_dim(queries, start, block, 0)
        own = lax.dynamic_slice_in_dim(segment, start, block, 0)
        scores = masked_scores(block_rows, keys, own, segment)
        top = jnp.max(scores, -1, keepdims=True)
        expo = jnp.exp(scores - top)
        total = jnp.sum(expo, -1, keepdims=True)
        shares = (expo / total).astype(jnp.bfloat16)
        mixed = jnp.einsum(
            "hqk,khd->qhd", shares, values, preferred_element_type=jnp.float32
        ).astype(jnp.bfloat16)
        return (mixed, (top + jnp.log(total))[..., 0])

    mixed, logsum = lax.map(one_block, jnp.arange(count))
    return (mixed.reshape(LENGTH, queries.shape[1], queries.shape[2]), logsum)


def attend_back(queries, keys, values, segment, outgrad, logsum, block):
    count = LENGTH // block

    def advance(carry, item):
        key_total, value_total = carry
        index, block_sum = item
        start = index * block
        block_rows = lax.dynamic_slice_in_dim(queries, start, block, 0)
        own = lax.dynamic_slice_in_dim(segment, start, block, 0)
        block_grad = lax.dynamic_slice_in_dim(outgrad, start, block, 0)
        scores = masked_scores(block_rows, keys, own, segment)
        shares = jnp.exp(scores - block_sum[..., None])
        rounded = shares.astype(jnp.bfloat16)
        value_total = value_total + jnp.einsum(
            "hqk,qhd->khd", rounded, block_grad, preferred_element_type=jnp.float32
        )
        dots = jnp.einsum("qhd,khd->hqk", block_grad, values, preferred_element_type=jnp.float32)
        centre = jnp.sum(shares * dots, -1, keepdims=True)
        score_back = (shares * (dots - centre)).astype(jnp.bfloat16)
        query_back = (
            jnp.einsum("hqk,khd->qhd", score_back, keys, preferred_element_type=jnp.float32) * 0.125
        ).astype(jnp.bfloat16)
        key_total = (
            key_total
            + jnp.einsum("hqk,qhd->khd", score_back, block_rows, preferred_element_type=jnp.float32)
            * 0.125
        )
        return ((key_total, value_total), query_back)

    zeros = jnp.zeros(keys.shape, jnp.float32)
    (key_total, value_total), query_back = lax.scan(
        advance, (zeros, zeros), (jnp.arange(count), logsum)
    )
    return (
        query_back.reshape(keys.shape),
        key_total.astype(jnp.bfloat16),
        value_total.astype(jnp.bfloat16),
    )


def body(
    tokens,
    cotangent,
    doc_lengths,
    query_weight,
    key_weight,
    value_weight,
    output_weight,
    inner_weight,
    outer_weight,
    query_offset,
    value_offset,
    inner_offset,
    output_offset,
    outer_offset,
    first_gain,
    first_shift,
    second_gain,
    second_shift,
):
    (
        query_full,
        key_full,
        value_full,
        output_full,
        inner_full,
        outer_full,
        query_bias,
        value_bias,
        inner_bias,
    ) = (
        lax.all_gather(query_weight, "dp", axis=0, tiled=True),
        lax.all_gather(key_weight, "dp", axis=0, tiled=True),
        lax.all_gather(value_weight, "dp", axis=0, tiled=True),
        lax.all_gather(output_weight, "dp", axis=1, tiled=True),
        lax.all_gather(inner_weight, "dp", axis=0, tiled=True),
        lax.all_gather(outer_weight, "dp", axis=1, tiled=True),
        lax.all_gather(query_offset, "dp", axis=0, tiled=True),
        lax.all_gather(value_offset, "dp", axis=0, tiled=True),
        lax.all_gather(inner_offset, "dp", axis=0, tiled=True),
    )
    vector_list = (
        lax.all_gather(output_offset, ("dp", "tensor"), axis=0, tiled=True),
        lax.all_gather(outer_offset, ("dp", "tensor"), axis=0, tiled=True),
        lax.all_gather(first_gain, ("dp", "tensor"), axis=0, tiled=True),
        lax.all_gather(first_shift, ("dp", "tensor"), axis=0, tiled=True),
        lax.all_gather(second_gain, ("dp", "tensor"), axis=0, tiled=True),
        lax.all_gather(second_shift, ("dp", "tensor"), axis=0, tiled=True),
    )
    output_bias, outer_bias, gain_one, shift_one, gain_two, shift_two = [
        piece.astype(jnp.float32) for piece in vector_list
    ]
    segment = segment_ids(doc_lengths)
    seqs = doc_lengths.shape[0]
    heads = query_full.shape[1] // HEAD_DIM
    block = min(512, LENGTH)
    shape = (seqs, LENGTH, heads, HEAD_DIM)
    gathered = lax.all_gather(tokens, "tensor", axis=0, tiled=True)
    queries = (
        jnp.dot(gathered, query_full, preferred_element_type=jnp.float32)
        + query_bias.astype(jnp.float32)
    ).astype(jnp.bfloat16)
    keys = jnp.dot(gathered, key_full, preferred_element_type=jnp.float32).astype(jnp.bfloat16)
    values = (
        jnp.dot(gathered, value_full, preferred_element_type=jnp.float32)
        + value_bias.astype(jnp.float32)
    ).astype(jnp.bfloat16)
    queries = queries.reshape(shape)
    keys = keys.reshape(shape)
    values = values.reshape(shape)
    mixed, logsum = lax.map(
        lambda item: attend_sequence(item[0], item[1], item[2], item[3], block),
        (queries, keys, values, segment),
    )
    flat = mixed.reshape(-1, heads * HEAD_DIM)
    first_in = (
        tokens.astype(jnp.float32)
        + lax.psum_scatter(
            jnp.dot(flat, output_full, preferred_element_type=jnp.float32),
            "tensor",
            scatter_dimension=0,
            tiled=True,
        )
        + output_bias
    )
    hidden, first_normed, first_scale = norm_rows(first_in, gain_one, shift_one)
    hidden_full = lax.all_gather(hidden.astype(jnp.bfloat16), "tensor", axis=0, tiled=True)
    inner = jnp.dot(
        hidden_full, inner_full, preferred_element_type=jnp.float32
    ) + inner_bias.astype(jnp.float32)
    active = jax.nn.gelu(inner, approximate=False).astype(jnp.bfloat16)
    second_in = (
        hidden
        + lax.psum_scatter(
            jnp.dot(active, outer_full, preferred_element_type=jnp.float32),
            "tensor",
            scatter_dimension=0,
            tiled=True,
        )
        + outer_bias
    )
    result, second_normed, second_scale = norm_rows(second_in, gain_two, shift_two)
    upstream = cotangent.astype(jnp.float32)
    second_grad = norm_back(upstream, second_normed, second_scale, gain_two)
    mlp_rows = lax.all_gather(second_grad.astype(jnp.bfloat16), "tensor", axis=0, tiled=True)
    weight_outer = jnp.einsum("rf,rd->fd", active, mlp_rows, preferred_element_type=jnp.float32)
    inner_back = (
        jnp.einsum("rd,fd->rf", mlp_rows, outer_full, preferred_element_type=jnp.float32)
        * gelu_slope(inner)
    ).astype(jnp.bfloat16)
    bias_inner = jnp.sum(inner_back, 0, dtype=jnp.float32)
    weight_inner = jnp.einsum(
        "rd,rf->df", hidden_full, inner_back, preferred_element_type=jnp.float32
    )
    hidden_grad = second_grad + lax.psum_scatter(
        jnp.einsum("rf,df->rd", inner_back, inner_full, preferred_element_type=jnp.float32).astype(
            jnp.bfloat16
        ),
        "tensor",
        scatter_dimension=0,
        tiled=True,
    ).astype(jnp.float32)
    first_grad = norm_back(hidden_grad, first_normed, first_scale, gain_one)
    partials = jnp.stack(
        [
            jnp.sum(first_grad, 0),
            jnp.sum(second_grad, 0),
            jnp.sum(hidden_grad * first_normed, 0),
            jnp.sum(hidden_grad, 0),
            jnp.sum(upstream * second_normed, 0),
            jnp.sum(upstream, 0),
        ]
    )
    attn_rows = lax.all_gather(first_grad.astype(jnp.bfloat16), "tensor", axis=0, tiled=True)
    weight_output = jnp.einsum("rh,rd->hd", flat, attn_rows, preferred_element_type=jnp.float32)
    mixed_grad = jnp.einsum(
        "rd,hd->rh", attn_rows, output_full, preferred_element_type=jnp.float32
    ).astype(jnp.bfloat16)
    query_back, key_back, value_back = lax.map(
        lambda item: attend_back(item[0], item[1], item[2], item[3], item[4], item[5], block),
        (queries, keys, values, segment, mixed_grad.reshape(shape), logsum),
    )
    query_back = query_back.reshape(-1, heads * HEAD_DIM)
    key_back = key_back.reshape(-1, heads * HEAD_DIM)
    value_back = value_back.reshape(-1, heads * HEAD_DIM)
    bias_query = jnp.sum(query_back, 0, dtype=jnp.float32)
    bias_value = jnp.sum(value_back, 0, dtype=jnp.float32)
    weight_query = jnp.einsum("rd,rh->dh", gathered, query_back, preferred_element_type=jnp.float32)
    weight_key = jnp.einsum("rd,rh->dh", gathered, key_back, preferred_element_type=jnp.float32)
    weight_value = jnp.einsum("rd,rh->dh", gathered, value_back, preferred_element_type=jnp.float32)
    tokens_grad = first_grad + lax.psum_scatter(
        (
            jnp.einsum("rh,dh->rd", query_back, query_full, preferred_element_type=jnp.float32)
            + jnp.einsum("rh,dh->rd", key_back, key_full, preferred_element_type=jnp.float32)
            + jnp.einsum("rh,dh->rd", value_back, value_full, preferred_element_type=jnp.float32)
        ).astype(jnp.bfloat16),
        "tensor",
        scatter_dimension=0,
        tiled=True,
    ).astype(jnp.float32)
    vector_sums = lax.psum_scatter(partials, ("dp", "tensor"), scatter_dimension=1, tiled=True)
    sent = (
        lax.psum_scatter(weight_query, "dp", scatter_dimension=0, tiled=True),
        lax.psum_scatter(weight_key, "dp", scatter_dimension=0, tiled=True),
        lax.psum_scatter(weight_value, "dp", scatter_dimension=0, tiled=True),
        lax.psum_scatter(weight_output, "dp", scatter_dimension=1, tiled=True),
        lax.psum_scatter(weight_inner, "dp", scatter_dimension=0, tiled=True),
        lax.psum_scatter(weight_outer, "dp", scatter_dimension=1, tiled=True),
        lax.psum_scatter(bias_query, "dp", scatter_dimension=0, tiled=True),
        lax.psum_scatter(bias_value, "dp", scatter_dimension=0, tiled=True),
        lax.psum_scatter(bias_inner, "dp", scatter_dimension=0, tiled=True),
    )
    return (
        result.astype(jnp.bfloat16),
        tokens_grad,
        sent[0],
        sent[1],
        sent[2],
        sent[3],
        sent[4],
        sent[5],
        sent[6],
        sent[7],
        sent[8],
        vector_sums[0],
        vector_sums[1],
        vector_sums[2],
        vector_sums[3],
        vector_sums[4],
        vector_sums[5],
    )


def solution(mesh):
    return jax.shard_map(
        body,
        mesh=mesh,
        in_specs=(
            P(("dp", "tensor"), None),
            P(("dp", "tensor"), None),
            P("dp", None),
            P("dp", "tensor"),
            P("dp", "tensor"),
            P("dp", "tensor"),
            P("tensor", "dp"),
            P("dp", "tensor"),
            P("tensor", "dp"),
            P(("tensor", "dp")),
            P(("tensor", "dp")),
            P(("tensor", "dp")),
            P(("dp", "tensor")),
            P(("dp", "tensor")),
            P(("dp", "tensor")),
            P(("dp", "tensor")),
            P(("dp", "tensor")),
            P(("dp", "tensor")),
        ),
        out_specs=(
            P(("dp", "tensor"), None),
            P(("dp", "tensor"), None),
            P("dp", "tensor"),
            P("dp", "tensor"),
            P("dp", "tensor"),
            P("tensor", "dp"),
            P("dp", "tensor"),
            P("tensor", "dp"),
            P(("tensor", "dp")),
            P(("tensor", "dp")),
            P(("tensor", "dp")),
            P(("dp", "tensor")),
            P(("dp", "tensor")),
            P(("dp", "tensor")),
            P(("dp", "tensor")),
            P(("dp", "tensor")),
            P(("dp", "tensor")),
        ),
        check_vma=False,
    )
```

profile of v0, /device:TPU:0, one launch (start us, length us, event | category | flops | bytes accessed | tf_op | source)
XLA Modules:
  0.0 924.6 jit_solution(12674874646503975845)
XLA Ops:
  13.3 15.5 %all-reduce.13 = (bf16[256]{0:T(256)(128)(2,1)S(1)}, bf16[256]{0:T(256)(128)(2,1)S(1)}) all-reduce(bf16[256]{0:T(256)(128)(2,1)S(1)} %dynamic-update-slice, bf16[256]{0:T(256)(128)(2,1)S(1)} %dynamic-update-slice.1), channel_id=1, replica_groups=mesh['dp'=8,'tensor'=4] {'dp'}, use_global_device_ids=true, to_apply=%add | all-reduce | flops 512 | bytes 2048
  29.0 9.2 all_gather.58
  38.1 9.5 %all_gather.60 = bf16[1024,256]{1,0:T(8,128)(2,1)S(1)} all-gather(bf16[128,256]{1,0:T(8,128)(2,1)} %param.26), channel_id=1, replica_groups=mesh['dp'=8,'tensor'=4] {'dp'}, dimensions={0}, use_global_device_ids=true | all-gather | bytes 589824 | tf_op jit(solution)/shard_map/all_gather | solution.py:140
  47.7 9.2 all_gather.61
  56.8 9.6 %all_gather.63 = bf16[256,1024]{1,0:T(8,128)(2,1)S(1)} all-gather(bf16[256,128]{1,0:T(8,128)(2,1)} %param.28), channel_id=1, replica_groups=mesh['dp'=8,'tensor'=4] {'dp'}, dimensions={1}, use_global_device_ids=true | all-gather | bytes 589824 | tf_op jit(solution)/shard_map/all_gather | solution.py:142
  66.5 2.6 convolution_convert_fusion.2
  69.1 2.3 fusion.57
  72.3 17.6 %while.47 = (s32[]{:T(128)}, bf16[2,512,4,64]{1,3,2,0:T(8,128)(2,1)S(1)}, f32[2,4,512]{2,1,0:T(4,128)S(1)}, s32[2]{0:T(128)S(1)}, s32[1024]{0:T(1024)S(1)}, /*in...) while((s32[]{:T(128)}, ...), condition=%wide.region_5.6_spmd, body=%wide.region_2.5_spmd.sunk | while | flops 562690048 | bytes 28911816 | solution.py:64
  75.7 2.3 fusion.143
  78.0 3.0 fusion.144
  84.5 2.3 fusion.143
  86.8 3.0 fusion.144
  91.3 2.8 fusion.72
  96.7 44.6 %all-reduce.12 = (bf16[1024]{0:T(1024)(128)(2,1)S(1)}, bf16[1024]{0:T(1024)(128)(2,1)S(1)}, bf16[1024]{0:T(1024)(128)(2,1)S(1)}, bf16[1024]{0:T(1024)(128)(2,1)S...) all-reduce(bf16[1024]{0:T(1024)(128)(2,1)S(1)} %dynamic-update-slic, ...), channel_id=1, replica_groups=mesh['dp'=8,'tensor'=4] {'dp','tensor'}, use_global_device_ids=true, to_apply=%add.2 | all-reduce | flops 6144 | bytes 24576
  141.3 31.1 %reduce-scatter.14.cloned.1.call-done = f32[256,1024]{1,0:T(8,128)} async-done(((f32[1024,1024]{1,0:T(8,128)}), f32[256,1024]{1,0:T(8,128)}) %reduce-scatter.14.cloned.1.call-update) | async-done | bytes 1048592 | tf_op jit(solution)/shard_map/reduce_scatter | solution.py:185
  175.9 8.7 all-gather
  184.6 36.8 %all-gather.10.cloned.1.call-done = bf16[1024,1024]{1,0:T(8,128)(2,1)} async-done(((bf16[256,1024]{1,0:T(8,128)(2,1)}), bf16[1024,1024]{1,0:T(8,128)(2,1)}) %all-gather.10.cloned.1.call-update) | async-done | bytes 2097168 | tf_op jit(solution)/shard_map/all_gather | solution.py:194
  221.4 14.5 %fusion.40 = (bf16[1024,1024]{1,0:T(8,128)(2,1)}, f32[1024,1024]{1,0:T(8,128)}) fusion(f32[1024]{0:T(1024)S(1)} %bitcast.162, bf16[1024,1024]{1,0:T(8,128)(2,1)} %all-gather.10.cloned.1.call-done, bf16[1024,1024]{1,0:T(8,128)(2,1)} %all-gather.12.cloned.1.call-done), kind=kOutput, calls=%fused_computation.49 | convolution fusion | flops 2216689664 | bytes 10489856 | tf_op jit(solution)/shard_map/dot_general | solution.py:195
  235.9 14.2 %all-gather.14.cloned.1.call-done = bf16[1024,1024]{1,0:T(8,128)(2,1)} async-done(((bf16[1024,128]{1,0:T(8,128)(2,1)}), bf16[1024,1024]{1,0:T(8,128)(2,1)}) %all-gather.14.cloned.1.call-update) | async-done | bytes 2097168 | tf_op jit(solution)/shard_map/all_gather | solution.py:144
  250.1 6.6 fusion.73
  256.8 76.8 %reduce-scatter.16.cloned.1.call-done = f32[256,1024]{1,0:T(8,128)} async-done(((f32[1024,1024]{1,0:T(8,128)}), f32[256,1024]{1,0:T(8,128)}) %reduce-scatter.16.cloned.1.call-update) | async-done | bytes 1048592 | tf_op jit(solution)/shard_map/reduce_scatter | solution.py:201
  337.9 46.5 %all-gather.16.cloned.1.call-done = bf16[1024,1024]{1,0:T(8,128)(2,1)} async-done(((bf16[256,1024]{1,0:T(8,128)(2,1)}), bf16[1024,1024]{1,0:T(8,128)(2,1)}) %all-gather.16.cloned.1.call-update) | async-done | bytes 2097168 | tf_op jit(solution)/shard_map/all_gather | solution.py:212
  384.4 6.6 convert_reduce_fusion
  392.4 3.7 convolution_convert_fusion
  396.2 42.7 %reduce-scatter.18.cloned.1.call-done = bf16[256,1024]{1,0:T(8,128)(2,1)} async-done(((bf16[1024,1024]{1,0:T(8,128)(2,1)}), bf16[256,1024]{1,0:T(8,128)(2,1)}) %reduce-scatter.18.cloned.1.call-update) | async-done | bytes 524304 | tf_op jit(solution)/shard_map/reduce_scatter | solution.py:222
  446.0 44.6 %all-gather.18.cloned.1.call-done = bf16[1024,1024]{1,0:T(8,128)(2,1)} async-done(((bf16[256,1024]{1,0:T(8,128)(2,1)}), bf16[1024,1024]{1,0:T(8,128)(2,1)}) %all-gather.18.cloned.1.call-update) | async-done | bytes 2097168 | tf_op jit(solution)/shard_map/all_gather | solution.py:241
  490.6 3.1 convolution_convert_fusion.1
  493.8 27.2 %while.48 = (s32[]{:T(128)}, f32[1024,4,64]{0,2,1:T(8,128)S(1)}, f32[1024,4,64]{0,2,1:T(8,128)}, bf16[2,512,4,64]{1,3,2,0:T(8,128)(2,1)S(1)}, s32[2]{0:T(128)S(1...) while((s32[]{:T(128)}, f32[1024,4,64]{0,2,1:T(8,128)S(1)}, ...), condition=%wide.region_19.20_spmd.clone, body=%wide.region_17.19_spmd.clone.sunk | while | flops 1375729664 | bytes 82643280 | solution.py:98
  496.9 2.5 fusion.156
  499.4 3.2 multiply_reduce_fusion.7
  502.6 2.4 multiply_convert_fusion.2
  510.5 2.6 fusion.156
  513.0 3.2 multiply_reduce_fusion.7
  516.2 2.4 multiply_convert_fusion.2
  522.6 3.3 convolution_bitcast_fusion
  526.0 3.5 convolution_bitcast_fusion.1
  538.9 6.6 fusion.78
  547.1 6.0 fusion.77
  554.1 3.3 fusion.76
  558.7 48.2 %reduce-scatter.34.cloned.1.call-done = f32[32,6]{1,0:T(8,128)} async-done(((f32[1024,6]{1,0:T(8,128)}), f32[32,6]{1,0:T(8,128)}) %reduce-scatter.34.cloned.1.call-update) | async-done | bytes 784
  611.7 12.1 %all-reduce.11 = (f32[256]{0:T(256)S(1)}, f32[256]{0:T(256)S(1)}, f32[1024]{0:T(1024)S(1)}) all-reduce(f32[256]{0:T(256)S(1)} %reduce_sum.194, f32[256]{0:T(256)S(1)} %reduce_sum.196, f32[1024]{0:T(1024)S(1)} %get-tuple-element.362), channel_id=12, replica_groups=mesh['dp'=8,'tensor'=4] {'dp'}, use_global_device_ids=true, to_apply=%region_28.29.clone | all-reduce | flops 1536 | bytes 12288
  625.6 16.5 %reduce-scatter.26.cloned.1.call-done = f32[128,256]{0,1:T(8,128)} async-done(((f32[1024,256]{0,1:T(8,128)}), f32[128,256]{0,1:T(8,128)}) %reduce-scatter.26.cloned.1.call-update) | async-done | bytes 131088 | tf_op jit(solution)/shard_map/reduce_scatter | solution.py:272
  643.8 37.6 %reduce-scatter.24.cloned.1.call-done = f32[128,256]{0,1:T(8,128)} async-done(((f32[1024,256]{0,1:T(8,128)}), f32[128,256]{0,1:T(8,128)}) %reduce-scatter.24.cloned.1.call-update) | async-done | bytes 131088 | tf_op jit(solution)/shard_map/reduce_scatter | solution.py:271
  683.0 37.6 %reduce-scatter.22.cloned.1.call-done = f32[128,256]{0,1:T(8,128)} async-done(((f32[1024,256]{0,1:T(8,128)}), f32[128,256]{0,1:T(8,128)}) %reduce-scatter.22.cloned.1.call-update) | async-done | bytes 131088 | tf_op jit(solution)/shard_map/reduce_scatter | solution.py:270
  722.2 44.5 %reduce-scatter.20.cloned.1.call-done = bf16[256,1024]{1,0:T(8,128)(2,1)} async-done(((bf16[1024,1024]{1,0:T(8,128)(2,1)}), bf16[256,1024]{1,0:T(8,128)(2,1)}) %reduce-scatter.20.cloned.1.call-update) | async-done | bytes 524304 | tf_op jit(solution)/shard_map/reduce_scatter | solution.py:258
  768.9 52.6 %reduce-scatter.32.cloned.1.call-done = f32[1024,128]{1,0:T(8,128)} async-done(((f32[1024,1024]{1,0:T(8,128)}), f32[1024,128]{1,0:T(8,128)}) %reduce-scatter.32.cloned.1.call-update) | async-done | bytes 524304 | tf_op jit(solution)/shard_map/reduce_scatter | solution.py:275
  821.5 55.3 %reduce-scatter.30.cloned.1.call-done = f32[128,1024]{1,0:T(8,128)} async-done(((f32[1024,1024]{1,0:T(8,128)}), f32[128,1024]{1,0:T(8,128)}) %reduce-scatter.30.cloned.1.call-update) | async-done | bytes 524304 | tf_op jit(solution)/shard_map/reduce_scatter | solution.py:274
  876.8 40.0 %reduce-scatter.28.cloned.1.call-done = f32[256,128]{1,0:T(8,128)} async-done(((f32[256,1024]{1,0:T(8,128)}), f32[256,128]{1,0:T(8,128)}) %reduce-scatter.28.cloned.1.call-update) | async-done | bytes 131088 | tf_op jit(solution)/shard_map/reduce_scatter | solution.py:273
  (212 shorter events, 68.1 us)
Async XLA Ops:
  8.0 58.5 %all-gather.8.cloned.1.call-start = ((), (), s32[]{:S(2)}) async-start(), calls=%async_computation.11 | async-start | bytes 2621440 | tf_op jit(solution)/shard_map/all_gather | solution.py:165
  8.8 163.7 %reduce-scatter.14.cloned.1.call-start = ((), (), s32[]{:S(2)}) async-start(), calls=%async_computation.12 | async-start | bytes 5242880 | tf_op jit(solution)/shard_map/reduce_scatter | solution.py:185
  38.1 33.3 %copy-start.14 = (bf16[1024,256]{1,0:T(8,128)(2,1)}, bf16[1024,256]{1,0:T(8,128)(2,1)S(1)}, u32[]{:S(2)}) copy-start(bf16[1024,256]{1,0:T(8,128)(2,1)S(1)} %all_gather.58) | copy-start | bytes 1572868
  47.7 18.8 %copy-start.16 = (bf16[1024,256]{1,0:T(8,128)(2,1)}, bf16[1024,256]{1,0:T(8,128)(2,1)S(1)}, u32[]{:S(2)}) copy-start(bf16[1024,256]{1,0:T(8,128)(2,1)S(1)} %all_gather.60) | copy-start | bytes 1572868
  56.8 15.4 %copy-start.12 = (bf16[1024,256]{1,0:T(8,128)(2,1)}, bf16[1024,256]{1,0:T(8,128)(2,1)S(1)}, u32[]{:S(2)}) copy-start(bf16[1024,256]{1,0:T(8,128)(2,1)S(1)} %all_gather.61) | copy-start | bytes 1572868
  66.5 24.0 %copy-start.17 = (bf16[256,1024]{1,0:T(8,128)(2,1)}, bf16[256,1024]{1,0:T(8,128)(2,1)S(1)}, u32[]{:S(2)}) copy-start(bf16[256,1024]{1,0:T(8,128)(2,1)S(1)} %all_gather.63) | copy-start | bytes 1572868
  66.5 5.0 copy-start
  94.1 1.2 copy-start.25
  94.1 1.4 copy-start.26
  94.1 1.7 copy-start.27
  94.1 1.9 copy-start.28
  94.1 2.1 copy-start.29
  94.1 2.4 copy-start.30
  94.1 78.3 %copy-start.11 = (bf16[256,1024]{1,0:T(8,128)(2,1)S(1)}, bf16[256,1024]{1,0:T(8,128)(2,1)}, u32[]{:S(2)}) copy-start(bf16[256,1024]{1,0:T(8,128)(2,1)} %param.22) | copy-start | bytes 1572868
  94.1 81.7 %copy-start.22 = (bf16[128]{0:T(256)(128)(2,1)S(1)}, bf16[128]{0:T(256)(128)(2,1)}, u32[]{:S(2)}) copy-start(bf16[128]{0:T(256)(128)(2,1)} %param.33) | copy-start | bytes 772
  94.2 90.4 %all-gather.12.cloned.1.call-start = ((), (), s32[]{:S(2)}) async-start(), calls=%async_computation.14 | async-start | bytes 2359296 | tf_op jit(solution)/shard_map/all_gather | solution.py:143
  94.7 126.6 %all-gather.10.cloned.1.call-start = ((), (), s32[]{:S(2)}) async-start(), calls=%async_computation.13 | async-start | bytes 2621440 | tf_op jit(solution)/shard_map/all_gather | solution.py:194
  175.2 74.9 %all-gather.14.cloned.1.call-start = ((), (), s32[]{:S(2)}) async-start(), calls=%async_computation.15 | async-start | bytes 2359296 | tf_op jit(solution)/shard_map/all_gather | solution.py:144
  175.8 157.8 %reduce-scatter.16.cloned.1.call-start = ((), (), s32[]{:S(2)}) async-start(), calls=%async_computation.16 | async-start | bytes 5242880 | tf_op jit(solution)/shard_map/reduce_scatter | solution.py:201
  256.7 78.8 %copy-start.19 = (bf16[256,1024]{1,0:T(8,128)(2,1)S(1)}, bf16[256,1024]{1,0:T(8,128)(2,1)}, u32[]{:S(2)}) copy-start(bf16[256,1024]{1,0:T(8,128)(2,1)} %param.23) | copy-start | bytes 1572868
  256.7 127.7 %all-gather.16.cloned.1.call-start = ((), (), s32[]{:S(2)}) async-start(), calls=%async_computation.17 | async-start | bytes 2621440 | tf_op jit(solution)/shard_map/all_gather | solution.py:212
  337.9 101.0 %reduce-scatter.18.cloned.1.call-start = ((), (), s32[]{:S(2)}) async-start(), calls=%async_computation.18 | async-start | bytes 2621440 | tf_op jit(solution)/shard_map/reduce_scatter | solution.py:222
  384.4 8.0 copy-start.24
  391.1 1.3 copy-start.31
  396.1 94.5 %all-gather.18.cloned.1.call-start = ((), (), s32[]{:S(2)}) async-start(), calls=%async_computation.19 | async-start | bytes 2621440 | tf_op jit(solution)/shard_map/all_gather | solution.py:241
  438.9 51.7 %copy-start.18 = (bf16[256,1024]{1,0:T(8,128)(2,1)S(1)}, bf16[256,1024]{1,0:T(8,128)(2,1)}, u32[]{:S(2)}) copy-start(bf16[256,1024]{1,0:T(8,128)(2,1)} %copy-done.17) | copy-start | bytes 1572868
  444.6 162.3 %reduce-scatter.34.cloned.1.call-start = ((), (), s32[]{:S(2)}) async-start(), calls=%async_computation.27 | async-start | bytes 540672
  445.8 196.3 %reduce-scatter.26.cloned.1.call-start = ((), (), s32[]{:S(2)}) async-start(), calls=%async_computation.23 | async-start | bytes 1179648 | tf_op jit(solution)/shard_map/reduce_scatter | solution.py:272
  495.5 1.3 copy-start.10
  495.5 1.4 copy-start.20
  499.4 3.2 copy-start.21
  509.1 1.3 copy-start.10
  509.1 1.4 copy-start.20
  513.0 3.2 copy-start.21
  521.0 4.9 copy-start.8
  525.9 155.4 %reduce-scatter.24.cloned.1.call-start = ((), (), s32[]{:S(2)}) async-start(), calls=%async_computation.22 | async-start | bytes 1179648 | tf_op jit(solution)/shard_map/reduce_scatter | solution.py:271
  526.0 6.2 copy-start.1
  529.5 191.0 %reduce-scatter.22.cloned.1.call-start = ((), (), s32[]{:S(2)}) async-start(), calls=%async_computation.21 | async-start | bytes 1179648 | tf_op jit(solution)/shard_map/reduce_scatter | solution.py:270
  533.9 2.0 copy-start.7
  533.9 2.0 copy-start.15
  534.0 2.8 copy-start.13
  534.0 232.7 %reduce-scatter.20.cloned.1.call-start = ((), (), s32[]{:S(2)}) async-start(), calls=%async_computation.20 | async-start | bytes 2621440 | tf_op jit(solution)/shard_map/reduce_scatter | solution.py:258
  538.9 282.7 %reduce-scatter.32.cloned.1.call-start = ((), (), s32[]{:S(2)}) async-start(), calls=%async_computation.26 | async-start | bytes 4718592 | tf_op jit(solution)/shard_map/reduce_scatter | solution.py:275
  545.5 1.6 copy-start.23
  545.5 331.3 %reduce-scatter.30.cloned.1.call-start = ((), (), s32[]{:S(2)}) async-start(), calls=%async_computation.25 | async-start | bytes 4718592 | tf_op jit(solution)/shard_map/reduce_scatter | solution.py:274
  553.1 58.3 %copy-start.9 = (bf16[2,512,4,64]{1,3,2,0:T(8,128)(2,1)S(1)}, bf16[2,512,4,64]{1,3,2,0:T(8,128)(2,1)}, u32[]{:S(2)}) copy-start(bf16[2,512,4,64]{1,3,2,0:T(8,128)(2,1)} %copy-done.8) | copy-start | bytes 1572868
  553.1 213.6 %copy-start.3 = (f32[256,1024]{1,0:T(8,128)S(1)}, f32[256,1024]{1,0:T(8,128)}, u32[]{:S(2)}) copy-start(f32[256,1024]{1,0:T(8,128)} %copy-done.2) | copy-start | bytes 3145732
  553.1 363.7 %reduce-scatter.28.cloned.1.call-start = ((), (), s32[]{:S(2)}) async-start(), calls=%async_computation.24 | async-start | bytes 1179648 | tf_op jit(solution)/shard_map/reduce_scatter | solution.py:273
  (4 other events, 3.6 us)
Sparse Core Ops, SparseCore 0:
  10.4 48.6 all-gather.7
  94.3 78.0 reduce-scatter.13
  338.0 46.3 all-gather.15
  396.2 42.5 reduce-scatter.17
  447.4 159.4 reduce-scatter.33
  609.9 32.1 reduce-scatter.25
  645.3 35.9 reduce-scatter.23
  684.5 35.9 reduce-scatter.21
  722.8 43.8 reduce-scatter.19
  770.9 50.6 reduce-scatter.31
  825.5 51.2 reduce-scatter.29
  880.7 36.0 reduce-scatter.27
Sparse Core Ops, SparseCore 1:
  96.5 28.1 all-gather.11
  175.3 46.0 all-gather.9
  223.3 26.8 all-gather.13
  256.8 76.7 reduce-scatter.15
  444.6 45.9 all-gather.17
where the time goes:
time: 933 us; the launch traced here: 925 us
  waiting for transfers between devices  627 us (67%)
  blocking collectives  118 us (13%)
  matrix products  100 us (11%)
  local copies, waits for them, and re-layouts  28.5 us (3%)
  other arithmetic  27.5 us (3%)
  between operations  18.6 us (2%)
    reduce_scatter x1, waiting for transfers between devices, body(): lax.psum_scatter(jnp.dot(active, outer_full, preferred_element_type=jnp.f...  76.8 us
    unnamed x3, blocking collectives  72.2 us
    reduce_scatter x1, waiting for transfers between devices, body(): lax.psum_scatter(weight_inner, 'dp', scatter_dimension=0, tiled=True)  55.3 us
    reduce_scatter x1, waiting for transfers between devices, body(): lax.psum_scatter(weight_outer, 'dp', scatter_dimension=1, tiled=True)  52.6 us
    unnamed x18, waiting for transfers between devices  50.1 us
    all_gather x1, waiting for transfers between devices, body(): lax.all_gather(second_grad.astype(jnp.bfloat16), 'tensor', axis=0, tiled=...  46.5 us
    all_gather x1, waiting for transfers between devices, body(): lax.all_gather(first_grad.astype(jnp.bfloat16), 'tensor', axis=0, tiled=T...  44.6 us
    reduce_scatter x1, waiting for transfers between devices, body(): lax.psum_scatter((jnp.einsum('rh,dh->rd', query_back, query_full, preferr...  44.5 us
  transfers between devices with their start and end apart: 17, of which 15 were waited for; matrix products, arithmetic and copies ran while one was open for 11% of the time, Pallas kernels for 0%

commit v1 on v0

v1 whole, which is shorter than its diff:
```python
import jax
import jax.numpy as jnp
from jax import lax
from jax.experimental import pallas as pl
from jax.experimental.pallas import tpu as pltpu
from jax.sharding import PartitionSpec as P

HEAD_DIM = 64
LENGTH = 1024
QUARTERS = 4
BLOCK = 256
HALF = 128
bf16 = jnp.bfloat16
f32 = jnp.float32
VMEM = pl.BlockSpec(memory_space=pltpu.VMEM)
SMEM = pl.BlockSpec(memory_space=pltpu.SMEM)
HBM = pl.BlockSpec(memory_space=pl.ANY)


def shape(dims, dtype):
    return jax.ShapeDtypeStruct(dims, dtype)


def call(kernel, name, operands, specs, outs, flops, scratch=(), moved=4 << 20, grid=()):
    return pl.pallas_call(
        kernel,
        grid=grid,
        name=name,
        out_shape=outs,
        in_specs=specs,
        out_specs=[VMEM] * len(outs),
        scratch_shapes=list(scratch),
        compiler_params=pltpu.CompilerParams(vmem_limit_bytes=52 << 20),
        cost_estimate=pl.CostEstimate(flops=flops, bytes_accessed=moved, transcendentals=0),
    )(*operands)


def dot(left, right, dims=((1,), (0,))):
    return lax.dot_general(left, right, (dims, ((), ())), preferred_element_type=f32)


NT = ((1,), (1,))
TN = ((0,), (0,))


def norm_back(grad, normed, scale, gain):
    scaled = grad * gain
    return scale * (
        scaled
        - jnp.mean(scaled, -1, keepdims=True)
        - normed * jnp.mean(scaled * normed, -1, keepdims=True)
    )


def lanes(ids, j):
    return pl.ds(pl.multiple_of((ids[0] ^ j) * BLOCK, BLOCK), BLOCK)


def segments(ids, docs, dims, axis):
    place = lax.broadcasted_iota(jnp.int32, dims, axis)
    place = ((ids[2] - (place >> 8) + QUARTERS) & (QUARTERS - 1)) * BLOCK + (place & (BLOCK - 1))
    bound = docs[0, 0]
    total = (place >= bound).astype(jnp.int32)
    for j in range(1, 8):
        bound = bound + docs[0, j]
        total = total + (place >= bound).astype(jnp.int32)
    return total


def attend_kernel(ids, docs, t0, t1, t2, t3, own, other, qb, vb, q, k, v, w, m0, m1, m2, m3, lse):
    core = ids[1]
    for j in range(4):
        base = (ids[0] ^ j) * BLOCK
        for source, side in ((own, core), (other, 1 - core)):
            rows = pl.ds(pl.multiple_of(base + side * HALF, HALF), HALF)
            for i in range(3):
                at = (j * 3 + i) * HALF
                w[rows, i * BLOCK : (i + 1) * BLOCK] = source[at : at + HALF, :]
    for b, t in enumerate((t0, t1, t2, t3)):
        rows = slice(b * BLOCK, (b + 1) * BLOCK)
        made = dot(t[...], w[...])
        q[rows, :] = (made[:, :BLOCK] + qb[...]).astype(bf16)
        k[rows, :] = made[:, BLOCK : 2 * BLOCK].astype(bf16)
        v[rows, :] = (made[:, 2 * BLOCK :] + vb[...]).astype(bf16)
    along = segments(ids, docs, (1, LENGTH), 1)
    down = segments(ids, docs, (LENGTH, 1), 0)
    for b, mixed in enumerate((m0, m1, m2, m3)):
        rows = slice(b * BLOCK, (b + 1) * BLOCK)
        same = down[rows] == along
        for h in range(4):
            cols = slice(h * HEAD_DIM, (h + 1) * HEAD_DIM)
            scores = dot(q[rows, cols] * bf16(0.125), k[:, cols], NT)
            scores = jnp.where(same, scores, -1e30)
            top = jnp.max(scores, -1, keepdims=True)
            expo = jnp.exp(scores - top)
            total = jnp.sum(expo, -1, keepdims=True)
            shares = (expo * (1.0 / total)).astype(bf16)
            mixed[:, cols] = dot(shares, v[:, cols]).astype(bf16)
            lse[rows, h : h + 1] = top + jnp.log(total)


def project_kernel(ids, tokens, x0, x1, x2, x3, *refs):
    own = refs[:16]
    other, bias, gain, shift, wo, normed, scale, low = refs[16:]
    core = ids[1]
    for k in range(4):
        for j in range(4):
            i = k * 4 + j
            mine = pl.ds(pl.multiple_of(k * BLOCK + core * HALF, HALF), HALF)
            theirs = pl.ds(pl.multiple_of(k * BLOCK + (1 - core) * HALF, HALF), HALF)
            wo[mine, lanes(ids, j)] = own[i][...]
            wo[theirs, lanes(ids, j)] = other[i * HALF : (i + 1) * HALF, :]
    total = tokens[...].astype(f32) + bias[...]
    for k, x in enumerate((x0, x1, x2, x3)):
        total = total + dot(x[...], wo[k * BLOCK : (k + 1) * BLOCK, :])
    centered = total - jnp.mean(total, -1, keepdims=True)
    r = lax.rsqrt(jnp.mean(centered * centered, -1, keepdims=True) + 1e-05)
    n = centered * r
    normed[...] = n
    scale[...] = jnp.broadcast_to(r, scale.shape)
    low[...] = (n * gain[...] + shift[...]).astype(bf16)


def fetch(blocks, held, sems):
    copies = [
        pltpu.make_async_copy(b.at[pl.ds(0, 1024)], held.at[i], sems.at[i])
        for i, b in enumerate(blocks)
    ]
    for copy in copies:
        copy.start()
    return copies


def forward_kernel(ids, mine, theirs, bias, *refs):
    blocks = refs[:16]
    active, slope, out_mine, out_theirs, held, rows, sems = refs[16:]
    copies = fetch(blocks, held, sems)
    rows[:BLOCK, :] = mine[...]
    rows[BLOCK:, :] = theirs[...]
    for k in range(4):
        for j in range(4):
            copies[k * 4 + j].wait()
        at = ((ids[2] - k + QUARTERS) & (QUARTERS - 1)) * 2 + ids[1]
        offset = bias[pl.ds(at, 1), :]
        for half in range(2):
            span = slice(half * BLOCK, (half + 1) * BLOCK)
            inner = jnp.broadcast_to(offset[:, span], (512, BLOCK))
            for j in range(4):
                inner = inner + dot(rows[:, lanes(ids, j)], held[k * 4 + j, span, :])
            phi = 0.5 * (1.0 + lax.erf(inner * 0.7071067811865476))
            active[k * 512 : (k + 1) * 512, span] = (inner * phi).astype(bf16)
            slope[k * 512 : (k + 1) * 512, span] = (
                phi + inner * jnp.exp(-0.5 * inner * inner) * 0.3989422804014327
            ).astype(bf16)
        for j in range(4):
            made = dot(active[k * 512 : (k + 1) * 512, :], held[k * 4 + j, 512:1024, :])
            at = lanes(ids, j)
            if k == 0:
                out_mine[:, at] = made[:BLOCK]
                out_theirs[:, at] = made[BLOCK:]
            else:
                out_mine[:, at] += made[:BLOCK]
                out_theirs[:, at] += made[BLOCK:]


def second_kernel(normed, gain1, shift1, mine, got, bias, gain, shift, cot, out, grad, low, sums):
    total = normed[...] * gain1[...] + shift1[...] + (mine[...] + got[...]) + bias[...]
    centered = total - jnp.mean(total, -1, keepdims=True)
    r = lax.rsqrt(jnp.mean(centered * centered, -1, keepdims=True) + 1e-05)
    n = centered * r
    out[...] = (n * gain[...] + shift[...]).astype(bf16)
    up = cot[...].astype(f32)
    back = norm_back(up, n, r, gain[...])
    grad[...] = back
    low[...] = back.astype(bf16)
    sums[0:1, :] = jnp.sum(back, 0, keepdims=True)
    sums[1:2, :] = jnp.sum(up * n, 0, keepdims=True)
    sums[2:3, :] = jnp.sum(up, 0, keepdims=True)


def backward_kernel(ids, mine, theirs, slope, *refs):
    blocks = refs[:16]
    back, out_mine, out_theirs, sums, held, rows, total, sems = refs[16:]
    copies = fetch(blocks, held, sems)
    rows[:BLOCK, :] = mine[...]
    rows[BLOCK:, :] = theirs[...]
    sums[...] = jnp.zeros(sums.shape, f32)
    for k in range(4):
        for j in range(4):
            copies[k * 4 + j].wait()
        span = slice(k * 512, (k + 1) * 512)
        made = dot(rows[:, lanes(ids, 0)], held[k * 4, 512:1024, :], NT)
        for j in range(1, 4):
            made = made + dot(rows[:, lanes(ids, j)], held[k * 4 + j, 512:1024, :], NT)
        made = (made * slope[span, :].astype(f32)).astype(bf16)
        back[span, :] = made
        at = ((ids[2] - k + QUARTERS) & (QUARTERS - 1)) * 2 + ids[1]
        sums[pl.ds(at, 1), :] = jnp.sum(made.astype(f32), 0, keepdims=True)
        for j in range(4):
            part = dot(made[:, :BLOCK], held[k * 4 + j, :BLOCK, :], NT) + dot(
                made[:, BLOCK:], held[k * 4 + j, BLOCK:512, :], NT
            )
            at = lanes(ids, j)
            if k == 0:
                total[:, at] = part
            else:
                total[:, at] += part
    out_mine[...] = total[:BLOCK, :]
    out_theirs[...] = total[BLOCK:, :].astype(bf16)


def weights_kernel(ids, active, back, mine, theirs, gmine, gtheirs, o0, o1, o2, o3):
    for j, out in enumerate((o0, o1, o2, o3)):
        at = lanes(ids, j)
        left = dot(mine[:, at], back[:BLOCK, :], TN) + dot(theirs[:, at], back[BLOCK:, :], TN)
        out[:BLOCK, :] = left[:, :BLOCK].astype(bf16)
        out[BLOCK:512, :] = left[:, BLOCK:].astype(bf16)
        out[512:1024, :] = (
            dot(active[:BLOCK, :], gmine[:, at], TN) + dot(active[BLOCK:, :], gtheirs[:, at], TN)
        ).astype(bf16)


def first_kernel(second, mine, got, normed, scale, gain, wo, grad, low, g0, g1, g2, g3, sums):
    hidden = second[...] + mine[...] + got[...].astype(f32)
    n = normed[...]
    back = norm_back(hidden, n, scale[:, :1], gain[...])
    grad[...] = back
    rounded = back.astype(bf16)
    low[...] = rounded
    for k, g in enumerate((g0, g1, g2, g3)):
        g[...] = dot(rounded, wo[k * BLOCK : (k + 1) * BLOCK, :], NT).astype(bf16)
    sums[0:1, :] = jnp.sum(back, 0, keepdims=True)
    sums[1:2, :] = jnp.sum(hidden * n, 0, keepdims=True)
    sums[2:3, :] = jnp.sum(hidden, 0, keepdims=True)


def output_grad_kernel(ids, x0, x1, x2, x3, low, own, send, made):
    core = ids[1]
    for k, x in enumerate((x0, x1, x2, x3)):
        made[...] = dot(x[...], low[...], TN)
        for out, side in ((own, core), (send, 1 - core)):
            rows = pl.ds(pl.multiple_of(side * HALF, HALF), HALF)
            for j in range(4):
                at = j * 512 + k * HALF
                out[at : at + HALF, :] = made[rows, lanes(ids, j)].astype(bf16)


def attend_back_kernel(
    ids, docs, q, k, v, lse, g0, g1, g2, g3, w, d0, d1, d2, d3, dqkv, sums, g, ktot, vtot
):
    for b, part in enumerate((g0, g1, g2, g3)):
        g[b * BLOCK : (b + 1) * BLOCK, :] = part[...]
    along = segments(ids, docs, (1, LENGTH), 1)
    down = segments(ids, docs, (LENGTH, 1), 0)
    logs = jnp.transpose(lse[...])
    for b in range(4):
        rows = slice(b * BLOCK, (b + 1) * BLOCK)
        same = down == along[:, rows]
        for h in range(4):
            cols = slice(h * HEAD_DIM, (h + 1) * HEAD_DIM)
            scaled = q[rows, cols] * bf16(0.125)
            scores = dot(k[:, cols], scaled, NT)
            scores = jnp.where(same, scores, -1e30)
            shares = jnp.exp(scores - logs[h : h + 1, rows])
            dots = dot(v[:, cols], g[rows, cols], NT)
            product = shares * dots
            centre = jnp.sum(product, 0, keepdims=True)
            back = (product - shares * centre).astype(bf16)
            vpart = dot(shares.astype(bf16), g[rows, cols])
            kpart = dot(back, scaled)
            if b == 0:
                vtot[:, cols] = vpart
                ktot[:, cols] = kpart
            else:
                vtot[:, cols] += vpart
                ktot[:, cols] += kpart
            dqkv[rows, cols] = (dot(back, k[:, cols], TN) * 0.125).astype(bf16)
    dqkv[:, BLOCK : 2 * BLOCK] = ktot[...].astype(bf16)
    dqkv[:, 2 * BLOCK :] = vtot[...].astype(bf16)
    sums[0:1, :] = jnp.sum(dqkv[:, :BLOCK].astype(f32), 0, keepdims=True)
    sums[1:2, :] = jnp.sum(dqkv[:, 2 * BLOCK :].astype(f32), 0, keepdims=True)
    for b, out in ((1, d1), (2, d2), (3, d3), (0, d0)):
        out[...] = dot(dqkv[b * BLOCK : (b + 1) * BLOCK, :], w[...], NT).astype(bf16)


def input_grad_kernel(ids, t0, t1, t2, t3, dqkv, own, send, made):
    core = ids[1]
    for j in range(4):
        at = lanes(ids, j)
        total = dot(t0[:, at], dqkv[:BLOCK, :], TN)
        for b, t in ((1, t1), (2, t2), (3, t3)):
            total = total + dot(t[:, at], dqkv[b * BLOCK : (b + 1) * BLOCK, :], TN)
        made[...] = total
        for out, side in ((own, core), (send, 1 - core)):
            rows = pl.ds(pl.multiple_of(side * HALF, HALF), HALF)
            for i in range(3):
                to = (j * 3 + i) * HALF
                out[to : to + HALF, :] = made[rows, i * BLOCK : (i + 1) * BLOCK].astype(bf16)


def body_for(dp, tensor):
    fast = dp == 8 and tensor == 4
    ring_pairs = [(i, (i + 1) % tensor) for i in range(tensor)]

    def flip(value, bit, axis="dp", size=dp):
        return lax.ppermute(value, axis, [(i, i ^ bit) for i in range(size)])

    def ring(value):
        return lax.ppermute(value, "tensor", ring_pairs)

    def swap(value):
        return flip(value, 1)

    def sum_all(value, over_tensor=True):
        bit = dp >> 1
        while bit:
            value = value + flip(value, bit)
            bit >>= 1
        bit = 1
        while over_tensor and bit < tensor:
            value = value + flip(value, bit, "tensor", tensor)
            bit <<= 1
        return value

    def spread(block, turn):
        by_x = flip(block, 2)
        by_y = flip(block, 4)
        far = flip(by_x, 4) if turn % 2 == 0 else flip(by_y, 2)
        return [block, by_x, by_y, far]

    def collect(parts, turn):
        own, by_x, by_y, far = parts
        if turn % 2 == 0:
            by_x = by_x + flip(far, 4)
        else:
            by_y = by_y + flip(far, 2)
        return own.astype(f32) + flip(by_x, 2).astype(f32) + flip(by_y, 4).astype(f32)

    def in_order(core, own, got, axis):
        return jnp.where(
            core == 0,
            jnp.concatenate([own, got], axis),
            jnp.concatenate([got, own], axis),
        )

    def gather_fast(core, wq, wk, wv, wo, w1, w2):
        def piece(side):
            a = lax.dynamic_slice_in_dim(w1, side * 512, 512, 1)
            b = lax.dynamic_slice_in_dim(w2, side * 512, 512, 0)
            c = lax.dynamic_slice_in_dim(wo, side * HALF, HALF, 0)
            return a, b, c

        a, b, c = piece(1 - core)
        got = swap(jnp.concatenate([a[:, i * HALF : (i + 1) * HALF] for i in range(4)] + [b, c], 0))
        a, b, c = piece(core)
        ga = jnp.concatenate([got[i * HALF : (i + 1) * HALF] for i in range(4)], 1)
        a = in_order(core, a, ga, 0)
        b = in_order(core, b, got[512:1024], 1)
        c = in_order(core, c, got[1024:], 1)
        block = jnp.concatenate([a[:, :BLOCK], a[:, BLOCK:], b, c], 0)
        first = jnp.concatenate([block, wq, wk, wv], 0)
        blocks = spread(first, 0)
        for turn in range(1, 4):
            block = ring(block)
            blocks = blocks + spread(block, turn)
        return blocks

    def gather_any(core, z, wq, wk, wv, wo, w1, w2):
        def whole(value, dim):
            value = lax.all_gather(value, "dp", axis=dim, tiled=True)
            return value

        def quarters(value):
            value = lax.all_gather(value, "tensor", axis=0, tiled=False)
            return jnp.take(value, (z - jnp.arange(tensor)) % tensor, axis=0)

        a = quarters(lax.dynamic_slice_in_dim(whole(w1, 0), core * 512, 512, 1))
        b = quarters(lax.dynamic_slice_in_dim(whole(w2, 1), core * 512, 512, 0))
        c = quarters(lax.dynamic_slice_in_dim(whole(wo, 1), core * HALF, HALF, 0))
        qkv = jnp.stack([whole(wq, 0), whole(wk, 0), whole(wv, 0)])
        qkv = qkv.reshape(3, 4, 2, HALF, BLOCK).transpose(2, 1, 0, 3, 4).reshape(2, 1536, BLOCK)
        blocks = []
        for k in range(4):
            for j in range(4):
                span = slice(j * BLOCK, (j + 1) * BLOCK)
                blocks.append(
                    jnp.concatenate(
                        [a[k, span, :BLOCK], a[k, span, BLOCK:], b[k][:, span], c[k][:, span]], 0
                    )
                )
        return blocks, qkv[core], qkv[1 - core]

    def body(
        tokens,
        cotangent,
        doc_lengths,
        query_weight,
        key_weight,
        value_weight,
        output_weight,
        inner_weight,
        outer_weight,
        query_offset,
        value_offset,
        inner_offset,
        output_offset,
        outer_offset,
        first_gain,
        first_shift,
        second_gain,
        second_shift,
    ):
        place = lax.axis_index("dp")
        z = lax.axis_index("tensor")
        core = place & 1
        chip = (place >> 1) if fast else jnp.zeros_like(place)
        ids = jnp.stack([chip, core, z]).astype(jnp.int32)
        rows = tokens.shape[0]
        width = tokens.shape[1]

        six = jnp.stack(
            [output_offset, outer_offset, first_gain, first_shift, second_gain, second_shift]
        ).astype(f32)
        piece = six.shape[1]
        six = jnp.where(
            jnp.arange(width) // piece == place * tensor + z, jnp.tile(six, (1, width // piece)), 0
        )
        two = jnp.stack([query_offset, value_offset]).astype(f32)
        piece = two.shape[1]
        two = jnp.where(
            jnp.arange(width) // piece == z * dp + place, jnp.tile(two, (1, width // piece)), 0
        )
        piece = inner_offset.shape[0]
        wide = piece * dp * tensor
        one = jnp.where(
            jnp.arange(wide) // piece == z * dp + place,
            jnp.tile(inner_offset.astype(f32), wide // piece),
            0,
        ).reshape(4, width)
        vectors = sum_all(jnp.concatenate([six, two, one], 0))
        six = [vectors[i : i + 1] for i in range(6)]
        output_bias, outer_bias, gain_one, shift_one, gain_two, shift_two = six
        query_bias = lax.dynamic_slice(vectors, (6, z * BLOCK), (1, BLOCK))
        value_bias = lax.dynamic_slice(vectors, (7, z * BLOCK), (1, BLOCK))
        inner_bias = vectors[8:12].reshape(8, 512)

        t = [tokens]
        weights = (query_weight, key_weight, value_weight, output_weight, inner_weight, outer_weight)
        if fast:
            blocks = gather_fast(core, *weights)
            own_in = jnp.concatenate([blocks[j][1152:1536] for j in range(4)], 0)
            other_in = swap(own_in)
        else:
            blocks, own_in, other_in = gather_any(core, z, *weights)
        for _ in range(3):
            t.append(ring(t[-1]))

        square = shape((LENGTH, BLOCK), bf16)
        tile = shape((BLOCK, BLOCK), bf16)
        q, k, v, w_in, m0, m1, m2, m3, lse = call(
            attend_kernel,
            "attend",
            (ids, doc_lengths, *t, own_in, other_in, query_bias, value_bias),
            [SMEM, SMEM] + [VMEM] * 8,
            [square] * 3
            + [shape((width, 3 * BLOCK), bf16)]
            + [tile] * 4
            + [shape((LENGTH, HALF), f32)],
            flops=6 << 30,
        )

        def shift(value, by):
            return lax.ppermute(value, "tensor", [(i, (i - by) % tensor) for i in range(tensor)])

        x = [m0, shift(m3, 3), shift(m2, 2), shift(m1, 1)]
        other_out = swap(jnp.concatenate([b[1024:1152] for b in blocks], 0))
        part = pl.BlockSpec((HALF, BLOCK), lambda i: (8, 0))
        wide_f = shape((rows, width), f32)
        wide_b = shape((rows, width), bf16)
        w_out, normed1, scale1, hidden_low = call(
            project_kernel,
            "project",
            (ids, tokens, *x, *blocks, other_out, output_bias, gain_one, shift_one),
            [SMEM] + [VMEM] * 5 + [part] * 16 + [VMEM] * 4,
            [shape((width, width), bf16), wide_f, shape((rows, HALF), f32), wide_b],
            flops=1 << 29,
            grid=(1,),
        )
        hidden_other = swap(hidden_low)
        tall = shape((2048, 512), bf16)
        held = [pltpu.VMEM((16, 1024, BLOCK), bf16), pltpu.VMEM((2 * rows, width), bf16)]
        active, slope, out_own, out_send = call(
            forward_kernel,
            "forward",
            (ids, hidden_low, hidden_other, inner_bias, *blocks),
            [SMEM] + [VMEM] * 3 + [HBM] * 16,
            [tall, tall, wide_f, wide_f],
            flops=4 << 30,
            scratch=held + [pltpu.SemaphoreType.DMA((16,))],
        )
        result, second_grad, second_low, second_sums = call(
            second_kernel,
            "second",
            (
                normed1,
                gain_one,
                shift_one,
                out_own,
                swap(out_send),
                outer_bias,
                gain_two,
                shift_two,
                cotangent,
            ),
            [VMEM] * 9,
            [wide_b, wide_f, wide_b, shape((3, width), f32)],
            flops=1 << 24,
        )
        second_other = swap(second_low)
        back, grad_own, grad_send, inner_sums = call(
            backward_kernel,
            "backward",
            (ids, second_low, second_other, slope, *blocks),
            [SMEM] + [VMEM] * 3 + [HBM] * 16,
            [tall, wide_f, wide_b, shape((8, 512), f32)],
            flops=4 << 30,
            scratch=held
            + [pltpu.VMEM((2 * rows, width), f32), pltpu.SemaphoreType.DMA((16,))],
        )

        def weights_of(turn):
            at = pl.BlockSpec((512, 512), lambda i: (turn, 0))
            return call(
                weights_kernel,
                "weights",
                (ids, active, back, hidden_low, hidden_other, second_low, second_other),
                [SMEM, at, at] + [VMEM] * 4,
                [shape((1024, BLOCK), bf16)] * 4,
                flops=2 << 30,
                grid=(1,),
            )

        grads = {turn: weights_of(turn) for turn in (1, 2, 3, 0)}
        first_grad, first_low, g0, g1, g2, g3, first_sums = call(
            first_kernel,
            "first",
            (second_grad, grad_own, swap(grad_send), normed1, scale1, gain_one, w_out),
            [VMEM] * 7,
            [wide_f, wide_b] + [tile] * 4 + [shape((3, width), f32)],
            flops=1 << 29,
        )
        g = [g0, shift(g3, 3), shift(g2, 2), shift(g1, 1)]
        out_part = shape((2048, BLOCK), bf16)
        wo_own, wo_send = call(
            output_grad_kernel,
            "output_grad",
            (ids, *x, first_low),
            [SMEM] + [VMEM] * 5,
            [out_part, out_part],
            flops=1 << 29,
            scratch=[pltpu.VMEM((BLOCK, width), f32)],
        )
        d0, d1, d2, d3, dqkv, head_sums = call(
            attend_back_kernel,
            "attend_back",
            (ids, doc_lengths, q, k, v, lse, *g, w_in),
            [SMEM, SMEM] + [VMEM] * 9,
            [wide_b] * 4 + [shape((LENGTH, 3 * BLOCK), bf16), shape((2, BLOCK), f32)],
            flops=12 << 30,
            scratch=[
                pltpu.VMEM((LENGTH, BLOCK), bf16),
                pltpu.VMEM((LENGTH, BLOCK), f32),
                pltpu.VMEM((LENGTH, BLOCK), f32),
            ],
        )
        in_part = shape((1536, BLOCK), bf16)
        in_own, in_send = call(
            input_grad_kernel,
            "input_grad",
            (ids, *t, dqkv),
            [SMEM] + [VMEM] * 5,
            [in_part, in_part],
            flops=2 << 30,
            scratch=[pltpu.VMEM((BLOCK, 3 * BLOCK), f32)],
        )

        moving = ring(d1)
        moving = ring((moving.astype(f32) + d2.astype(f32)).astype(bf16))
        moving = ring((moving.astype(f32) + d3.astype(f32)).astype(bf16))
        tokens_grad = first_grad + (moving.astype(f32) + d0.astype(f32))

        if fast:
            def around(parts):
                moving = ring(parts[1].astype(bf16))
                moving = ring((parts[2] + moving.astype(f32)).astype(bf16))
                moving = ring((parts[3] + moving.astype(f32)).astype(bf16))
                return parts[0] + moving.astype(f32)

            parts = {turn: collect(grads[turn], turn) for turn in (1, 2, 3, 0)}
            mine = around(parts)
            left = mine[:512].reshape(2, 2, HALF, BLOCK)
            right = mine[512:]

            def sides(side):
                a = lax.dynamic_index_in_dim(left, side, 1, False)
                b = lax.dynamic_slice_in_dim(right, side * HALF, HALF, 1)
                return a, b

            a, b = sides(1 - core)
            got = swap(
                jnp.concatenate(
                    [a[0, :, :HALF], a[0, :, HALF:], a[1, :, :HALF], a[1, :, HALF:], b], 0
                ).astype(bf16)
            ).astype(f32)
            a, b = sides(core)
            ga = jnp.concatenate([got[i * HALF : (i + 1) * HALF] for i in range(4)], 1)
            inner_grad = in_order(core, jnp.concatenate([a[0], a[1]], 1), ga, 1)
            outer_grad = in_order(core, b, got[512:], 0)

            total = (wo_own.astype(f32) + swap(wo_send).astype(f32)).astype(bf16)
            total = collect([total[j * 512 : (j + 1) * 512] for j in range(4)], 0)
            total = around([total[i * HALF : (i + 1) * HALF] for i in range(4)])
            got = swap(lax.dynamic_slice_in_dim(total, (1 - core) * HALF, HALF, 1))
            total = lax.dynamic_slice_in_dim(total, core * HALF, HALF, 1)
            output_grad = in_order(core, total, got, 0)

            total = (in_own.astype(f32) + swap(in_send).astype(f32)).astype(bf16)
            total = collect([total[j * 384 : (j + 1) * 384] for j in range(4)], 1)
            query_grad, key_grad, value_grad = [
                total[i * HALF : (i + 1) * HALF] for i in range(3)
            ]
        else:
            def scatter(value, dim):
                return lax.psum_scatter(value, "dp", scatter_dimension=dim, tiled=True)

            def quarter(parts):
                found = jnp.stack(parts).astype(f32)
                found = jnp.take(found, (z - jnp.arange(tensor)) % tensor, axis=0)
                return lax.psum_scatter(found, "tensor", scatter_dimension=0, tiled=False)

            def half(value, dim):
                field = jnp.zeros_like(value)
                return jnp.where(
                    core == 0,
                    jnp.concatenate([value, field], dim),
                    jnp.concatenate([field, value], dim),
                )

            a = quarter(
                [
                    jnp.concatenate(
                        [jnp.concatenate([p[:BLOCK], p[BLOCK:512]], 1) for p in grads[turn]], 0
                    )
                    for turn in range(4)
                ]
            )
            b = quarter(
                [jnp.concatenate([p[512:1024] for p in grads[turn]], 1) for turn in range(4)]
            )
            inner_grad = scatter(half(a, 1), 0)
            outer_grad = scatter(half(b, 0), 1)

            def heads(value):
                return value.reshape(4, 4, HALF, BLOCK).transpose(1, 2, 0, 3).reshape(4, HALF, width)

            mine, theirs = quarter(list(heads(wo_own))), quarter(list(heads(wo_send)))
            output_grad = scatter(in_order(core, mine, theirs, 0), 1)
            own, send = [p.astype(f32).reshape(4, 3, HALF, BLOCK) for p in (in_own, in_send)]
            both = jnp.where(core == 0, jnp.stack([own, send], 1), jnp.stack([send, own], 1))
            both = both.transpose(2, 0, 1, 3, 4).reshape(3, width, BLOCK)
            query_grad, key_grad, value_grad = [scatter(both[i], 0) for i in range(3)]

        sums = sum_all(jnp.concatenate([first_sums, second_sums, inner_sums.reshape(4, width)], 0))
        head_sums = sum_all(head_sums, False)
        six = lax.dynamic_slice_in_dim(sums[:6], (place * tensor + z) * (width // dp // tensor), width // dp // tensor, 1)
        offset_inner = lax.dynamic_slice_in_dim(
            sums[6:].reshape(-1), (z * dp + place) * inner_offset.shape[0], inner_offset.shape[0], 0
        )
        head_sums = lax.dynamic_slice_in_dim(head_sums, place * (BLOCK // dp), BLOCK // dp, 1)
        return (
            result,
            tokens_grad,
            query_grad,
            key_grad,
            value_grad,
            output_grad,
            inner_grad,
            outer_grad,
            head_sums[0],
            head_sums[1],
            offset_inner,
            six[0],
            six[3],
            six[1],
            six[2],
            six[4],
            six[5],
        )

    return body


def solution(mesh):
    return jax.shard_map(
        body_for(mesh.shape["dp"], mesh.shape["tensor"]),
        mesh=mesh,
        in_specs=(
            P(("dp", "tensor"), None),
            P(("dp", "tensor"), None),
            P("dp", None),
            P("dp", "tensor"),
            P("dp", "tensor"),
            P("dp", "tensor"),
            P("tensor", "dp"),
            P("dp", "tensor"),
            P("tensor", "dp"),
            P(("tensor", "dp")),
            P(("tensor", "dp")),
            P(("tensor", "dp")),
            P(("dp", "tensor")),
            P(("dp", "tensor")),
            P(("dp", "tensor")),
            P(("dp", "tensor")),
            P(("dp", "tensor")),
            P(("dp", "tensor")),
        ),
        out_specs=(
            P(("dp", "tensor"), None),
            P(("dp", "tensor"), None),
            P("dp", "tensor"),
            P("dp", "tensor"),
            P("dp", "tensor"),
            P("tensor", "dp"),
            P("dp", "tensor"),
            P("tensor", "dp"),
            P(("tensor", "dp")),
            P(("tensor", "dp")),
            P(("tensor", "dp")),
            P(("dp", "tensor")),
            P(("dp", "tensor")),
            P(("dp", "tensor")),
            P(("dp", "tensor")),
            P(("dp", "tensor")),
            P(("dp", "tensor")),
        ),
        check_vma=False,
    )
```

time: 933 us -> 413 us (0.44)
  waiting for transfers between devices: 627 us -> 182 us
  blocking collectives: 118 us -> 0 us
  matrix products: 100 us -> 0 us
  Pallas kernels: 0 us -> 95 us
  starting transfers between devices: 1.55 us -> 75.4 us
  between operations: 18.6 us -> 2.08 us
  other arithmetic: 27.5 us -> 13.2 us
  local copies, waits for them, and re-layouts: 28.5 us -> 41.5 us
    reduce_scatter x10 -> x0, waiting for transfers between devices: 435 us -> none  [the longest x1 76.8 us: body(): lax.psum_scatter(jnp.dot(active, outer_full, preferred_element_type=jnp.f...]
    ppermute x0 -> x75, waiting for transfers between devices: none -> 182 us  [the longest x54 107 us: flip(): return lax.ppermute(value, axis, [(i, i ^ bit) for i in range(size)])]
    all_gather x6 -> x0, waiting for transfers between devices: 142 us -> none  [the longest x1 46.5 us: body(): lax.all_gather(second_grad.astype(jnp.bfloat16), 'tensor', axis=0, tiled=...]
    dot_general x32 -> x0, matrix products: 100 us -> none  [the longest x1 14.5 us: body(): jnp.dot(hidden_full, inner_full, preferred_element_type=jnp.float32)]
    pallas_call x0 -> x13, Pallas kernels: none -> 95 us  [call(): pl.pallas_call(kernel, grid=grid, name=name, out_shape=outs, in_specs=spe...]
    ppermute x0 -> x75, starting transfers between devices: none -> 75.4 us  [the longest x54 51.2 us: flip(): return lax.ppermute(value, axis, [(i, i ^ bit) for i in range(size)])]
    unnamed x3 -> x0, blocking collectives: 72.2 us -> none
    unnamed x18 -> x0, waiting for transfers between devices: 50.1 us -> none
  transfers between devices with their start and end apart: 17 -> 75, of which waited for: 15 -> 33; matrix products, arithmetic and copies ran while one was open for 11% -> 8% of each run, Pallas kernels for 0% -> 16%
where the time goes in v1:
time: 413 us; the launch traced here: 409 us
  waiting for transfers between devices  182 us (44%)
  Pallas kernels  95 us (23%)
  starting transfers between devices  75.4 us (18%)
  local copies, waits for them, and re-layouts  41.5 us (10%)
  other arithmetic  13.2 us (3%)
    ppermute x54, waiting for transfers between devices, flip(): return lax.ppermute(value, axis, [(i, i ^ bit) for i in range(size)])  107 us
    pallas_call x13, Pallas kernels, call(): pl.pallas_call(kernel, grid=grid, name=name, out_shape=outs, in_specs=spe...  95 us
    ppermute x15, waiting for transfers between devices, ring(): return lax.ppermute(value, 'tensor', ring_pairs)  60.1 us
    ppermute x54, starting transfers between devices, flip(): return lax.ppermute(value, axis, [(i, i ^ bit) for i in range(size)])  51.2 us
    unnamed x171, local copies, waits for them, and re-layouts  32.3 us
    ppermute x6, waiting for transfers between devices, shift(): lax.ppermute(value, 'tensor', [(i, (i - by) % tensor) for i in range(tens...  14.6 us
    ppermute x15, starting transfers between devices, ring(): return lax.ppermute(value, 'tensor', ring_pairs)  13.6 us
    ppermute x6, starting transfers between devices, shift(): lax.ppermute(value, 'tensor', [(i, (i - by) % tensor) for i in range(tens...  10.6 us
  transfers between devices with their start and end apart: 75, of which 33 were waited for; matrix products, arithmetic and copies ran while one was open for 8% of the time, Pallas kernels for 16%

profile of v1, /device:TPU:0, one launch (start us, length us, event | category | flops | bytes accessed | tf_op | source)
XLA Modules:
  0.0 409.0 jit_solution(5875491199760353503)
XLA Ops:
  6.1 2.6 collective-permute-start
  22.2 2.9 collective-permute-done.8
  25.7 12.5 %collective-permute-done.9 = f32[12,1024]{1,0:T(8,128)S(1)} collective-permute-done((f32[12,1024]{1,0:T(8,128)S(1)}, f32[12,1024]{1,0:T(8,128)S(1)}, u32[]{:S(2)}, u32[]{:S(2)}) %collective-permute-start.9) | collective-permute-done | bytes 49184 | tf_op jit(solution)/shard_map/ppermute | solution.py:306
  41.1 2.7 collective-permute-done.11
  55.0 5.6 %collective-permute-done.1.t2 = bf16[256,1024]{1,0:T(8,128)(2,1)S(1)} collective-permute-done((bf16[256,1024]{1,0:T(8,128)(2,1)S(1)}, bf16[256,1024]{1,0:T(8,128)(2,1)S(1)}, u32[]{:S(2)}, u32[]{:S(2)}) %collective-permute-start.1) | collective-permute-done | bytes 524320 | tf_op jit(solution)/shard_map/ppermute | solution.py:309
  61.4 10.6 %collective-permute-done.20.refs_8_ = bf16[1152,256]{1,0:T(8,128)(2,1)S(1)} collective-permute-done((bf16[1152,256]{1,0:T(8,128)(2,1)S(1)}, bf16[1152,256]{1,0:T(8,128)(2,1)S(1)}, u32[]{:S(2)}, u32[]{:S(2)}) %collective-permute-start.20) | collective-permute-done | bytes 589856 | tf_op jit(solution)/shard_map/ppermute | solution.py:309
  75.6 2.6 collective-permute-start.24
  81.3 15.9 %collective-permute-done.19.refs_7_ = bf16[1152,256]{1,0:T(8,128)(2,1)S(1)} collective-permute-done((bf16[1152,256]{1,0:T(8,128)(2,1)S(1)}, bf16[1152,256]{1,0:T(8,128)(2,1)S(1)}, u32[]{:S(2)}, u32[]{:S(2)}) %collective-permute-start.19) | collective-permute-done | bytes 589856 | tf_op jit(solution)/shard_map/ppermute | solution.py:306
  102.7 10.8 %collective-permute-done.22.refs_10_ = bf16[1152,256]{1,0:T(8,128)(2,1)S(1)} collective-permute-done((bf16[1152,256]{1,0:T(8,128)(2,1)S(1)}, bf16[1152,256]{1,0:T(8,128)(2,1)S(1)}, u32[]{:S(2)}, u32[]{:S(2)}) %collective-permute-start.22) | collective-permute-done | bytes 589856 | tf_op jit(solution)/shard_map/ppermute | solution.py:306
  115.7 10.5 %collective-permute-done.23.refs_11_ = bf16[1152,256]{1,0:T(8,128)(2,1)S(1)} collective-permute-done((bf16[1152,256]{1,0:T(8,128)(2,1)S(1)}, bf16[1152,256]{1,0:T(8,128)(2,1)S(1)}, u32[]{:S(2)}, u32[]{:S(2)}) %collective-permute-start.23) | collective-permute-done | bytes 589856 | tf_op jit(solution)/shard_map/ppermute | solution.py:306
  126.2 7.3 %collective-permute-done.26.refs_14_ = bf16[1152,256]{1,0:T(8,128)(2,1)S(1)} collective-permute-done((bf16[1152,256]{1,0:T(8,128)(2,1)S(1)}, bf16[1152,256]{1,0:T(8,128)(2,1)S(1)}, u32[]{:S(2)}, u32[]{:S(2)}) %collective-permute-start.26) | collective-permute-done | bytes 589856 | tf_op jit(solution)/shard_map/ppermute | solution.py:306
  137.5 5.9 %collective-permute-done.27.refs_15_ = bf16[1152,256]{1,0:T(8,128)(2,1)S(1)} collective-permute-done((bf16[1152,256]{1,0:T(8,128)(2,1)S(1)}, bf16[1152,256]{1,0:T(8,128)(2,1)S(1)}, u32[]{:S(2)}, u32[]{:S(2)}) %collective-permute-start.27) | collective-permute-done | bytes 589856 | tf_op jit(solution)/shard_map/ppermute | solution.py:306
  145.4 15.8 %attend.1 = (bf16[1024,256]{1,0:T(8,128)(2,1)S(1)}, bf16[1024,256]{1,0:T(8,128)(2,1)S(1)}, bf16[1024,256]{1,0:T(8,128)(2,1)}, bf16[1024,768]{1,0:T(8,128)(2,1)},...) custom-call(s32[3]{0:T(128)S(1)} %pad_add_fusion.ids, ...), custom_call_target="tpu_custom_call" | custom-call | flops 6442450944 | bytes 4194304 | tf_op jit(solution)/shard_map/attend/pallas_call | solution.py:25
  161.9 5.0 %collective-permute-start.14 = (bf16[256,256]{1,0:T(8,128)(2,1)S(1)}, bf16[256,256]{1,0:T(8,128)(2,1)S(1)}, u32[]{:S(2)}, u32[]{:S(2)}) collective-permute-start(bf16[256,256]{1,0:T(8,128)(2,1)S(1)} %get-tuple-element.77), channel_id=1, source_target_pairs={{0,2},{1,3},{2,0},{3,1},{4,6},{5,7},{6,4},{7,5},{8,10},{9,11},{10,... | collective-permute-start | bytes 393224 | tf_op jit(solution)/shard_map/ppermute | solution.py:473
  166.9 3.9 collective-permute-done.13.x1
  170.8 5.3 %collective-permute-done.14.x2 = bf16[256,256]{1,0:T(8,128)(2,1)S(1)} collective-permute-done((bf16[256,256]{1,0:T(8,128)(2,1)S(1)}, bf16[256,256]{1,0:T(8,128)(2,1)S(1)}, u32[]{:S(2)}, u32[]{:S(2)}) %collective-permute-start.14) | collective-permute-done | bytes 131104 | tf_op jit(solution)/shard_map/ppermute | solution.py:473
  176.2 4.1 %project.1 = (bf16[1024,1024]{1,0:T(8,128)(2,1)}, f32[256,1024]{1,0:T(8,128)}, f32[256,128]{1,0:T(8,128)S(1)}, bf16[256,1024]{1,0:T(8,128)(2,1)S(1)}) custom-call(s32[3]{0:T(128)S(1)} %pad_add_fusion.ids, bf16[256,1024]{1,0:T(8,128)(2,1)S(1)} %copy-done.2, bf16[256,256]{1,0:T(8,128)(2,1)S(1)} %get-tuple-element.75.x0, ...), custom_call_target="tpu_custom_call" | custom-call | flops 536870912 | bytes 4194304 | tf_op jit(solution)/shard_map/project/pallas_call | solution.py:25
  182.9 11.2 %forward.1 = (bf16[2048,512]{1,0:T(8,128)(2,1)}, bf16[2048,512]{1,0:T(8,128)(2,1)}, f32[256,1024]{1,0:T(8,128)}, f32[256,1024]{1,0:T(8,128)}) custom-call(s32[3]{0:T(128)S(1)} %pad_add_fusion.ids, bf16[256,1024]{1,0:T(8,128)(2,1)S(1)} %get-tuple-element.80.mine, bf16[256,1024]{1,0:T(8,128)(2,1)S(1)} %collective-permute-done.29.theirs, ...), custom_call_target="tpu_custom_call" | custom-call | flops 4294967296 | bytes 4194304 | tf_op jit(solution)/shard_map/forward/pallas_call | solution.py:25
  194.3 2.7 collective-permute-done.30.got
  198.1 4.0 second.1
  204.0 10.4 %backward.1 = (bf16[2048,512]{1,0:T(8,128)(2,1)}, f32[256,1024]{1,0:T(8,128)}, bf16[256,1024]{1,0:T(8,128)(2,1)}, f32[8,512]{1,0:T(8,128)S(1)}) custom-call(s32[3]{0:T(128)S(1)} %pad_add_fusion.ids, bf16[256,1024]{1,0:T(8,128)(2,1)S(1)} %get-tuple-element.85.mine.gmine, bf16[256,1024]{1,0:T(8,128)(2,1)S(1)} %collective-permute-done.31.theirs.gtheirs, ...), custom_call_target="tpu_custom_call" | custom-call | flops 4294967296 | bytes 4194304 | tf_op jit(solution)/shard_map/backward/pallas_call | solution.py:25
  214.6 4.2 %weights.4 = (bf16[1024,256]{1,0:T(8,128)(2,1)S(1)}, bf16[1024,256]{1,0:T(8,128)(2,1)S(1)}, bf16[1024,256]{1,0:T(8,128)(2,1)S(1)}, bf16[1024,256]{1,0:T(8,128)(2,1)}) custom-call(s32[3]{0:T(128)S(1)} %pad_add_fusion.ids, bf16[2048,512]{1,0:T(8,128)(2,1)} %get-tuple-element.111.active, bf16[2048,512]{1,0:T(8,128)(2,1)} %get-tuple-element.112.back, ...), custom_call_target="tpu_custom_call" | custom-call | flops 2147483648 | bytes 4194304 | tf_op jit(solution)/shard_map/weights/pallas_call | solution.py:25
  220.4 4.0 weights.5
  226.7 4.0 weights.6
  231.4 4.6 %first.1 = (f32[256,1024]{1,0:T(8,128)}, bf16[256,1024]{1,0:T(8,128)(2,1)S(1)}, bf16[256,256]{1,0:T(8,128)(2,1)S(1)}, bf16[256,256]{1,0:T(8,128)(2,1)S(1)}, bf16...) custom-call(f32[256,1024]{1,0:T(8,128)} %get-tuple-element.84.second, ...), custom_call_target="tpu_custom_call" | custom-call | flops 536870912 | bytes 4194304 | tf_op jit(solution)/shard_map/first/pallas_call | solution.py:25
  237.5 4.0 weights.7
  243.9 3.3 collective-permute-start.33
  247.2 2.4 collective-permute-start.35
  249.6 2.3 collective-permute-done.33.g1
  253.4 3.1 collective-permute-done.34.g2
  258.5 21.0 %attend_back.1 = (bf16[256,1024]{1,0:T(8,128)(2,1)S(1)}, bf16[256,1024]{1,0:T(8,128)(2,1)S(1)}, bf16[256,1024]{1,0:T(8,128)(2,1)}, bf16[256,1024]{1,0:T(8,128)(2...) custom-call(s32[3]{0:T(128)S(1)} %pad_add_fusion.ids, s32[1,8]{1,0:T(1,128)S(1)} %copy-done.38, ...), custom_call_target="tpu_custom_call" | custom-call | flops 12884901888 | bytes 4194304 | tf_op jit(solution)/shard_map/attend_back/pallas_call | solution.py:25
  282.6 2.1 collective-permute-done.67
  288.2 2.7 output_grad.1
  299.6 2.8 collective-permute-start.73
  302.5 5.0 %input_grad.1 = (bf16[1536,256]{1,0:T(8,128)(2,1)}, bf16[1536,256]{1,0:T(8,128)(2,1)}) custom-call(s32[3]{0:T(128)S(1)} %pad_add_fusion.ids, bf16[256,1024]{1,0:T(8,128)(2,1)S(1)} %copy-done.2, bf16[256,1024]{1,0:T(8,128)(2,1)S(1)} %copy-done.19, bf16[256,1024]{1,0:T(8,128)(2,1)S(1)} %copy-done.21, bf16[256,1024]{1,0:T(8,128)(2,1)} %collective-permute-done.2.t3, ...), custom_call_target="tpu_custom_call" | custom-call | flops 2147483648 | bytes 4194304 | tf_op jit(solution)/shard_map/input_grad/pallas_call | solution.py:25
  308.1 2.7 collective-permute-start.74
  311.3 2.7 collective-permute-done.74
  315.3 2.3 collective-permute-done.60
  319.2 10.3 %collective-permute-done.36 = bf16[256,1024]{1,0:T(8,128)(2,1)S(1)} collective-permute-done((bf16[256,1024]{1,0:T(8,128)(2,1)S(1)}, bf16[256,1024]{1,0:T(8,128)(2,1)S(1)}, u32[]{:S(2)}, u32[]{:S(2)}) %collective-permute-start.36) | collective-permute-done | bytes 524320 | tf_op jit(solution)/shard_map/ppermute | solution.py:309
  335.4 8.1 %collective-permute-done.58 = bf16[1024,256]{1,0:T(8,128)(2,1)S(1)} collective-permute-done((bf16[1024,256]{1,0:T(8,128)(2,1)S(1)}, bf16[1024,256]{1,0:T(8,128)(2,1)S(1)}, u32[]{:S(2)}, u32[]{:S(2)}) %collective-permute-start.58) | collective-permute-done | bytes 524320 | tf_op jit(solution)/shard_map/ppermute | solution.py:306
  344.8 4.2 %collective-permute-done.63 = bf16[1024,256]{1,0:T(8,128)(2,1)S(1)} collective-permute-done((bf16[1024,256]{1,0:T(8,128)(2,1)S(1)}, bf16[1024,256]{1,0:T(8,128)(2,1)S(1)}, u32[]{:S(2)}, u32[]{:S(2)}) %collective-permute-start.63) | collective-permute-done | bytes 524320 | tf_op jit(solution)/shard_map/ppermute | solution.py:309
  351.2 4.1 %collective-permute-done.44 = bf16[512,256]{1,0:T(8,128)(2,1)S(1)} collective-permute-done((bf16[512,256]{1,0:T(8,128)(2,1)S(1)}, bf16[512,256]{1,0:T(8,128)(2,1)S(1)}, u32[]{:S(2)}, u32[]{:S(2)}) %collective-permute-start.44) | collective-permute-done | bytes 262176 | tf_op jit(solution)/shard_map/ppermute | solution.py:306
  359.4 2.4 collective-permute-done.45
  361.9 2.8 collective-permute-done.46
  366.9 5.6 %collective-permute-done.42 = bf16[384,256]{1,0:T(8,128)(2,1)S(1)} collective-permute-done((bf16[384,256]{1,0:T(8,128)(2,1)S(1)}, bf16[384,256]{1,0:T(8,128)(2,1)S(1)}, u32[]{:S(2)}, u32[]{:S(2)}) %collective-permute-start.42) | collective-permute-done | bytes 196640 | tf_op jit(solution)/shard_map/ppermute | solution.py:306
  372.6 6.7 %collective-permute-done.47 = bf16[128,256]{1,0:T(8,128)(2,1)S(1)} collective-permute-done((bf16[128,256]{1,0:T(8,128)(2,1)S(1)}, bf16[128,256]{1,0:T(8,128)(2,1)S(1)}, u32[]{:S(2)}, u32[]{:S(2)}) %collective-permute-start.47) | collective-permute-done | bytes 65568 | tf_op jit(solution)/shard_map/ppermute | solution.py:309
  381.2 15.6 %collective-permute-done.48 = bf16[128,256]{1,0:T(8,128)(2,1)S(1)} collective-permute-done((bf16[128,256]{1,0:T(8,128)(2,1)S(1)}, bf16[128,256]{1,0:T(8,128)(2,1)S(1)}, u32[]{:S(2)}, u32[]{:S(2)}) %collective-permute-start.48) | collective-permute-done | bytes 65568 | tf_op jit(solution)/shard_map/ppermute | solution.py:309
  397.6 5.5 %collective-permute-done.49 = bf16[128,256]{1,0:T(8,128)(2,1)S(1)} collective-permute-done((bf16[128,256]{1,0:T(8,128)(2,1)S(1)}, bf16[128,256]{1,0:T(8,128)(2,1)S(1)}, u32[]{:S(2)}, u32[]{:S(2)}) %collective-permute-start.49) | collective-permute-done | bytes 65568 | tf_op jit(solution)/shard_map/ppermute | solution.py:309
  (373 shorter events, 116.0 us)
Async XLA Ops:
  6.1 37.8 %collective-permute-start = (bf16[256,1024]{1,0:T(8,128)(2,1)}, bf16[256,1024]{1,0:T(8,128)(2,1)S(1)}, u32[]{:S(2)}, u32[]{:S(2)}) collective-permute-start(bf16[256,1024]{1,0:T(8,128)(2,1)} %t0.3), channel_id=1, source_target_pairs={{0,1},{1,2},{2,3},{3,0},{4,5},{5,6},{6,7},{7,4},{8,9},{9,10},{10,1... | collective-permute-start | bytes 1572872 | tf_op jit(solution)/shard_map/ppermute | solution.py:309
  16.9 31.6 %collective-permute-start.4 = (bf16[1536,256]{1,0:T(8,128)(2,1)}, bf16[1536,256]{1,0:T(8,128)(2,1)S(1)}, u32[]{:S(2)}, u32[]{:S(2)}) collective-permute-start(bf16[1536,256]{1,0:T(8,128)(2,1)} %get-tuple-element.168.refs_0_), channel_id=1, source_target_pairs={{0,8},{4,12},{8,0},{12,4},{16,24},{20,28},{24,16},{28,20},{1,9},{5... | collective-permute-start | bytes 2359304 | tf_op jit(solution)/shard_map/ppermute | solution.py:306
  18.5 27.0 %collective-permute-start.16 = (bf16[1152,256]{1,0:T(8,128)(2,1)S(1)}, bf16[1152,256]{1,0:T(8,128)(2,1)S(1)}, u32[]{:S(2)}, u32[]{:S(2)}) collective-permute-start(bf16[1152,256]{1,0:T(8,128)(2,1)S(1)} %pad_maximum_fusion), channel_id=1, source_target_pairs={{0,1},{1,2},{2,3},{3,0},{4,5},{5,6},{6,7},{7,4},{8,9},{9,10},{10,1... | collective-permute-start | bytes 1769480 | tf_op jit(solution)/shard_map/ppermute | solution.py:309
  21.7 29.7 %collective-permute-start.5 = (bf16[1536,256]{1,0:T(8,128)(2,1)}, bf16[1536,256]{1,0:T(8,128)(2,1)}, u32[]{:S(2)}, u32[]{:S(2)}) collective-permute-start(bf16[1536,256]{1,0:T(8,128)(2,1)} %get-tuple-element.168.refs_0_), channel_id=1, source_target_pairs={{0,16},{4,20},{8,24},{12,28},{16,0},{20,4},{24,8},{28,12},{1,17},{... | collective-permute-start | bytes 2359304 | tf_op jit(solution)/shard_map/ppermute | solution.py:306
  25.1 13.1 %collective-permute-start.9 = (f32[12,1024]{1,0:T(8,128)S(1)}, f32[12,1024]{1,0:T(8,128)S(1)}, u32[]{:S(2)}, u32[]{:S(2)}) collective-permute-start(f32[12,1024]{1,0:T(8,128)S(1)} %fusion.20), channel_id=1, source_target_pairs={{0,8},{4,12},{8,0},{12,4},{16,24},{20,28},{24,16},{28,20},{1,9},{5... | collective-permute-start | bytes 147464 | tf_op jit(solution)/shard_map/ppermute | solution.py:306
  43.9 16.8 %collective-permute-start.1 = (bf16[256,1024]{1,0:T(8,128)(2,1)S(1)}, bf16[256,1024]{1,0:T(8,128)(2,1)S(1)}, u32[]{:S(2)}, u32[]{:S(2)}) collective-permute-start(bf16[256,1024]{1,0:T(8,128)(2,1)S(1)} %collective-permute-done.t1), channel_id=1, source_target_pairs={{0,1},{1,2},{2,3},{3,0},{4,5},{5,6},{6,7},{7,4},{8,9},{9,10},{10,1... | collective-permute-start | bytes 1572872 | tf_op jit(solution)/shard_map/ppermute | solution.py:309
  45.5 30.1 %collective-permute-start.17 = (bf16[1152,256]{1,0:T(8,128)(2,1)S(1)}, bf16[1152,256]{1,0:T(8,128)(2,1)S(1)}, u32[]{:S(2)}, u32[]{:S(2)}) collective-permute-start(bf16[1152,256]{1,0:T(8,128)(2,1)S(1)} %collective-permute-done.16.refs_4_), channel_id=1, source_target_pairs={{0,8},{4,12},{8,0},{12,4},{16,24},{20,28},{24,16},{28,20},{1,9},{5... | collective-permute-start | bytes 1769480 | tf_op jit(solution)/shard_map/ppermute | solution.py:306
  47.0 25.0 %collective-permute-start.20 = (bf16[1152,256]{1,0:T(8,128)(2,1)S(1)}, bf16[1152,256]{1,0:T(8,128)(2,1)S(1)}, u32[]{:S(2)}, u32[]{:S(2)}) collective-permute-start(bf16[1152,256]{1,0:T(8,128)(2,1)S(1)} %collective-permute-done.16.refs_4_), channel_id=1, source_target_pairs={{0,1},{1,2},{2,3},{3,0},{4,5},{5,6},{6,7},{7,4},{8,9},{9,10},{10,1... | collective-permute-start | bytes 1769480 | tf_op jit(solution)/shard_map/ppermute | solution.py:309
  48.6 24.3 %collective-permute-start.6 = (bf16[1536,256]{1,0:T(8,128)(2,1)S(1)}, bf16[1536,256]{1,0:T(8,128)(2,1)S(1)}, u32[]{:S(2)}, u32[]{:S(2)}) collective-permute-start(bf16[1536,256]{1,0:T(8,128)(2,1)S(1)} %collective-permute-done.4.refs_1_), channel_id=1, source_target_pairs={{0,16},{4,20},{8,24},{12,28},{16,0},{20,4},{24,8},{28,12},{1,17},{... | collective-permute-start | bytes 2359304 | tf_op jit(solution)/shard_map/ppermute | solution.py:306
  51.4 27.4 %collective-permute-start.18 = (bf16[1152,256]{1,0:T(8,128)(2,1)S(1)}, bf16[1152,256]{1,0:T(8,128)(2,1)S(1)}, u32[]{:S(2)}, u32[]{:S(2)}) collective-permute-start(bf16[1152,256]{1,0:T(8,128)(2,1)S(1)} %collective-permute-done.16.refs_4_), channel_id=1, source_target_pairs={{0,16},{4,20},{8,24},{12,28},{16,0},{20,4},{24,8},{28,12},{1,17},{... | collective-permute-start | bytes 1769480 | tf_op jit(solution)/shard_map/ppermute | solution.py:306
  60.6 83.8 %collective-permute-start.12 = (f32[12,1024]{1,0:T(8,128)S(1)}, f32[12,1024]{1,0:T(8,128)S(1)}, u32[]{:S(2)}, u32[]{:S(2)}) collective-permute-start(f32[12,1024]{1,0:T(8,128)S(1)} %add.196), channel_id=1, source_target_pairs={{0,2},{1,3},{2,0},{3,1},{4,6},{5,7},{6,4},{7,5},{8,10},{9,11},{10,... | collective-permute-start | bytes 147464 | tf_op jit(solution)/shard_map/ppermute | solution.py:306
  72.0 72.5 %collective-permute-start.2 = (bf16[256,1024]{1,0:T(8,128)(2,1)S(1)}, bf16[256,1024]{1,0:T(8,128)(2,1)}, u32[]{:S(2)}, u32[]{:S(2)}) collective-permute-start(bf16[256,1024]{1,0:T(8,128)(2,1)S(1)} %collective-permute-done.1.t2), channel_id=1, source_target_pairs={{0,1},{1,2},{2,3},{3,0},{4,5},{5,6},{6,7},{7,4},{8,9},{9,10},{10,1... | collective-permute-start | bytes 1572872 | tf_op jit(solution)/shard_map/ppermute | solution.py:309
  72.8 26.0 %collective-permute-start.21 = (bf16[1152,256]{1,0:T(8,128)(2,1)S(1)}, bf16[1152,256]{1,0:T(8,128)(2,1)S(1)}, u32[]{:S(2)}, u32[]{:S(2)}) collective-permute-start(bf16[1152,256]{1,0:T(8,128)(2,1)S(1)} %collective-permute-done.20.refs_8_), channel_id=1, source_target_pairs={{0,8},{4,12},{8,0},{12,4},{16,24},{20,28},{24,16},{28,20},{1,9},{5... | collective-permute-start | bytes 1769480 | tf_op jit(solution)/shard_map/ppermute | solution.py:306
  75.6 23.7 %collective-permute-start.24 = (bf16[1152,256]{1,0:T(8,128)(2,1)S(1)}, bf16[1152,256]{1,0:T(8,128)(2,1)S(1)}, u32[]{:S(2)}, u32[]{:S(2)}) collective-permute-start(bf16[1152,256]{1,0:T(8,128)(2,1)S(1)} %collective-permute-done.20.refs_8_), channel_id=1, source_target_pairs={{0,1},{1,2},{2,3},{3,0},{4,5},{5,6},{6,7},{7,4},{8,9},{9,10},{10,1... | collective-permute-start | bytes 1769480 | tf_op jit(solution)/shard_map/ppermute | solution.py:309
  78.8 18.4 %collective-permute-start.19 = (bf16[1152,256]{1,0:T(8,128)(2,1)S(1)}, bf16[1152,256]{1,0:T(8,128)(2,1)S(1)}, u32[]{:S(2)}, u32[]{:S(2)}) collective-permute-start(bf16[1152,256]{1,0:T(8,128)(2,1)S(1)} %collective-permute-done.18.refs_6_), channel_id=1, source_target_pairs={{0,8},{4,12},{8,0},{12,4},{16,24},{20,28},{24,16},{28,20},{1,9},{5... | collective-permute-start | bytes 1769480 | tf_op jit(solution)/shard_map/ppermute | solution.py:306
  97.3 16.3 %collective-permute-start.22 = (bf16[1152,256]{1,0:T(8,128)(2,1)S(1)}, bf16[1152,256]{1,0:T(8,128)(2,1)S(1)}, u32[]{:S(2)}, u32[]{:S(2)}) collective-permute-start(bf16[1152,256]{1,0:T(8,128)(2,1)S(1)} %collective-permute-done.20.refs_8_), channel_id=1, source_target_pairs={{0,16},{4,20},{8,24},{12,28},{16,0},{20,4},{24,8},{28,12},{1,17},{... | collective-permute-start | bytes 1769480 | tf_op jit(solution)/shard_map/ppermute | solution.py:306
  98.8 27.4 %collective-permute-start.23 = (bf16[1152,256]{1,0:T(8,128)(2,1)S(1)}, bf16[1152,256]{1,0:T(8,128)(2,1)S(1)}, u32[]{:S(2)}, u32[]{:S(2)}) collective-permute-start(bf16[1152,256]{1,0:T(8,128)(2,1)S(1)} %collective-permute-done.21.refs_9_), channel_id=1, source_target_pairs={{0,16},{4,20},{8,24},{12,28},{16,0},{20,4},{24,8},{28,12},{1,17},{... | collective-permute-start | bytes 1769480 | tf_op jit(solution)/shard_map/ppermute | solution.py:306
  99.3 34.1 %collective-permute-start.26 = (bf16[1152,256]{1,0:T(8,128)(2,1)S(1)}, bf16[1152,256]{1,0:T(8,128)(2,1)S(1)}, u32[]{:S(2)}, u32[]{:S(2)}) collective-permute-start(bf16[1152,256]{1,0:T(8,128)(2,1)S(1)} %collective-permute-done.24.refs_12_), channel_id=1, source_target_pairs={{0,16},{4,20},{8,24},{12,28},{16,0},{20,4},{24,8},{28,12},{1,17},{... | collective-permute-start | bytes 1769480 | tf_op jit(solution)/shard_map/ppermute | solution.py:306
  113.5 22.7 %collective-permute-start.25 = (bf16[1152,256]{1,0:T(8,128)(2,1)S(1)}, bf16[1152,256]{1,0:T(8,128)(2,1)S(1)}, u32[]{:S(2)}, u32[]{:S(2)}) collective-permute-start(bf16[1152,256]{1,0:T(8,128)(2,1)S(1)} %collective-permute-done.24.refs_12_), channel_id=1, source_target_pairs={{0,8},{4,12},{8,0},{12,4},{16,24},{20,28},{24,16},{28,20},{1,9},{5... | collective-permute-start | bytes 1769480 | tf_op jit(solution)/shard_map/ppermute | solution.py:306
  126.2 18.3 %collective-permute-start.7 = (bf16[1536,256]{1,0:T(8,128)(2,1)}, bf16[1536,256]{1,0:T(8,128)(2,1)S(1)}, u32[]{:S(2)}, u32[]{:S(2)}) collective-permute-start(bf16[1536,256]{1,0:T(8,128)(2,1)} %slice_dynamic-update-slice_fusion.own), channel_id=1, source_target_pairs={{0,4},{4,0},{8,12},{12,8},{16,20},{20,16},{24,28},{28,24},{1,5},{5... | collective-permute-start | bytes 2359304 | tf_op jit(solution)/shard_map/ppermute | solution.py:306
  144.1 32.0 %collective-permute-start.28 = (bf16[2048,256]{1,0:T(8,128)(2,1)}, bf16[2048,256]{1,0:T(8,128)(2,1)}, u32[]{:S(2)}, u32[]{:S(2)}) collective-permute-start(bf16[2048,256]{1,0:T(8,128)(2,1)} %constant_dynamic-update-slice_fusion.15), channel_id=1, source_target_pairs={{0,4},{4,0},{8,12},{12,8},{16,20},{20,16},{24,28},{28,24},{1,5},{5... | collective-permute-start | bytes 3145736 | tf_op jit(solution)/shard_map/ppermute | solution.py:306
  161.9 14.2 %collective-permute-start.14 = (bf16[256,256]{1,0:T(8,128)(2,1)S(1)}, bf16[256,256]{1,0:T(8,128)(2,1)S(1)}, u32[]{:S(2)}, u32[]{:S(2)}) collective-permute-start(bf16[256,256]{1,0:T(8,128)(2,1)S(1)} %get-tuple-element.77), channel_id=1, source_target_pairs={{0,2},{1,3},{2,0},{3,1},{4,6},{5,7},{6,4},{7,5},{8,10},{9,11},{10,... | collective-permute-start | bytes 393224 | tf_op jit(solution)/shard_map/ppermute | solution.py:473
  214.4 17.0 %collective-permute-start.32 = (bf16[256,1024]{1,0:T(8,128)(2,1)}, bf16[256,1024]{1,0:T(8,128)(2,1)}, u32[]{:S(2)}, u32[]{:S(2)}) collective-permute-start(bf16[256,1024]{1,0:T(8,128)(2,1)} %get-tuple-element.88), channel_id=1, source_target_pairs={{0,4},{4,0},{8,12},{12,8},{16,20},{20,16},{24,28},{28,24},{1,5},{5... | collective-permute-start | bytes 1572872 | tf_op jit(solution)/shard_map/ppermute | solution.py:306
  218.8 65.9 %collective-permute-start.51 = (bf16[1024,256]{1,0:T(8,128)(2,1)}, bf16[1024,256]{1,0:T(8,128)(2,1)}, u32[]{:S(2)}, u32[]{:S(2)}) collective-permute-start(bf16[1024,256]{1,0:T(8,128)(2,1)} %get-tuple-element.115), channel_id=1, source_target_pairs={{0,16},{4,20},{8,24},{12,28},{16,0},{20,4},{24,8},{28,12},{1,17},{... | collective-permute-start | bytes 1572872 | tf_op jit(solution)/shard_map/ppermute | solution.py:306
  225.2 67.1 %collective-permute-start.55 = (bf16[1024,256]{1,0:T(8,128)(2,1)}, bf16[1024,256]{1,0:T(8,128)(2,1)}, u32[]{:S(2)}, u32[]{:S(2)}) collective-permute-start(bf16[1024,256]{1,0:T(8,128)(2,1)} %get-tuple-element.120), channel_id=1, source_target_pairs={{0,8},{4,12},{8,0},{12,4},{16,24},{20,28},{24,16},{28,20},{1,9},{5... | collective-permute-start | bytes 1572872 | tf_op jit(solution)/shard_map/ppermute | solution.py:306
  251.9 45.0 %collective-permute-start.57 = (bf16[1024,256]{1,0:T(8,128)(2,1)}, bf16[1024,256]{1,0:T(8,128)(2,1)}, u32[]{:S(2)}, u32[]{:S(2)}) collective-permute-start(bf16[1024,256]{1,0:T(8,128)(2,1)} %get-tuple-element.123), channel_id=1, source_target_pairs={{0,16},{4,20},{8,24},{12,28},{16,0},{20,4},{24,8},{28,12},{1,17},{... | collective-permute-start | bytes 1572872 | tf_op jit(solution)/shard_map/ppermute | solution.py:306
  256.5 38.5 %collective-permute-start.61 = (bf16[1024,256]{1,0:T(8,128)(2,1)}, bf16[1024,256]{1,0:T(8,128)(2,1)}, u32[]{:S(2)}, u32[]{:S(2)}) collective-permute-start(bf16[1024,256]{1,0:T(8,128)(2,1)} %get-tuple-element.128), channel_id=1, source_target_pairs={{0,8},{4,12},{8,0},{12,4},{16,24},{20,28},{24,16},{28,20},{1,9},{5... | collective-permute-start | bytes 1572872 | tf_op jit(solution)/shard_map/ppermute | solution.py:306
  257.1 24.1 %collective-permute-start.71 = (f32[10,1024]{1,0:T(8,128)S(1)}, f32[10,1024]{1,0:T(8,128)S(1)}, u32[]{:S(2)}, u32[]{:S(2)}) collective-permute-start(f32[10,1024]{1,0:T(8,128)S(1)} %fusion.19), channel_id=1, source_target_pairs={{0,8},{4,12},{8,0},{12,4},{16,24},{20,28},{24,16},{28,20},{1,9},{5... | collective-permute-start | bytes 122888 | tf_op jit(solution)/shard_map/ppermute | solution.py:306
  284.7 14.9 %collective-permute-start.72 = (f32[10,1024]{1,0:T(8,128)S(1)}, f32[10,1024]{1,0:T(8,128)S(1)}, u32[]{:S(2)}, u32[]{:S(2)}) collective-permute-start(f32[10,1024]{1,0:T(8,128)S(1)} %add.236), channel_id=1, source_target_pairs={{0,4},{4,0},{8,12},{12,8},{16,20},{20,16},{24,28},{28,24},{1,5},{5... | collective-permute-start | bytes 122888 | tf_op jit(solution)/shard_map/ppermute | solution.py:306
  284.7 17.7 %collective-permute-start.68 = (f32[2,256]{1,0:T(2,128)S(1)}, f32[2,256]{1,0:T(2,128)S(1)}, u32[]{:S(2)}, u32[]{:S(2)}) collective-permute-start(f32[2,256]{1,0:T(2,128)S(1)} %add.231), channel_id=1, source_target_pairs={{0,8},{4,12},{8,0},{12,4},{16,24},{20,28},{24,16},{28,20},{1,9},{5... | collective-permute-start | bytes 6152 | tf_op jit(solution)/shard_map/ppermute | solution.py:306
  292.3 87.8 %collective-permute-start.54 = (bf16[1024,256]{1,0:T(8,128)(2,1)S(1)}, bf16[1024,256]{1,0:T(8,128)(2,1)S(1)}, u32[]{:S(2)}, u32[]{:S(2)}) collective-permute-start(bf16[1024,256]{1,0:T(8,128)(2,1)S(1)} %copy-done.25), channel_id=1, source_target_pairs={{0,8},{4,12},{8,0},{12,4},{16,24},{20,28},{24,16},{28,20},{1,9},{5... | collective-permute-start | bytes 1572872 | tf_op jit(solution)/shard_map/ppermute | solution.py:306
  295.0 22.6 %collective-permute-start.60 = (bf16[1024,256]{1,0:T(8,128)(2,1)S(1)}, bf16[1024,256]{1,0:T(8,128)(2,1)S(1)}, u32[]{:S(2)}, u32[]{:S(2)}) collective-permute-start(bf16[1024,256]{1,0:T(8,128)(2,1)S(1)} %copy-done.29), channel_id=1, source_target_pairs={{0,8},{4,12},{8,0},{12,4},{16,24},{20,28},{24,16},{28,20},{1,9},{5... | collective-permute-start | bytes 1572872 | tf_op jit(solution)/shard_map/ppermute | solution.py:306
  296.9 22.1 %collective-permute-start.62 = (bf16[1024,256]{1,0:T(8,128)(2,1)S(1)}, bf16[1024,256]{1,0:T(8,128)(2,1)S(1)}, u32[]{:S(2)}, u32[]{:S(2)}) collective-permute-start(bf16[1024,256]{1,0:T(8,128)(2,1)S(1)} %add.224), channel_id=1, source_target_pairs={{0,16},{4,20},{8,24},{12,28},{16,0},{20,4},{24,8},{28,12},{1,17},{... | collective-permute-start | bytes 1572872 | tf_op jit(solution)/shard_map/ppermute | solution.py:306
  307.5 23.2 %collective-permute-start.39 = (bf16[1536,256]{1,0:T(8,128)(2,1)}, bf16[1536,256]{1,0:T(8,128)(2,1)S(1)}, u32[]{:S(2)}, u32[]{:S(2)}) collective-permute-start(bf16[1536,256]{1,0:T(8,128)(2,1)} %get-tuple-element.107), channel_id=1, source_target_pairs={{0,4},{4,0},{8,12},{12,8},{16,20},{20,16},{24,28},{28,24},{1,5},{5... | collective-permute-start | bytes 2359304 | tf_op jit(solution)/shard_map/ppermute | solution.py:306
  314.0 15.5 %collective-permute-start.36 = (bf16[256,1024]{1,0:T(8,128)(2,1)S(1)}, bf16[256,1024]{1,0:T(8,128)(2,1)S(1)}, u32[]{:S(2)}, u32[]{:S(2)}) collective-permute-start(bf16[256,1024]{1,0:T(8,128)(2,1)S(1)} %copy-done.31), channel_id=1, source_target_pairs={{0,1},{1,2},{2,3},{3,0},{4,5},{5,6},{6,7},{7,4},{8,9},{9,10},{10,1... | collective-permute-start | bytes 1572872 | tf_op jit(solution)/shard_map/ppermute | solution.py:309
  317.6 16.0 %collective-permute-start.59 = (bf16[1024,256]{1,0:T(8,128)(2,1)S(1)}, bf16[1024,256]{1,0:T(8,128)(2,1)S(1)}, u32[]{:S(2)}, u32[]{:S(2)}) collective-permute-start(bf16[1024,256]{1,0:T(8,128)(2,1)S(1)} %copy-done.27), channel_id=1, source_target_pairs={{0,16},{4,20},{8,24},{12,28},{16,0},{20,4},{24,8},{28,12},{1,17},{... | collective-permute-start | bytes 1572872 | tf_op jit(solution)/shard_map/ppermute | solution.py:306
  319.0 13.3 %collective-permute-start.43 = (bf16[2048,256]{1,0:T(8,128)(2,1)S(1)}, bf16[2048,256]{1,0:T(8,128)(2,1)S(1)}, u32[]{:S(2)}, u32[]{:S(2)}) collective-permute-start(bf16[2048,256]{1,0:T(8,128)(2,1)S(1)} %copy-done.63), channel_id=1, source_target_pairs={{0,4},{4,0},{8,12},{12,8},{16,20},{20,16},{24,28},{28,24},{1,5},{5... | collective-permute-start | bytes 3145736 | tf_op jit(solution)/shard_map/ppermute | solution.py:306
  329.5 50.6 %collective-permute-start.56 = (bf16[1024,256]{1,0:T(8,128)(2,1)S(1)}, bf16[1024,256]{1,0:T(8,128)(2,1)S(1)}, u32[]{:S(2)}, u32[]{:S(2)}) collective-permute-start(bf16[1024,256]{1,0:T(8,128)(2,1)S(1)} %add.218), channel_id=1, source_target_pairs={{0,16},{4,20},{8,24},{12,28},{16,0},{20,4},{24,8},{28,12},{1,17},{... | collective-permute-start | bytes 1572872 | tf_op jit(solution)/shard_map/ppermute | solution.py:306
  330.7 12.8 %collective-permute-start.58 = (bf16[1024,256]{1,0:T(8,128)(2,1)S(1)}, bf16[1024,256]{1,0:T(8,128)(2,1)S(1)}, u32[]{:S(2)}, u32[]{:S(2)}) collective-permute-start(bf16[1024,256]{1,0:T(8,128)(2,1)S(1)} %add.220), channel_id=1, source_target_pairs={{0,8},{4,12},{8,0},{12,4},{16,24},{20,28},{24,16},{28,20},{1,9},{5... | collective-permute-start | bytes 1572872 | tf_op jit(solution)/shard_map/ppermute | solution.py:306
  332.3 16.7 %collective-permute-start.63 = (bf16[1024,256]{1,0:T(8,128)(2,1)S(1)}, bf16[1024,256]{1,0:T(8,128)(2,1)S(1)}, u32[]{:S(2)}, u32[]{:S(2)}) collective-permute-start(bf16[1024,256]{1,0:T(8,128)(2,1)S(1)} %add_convert_fusion.4), channel_id=1, source_target_pairs={{0,1},{1,2},{2,3},{3,0},{4,5},{5,6},{6,7},{7,4},{8,9},{9,10},{10,1... | collective-permute-start | bytes 1572872 | tf_op jit(solution)/shard_map/ppermute | solution.py:309
  333.6 24.3 %collective-permute-start.37 = (bf16[256,1024]{1,0:T(8,128)(2,1)S(1)}, bf16[256,1024]{1,0:T(8,128)(2,1)S(1)}, u32[]{:S(2)}, u32[]{:S(2)}) collective-permute-start(bf16[256,1024]{1,0:T(8,128)(2,1)S(1)} %add_convert_fusion.6), channel_id=1, source_target_pairs={{0,1},{1,2},{2,3},{3,0},{4,5},{5,6},{6,7},{7,4},{8,9},{9,10},{10,1... | collective-permute-start | bytes 1572872 | tf_op jit(solution)/shard_map/ppermute | solution.py:309
  350.7 15.5 %collective-permute-start.40 = (bf16[384,256]{1,0:T(8,128)(2,1)S(1)}, bf16[384,256]{1,0:T(8,128)(2,1)S(1)}, u32[]{:S(2)}, u32[]{:S(2)}) collective-permute-start(bf16[384,256]{1,0:T(8,128)(2,1)S(1)} %get-tuple-element.141), channel_id=1, source_target_pairs={{0,8},{4,12},{8,0},{12,4},{16,24},{20,28},{24,16},{28,20},{1,9},{5... | collective-permute-start | bytes 589832 | tf_op jit(solution)/shard_map/ppermute | solution.py:306
  361.9 18.4 %collective-permute-start.64 = (bf16[1024,256]{1,0:T(8,128)(2,1)S(1)}, bf16[1024,256]{1,0:T(8,128)(2,1)S(1)}, u32[]{:S(2)}, u32[]{:S(2)}) collective-permute-start(bf16[1024,256]{1,0:T(8,128)(2,1)S(1)} %add_convert_fusion.3), channel_id=1, source_target_pairs={{0,1},{1,2},{2,3},{3,0},{4,5},{5,6},{6,7},{7,4},{8,9},{9,10},{10,1... | collective-permute-start | bytes 1572872 | tf_op jit(solution)/shard_map/ppermute | solution.py:309
  366.2 37.0 %collective-permute-start.53 = (bf16[1024,256]{1,0:T(8,128)(2,1)S(1)}, bf16[1024,256]{1,0:T(8,128)(2,1)S(1)}, u32[]{:S(2)}, u32[]{:S(2)}) collective-permute-start(bf16[1024,256]{1,0:T(8,128)(2,1)S(1)} %copy-done.23), channel_id=1, source_target_pairs={{0,16},{4,20},{8,24},{12,28},{16,0},{20,4},{24,8},{28,12},{1,17},{... | collective-permute-start | bytes 1572872 | tf_op jit(solution)/shard_map/ppermute | solution.py:306
  379.3 23.9 %collective-permute-start.52 = (bf16[1024,256]{1,0:T(8,128)(2,1)S(1)}, bf16[1024,256]{1,0:T(8,128)(2,1)S(1)}, u32[]{:S(2)}, u32[]{:S(2)}) collective-permute-start(bf16[1024,256]{1,0:T(8,128)(2,1)S(1)} %add.214), channel_id=1, source_target_pairs={{0,8},{4,12},{8,0},{12,4},{16,24},{20,28},{24,16},{28,20},{1,9},{5... | collective-permute-start | bytes 1572872 | tf_op jit(solution)/shard_map/ppermute | solution.py:306
  380.1 24.1 %collective-permute-start.38 = (bf16[256,1024]{1,0:T(8,128)(2,1)S(1)}, bf16[256,1024]{1,0:T(8,128)(2,1)S(1)}, u32[]{:S(2)}, u32[]{:S(2)}) collective-permute-start(bf16[256,1024]{1,0:T(8,128)(2,1)S(1)} %add_convert_fusion.5), channel_id=1, source_target_pairs={{0,1},{1,2},{2,3},{3,0},{4,5},{5,6},{6,7},{7,4},{8,9},{9,10},{10,1... | collective-permute-start | bytes 1572872 | tf_op jit(solution)/shard_map/ppermute | solution.py:309
  380.2 16.6 %collective-permute-start.48 = (bf16[128,256]{1,0:T(8,128)(2,1)S(1)}, bf16[128,256]{1,0:T(8,128)(2,1)S(1)}, u32[]{:S(2)}, u32[]{:S(2)}) collective-permute-start(bf16[128,256]{1,0:T(8,128)(2,1)S(1)} %fusion.2), channel_id=1, source_target_pairs={{0,1},{1,2},{2,3},{3,0},{4,5},{5,6},{6,7},{7,4},{8,9},{9,10},{10,1... | collective-permute-start | bytes 196616 | tf_op jit(solution)/shard_map/ppermute | solution.py:309
  380.5 22.7 %collective-permute-start.65 = (bf16[1024,256]{1,0:T(8,128)(2,1)S(1)}, bf16[1024,256]{1,0:T(8,128)(2,1)S(1)}, u32[]{:S(2)}, u32[]{:S(2)}) collective-permute-start(bf16[1024,256]{1,0:T(8,128)(2,1)S(1)} %add_convert_fusion.2), channel_id=1, source_target_pairs={{0,1},{1,2},{2,3},{3,0},{4,5},{5,6},{6,7},{7,4},{8,9},{9,10},{10,1... | collective-permute-start | bytes 1572872 | tf_op jit(solution)/shard_map/ppermute | solution.py:309
  (93 other events, 1472.0 us)

commit v2 on v1

v2 whole, which is shorter than its diff:
```python
import functools

import jax
import jax.numpy as jnp
from jax import lax
from jax.experimental import pallas as pl
from jax.experimental.pallas import tpu as pltpu
from jax.sharding import PartitionSpec as P

HEAD_DIM = 64
LENGTH = 1024
QUARTERS = 4
BLOCK = 256
HALF = 128
bf16 = jnp.bfloat16
f32 = jnp.float32
VMEM = pl.BlockSpec(memory_space=pltpu.VMEM)
SMEM = pl.BlockSpec(memory_space=pltpu.SMEM)
HBM = pl.BlockSpec(memory_space=pl.ANY)


RATE = 4e9
SPAN = {
    "prepare": 0.7,
    "assemble": 2.5,
    "pack_in": 2.5,
    "attend": 15.0,
    "pack_out": 1.6,
    "vectors": 1.6,
    "project": 5.0,
    "forward": 8.0,
    "second": 4.0,
    "backward": 10.5,
    "weights": 5.6,
    "first": 4.6,
    "output_grad": 2.9,
    "attend_back": 10.7,
    "token_grad": 5.0,
    "input_grad": 5.0,
}


def shape(dims, dtype):
    return jax.ShapeDtypeStruct(dims, dtype)


def call(kernel, name, operands, specs, outs, scratch=(), grid=()):
    return pl.pallas_call(
        kernel,
        grid=grid,
        name=name,
        out_shape=outs,
        in_specs=specs,
        out_specs=[VMEM] * len(outs),
        scratch_shapes=list(scratch),
        compiler_params=pltpu.CompilerParams(vmem_limit_bytes=26 << 20),
        cost_estimate=pl.CostEstimate(
            flops=int(SPAN[name] * RATE), bytes_accessed=0, transcendentals=0
        ),
    )(*operands)


def dot(left, right, dims=((1,), (0,))):
    return lax.dot_general(left, right, (dims, ((), ())), preferred_element_type=f32)


NT = ((1,), (1,))
TN = ((0,), (0,))


def norm_back(grad, normed, scale, gain):
    scaled = grad * gain
    return scale * (
        scaled
        - jnp.mean(scaled, -1, keepdims=True)
        - normed * jnp.mean(scaled * normed, -1, keepdims=True)
    )


def lanes(ids, j):
    return pl.ds(pl.multiple_of((ids[0] ^ j) * BLOCK, BLOCK), BLOCK)


def segments(ids, docs, dims, axis):
    place = lax.broadcasted_iota(jnp.int32, dims, axis)
    place = ((ids[2] - (place >> 8) + QUARTERS) & (QUARTERS - 1)) * BLOCK + (place & (BLOCK - 1))
    bound = docs[0, 0]
    total = (place >= bound).astype(jnp.int32)
    for j in range(1, 8):
        bound = bound + docs[0, j]
        total = total + (place >= bound).astype(jnp.int32)
    return total


SPLIT = (896, 512, 512, 512)


def find(blocks, k, j, row):
    cut = SPLIT[k]
    if j < 3:
        return blocks[k * 5 + j], row
    return (blocks[k * 5 + 3], row) if row < cut else (blocks[k * 5 + 4], row - cut)


def place_w1(k):
    return k, 0


def place_w2(k):
    return k, SPLIT[k]


def place_wo(k):
    return {0: (0, 1408), 1: (1, 1024), 2: (2, 1024), 3: (0, 1536)}[k]


def place_vectors(k):
    return {0: (0, 1664), 1: (1, 1152), 2: (2, 1152), 3: (0, 1696)}[k]


def prepare_kernel(ids, six, two, inner, wo, out):
    out[:BLOCK, :] = wo[...]
    out[BLOCK:, :] = jnp.zeros((32, HALF), bf16)
    size = six.shape[1]
    row = lax.broadcasted_iota(jnp.int32, (size, HALF), 0)
    col = lax.broadcasted_iota(jnp.int32, (size, HALF), 1)
    here = (col == row + ids[2] * size).astype(bf16)
    out[BLOCK : BLOCK + 6, :] = dot(six[...], here).astype(bf16)
    for half in range(2):
        here = (col + half * HALF == row + ids[3] * size).astype(bf16)
        at = BLOCK + half * 16
        out[at + 6 : at + 8, :] = dot(two[...], here).astype(bf16)
    out[BLOCK + 8 : BLOCK + 9, :] = inner[...]


def assemble_kernel(ids, w1, r1, w2, r2, p, rp, pb, rpb, wq, wk, wv, first, block, sems):
    core = ids[1]
    copies = []

    def put(source, out, rows, size, cols=None):
        to = out.at[pl.ds(rows, size)] if cols is None else out.at[pl.ds(rows, size), cols]
        copies.append(pltpu.make_async_copy(source, to, sems.at[len(copies)]))

    for side, v1, v2, v, vb in ((core, w1, w2, p, pb), (1 - core, r1, r2, rp, rpb)):
        cols = pl.ds(pl.multiple_of(side * HALF, HALF), HALF)
        wide = pl.ds(pl.multiple_of(core * 512, 512), 512)
        deep = pl.ds(pl.multiple_of(core * HALF, HALF), HALF)
        for out, w2_at, wo_at, vec_at in ((first, 896, 1408, 1664), (block, 512, 1024, 1152)):
            for half in range(2):
                from_cols = pl.ds(pl.multiple_of(core * 512 + half * BLOCK, BLOCK), BLOCK)
                at = pl.multiple_of(half * BLOCK + side * HALF, HALF)
                put(v1.at[:, from_cols], out, at, HALF)
                piece = v.at[pl.ds(BLOCK + half * 16, 16)]
                at = pl.multiple_of(vec_at + side * 16, 16)
                put(piece, out, at, 16, pl.ds(half * HALF, HALF))
            put(v2.at[wide], out, w2_at, 512, cols)
            put(v.at[deep], out, wo_at, HALF, cols)
        put(vb.at[deep], first, 1536, HALF, cols)
        for half in range(2):
            piece = vb.at[pl.ds(BLOCK + half * 16, 16)]
            at = pl.multiple_of(1696 + side * 16, 16)
            put(piece, first, at, 16, pl.ds(half * HALF, HALF))
    for i, piece in enumerate((wq, wk, wv)):
        put(piece, first, 512 + i * HALF, HALF)
    for copy in copies:
        copy.start()
    for copy in copies:
        copy.wait()


def pack_in_kernel(p0, p1, p2, p3, v3, out, bias):
    total = jnp.zeros((2, BLOCK), f32)
    for j, part in enumerate((p0, p1, p2, p3)):
        out[j * 384 : (j + 1) * 384, :] = part[512:896, :]
        source, row = (part, 1664) if j < 3 else (v3, 1664 - 896)
        for side in range(2):
            vectors = source[row + side * 16 : row + side * 16 + 16, :].astype(f32)
            total = total + vectors[6:8, :]
    bias[...] = total


def pack_out_kernel(turns, count, *refs):
    blocks, out, sems = refs[:count], refs[count], refs[count + 1]
    copies = []
    for n, k in enumerate(turns):
        turn, row = place_wo(k)
        for j in range(4):
            ref, row_in = find(blocks, turn, j, row)
            i = n * 4 + j
            copies.append(
                pltpu.make_async_copy(
                    ref.at[pl.ds(row_in, HALF)], out.at[pl.ds(i * HALF, HALF)], sems.at[i]
                )
            )
    for copy in copies:
        copy.start()
    for copy in copies:
        copy.wait()


def vectors_kernel(ids, *refs):
    blocks = refs[:15]
    six, inner, held, sems = refs[15:]
    copies = []
    for k in range(4):
        turn, row = place_vectors(k)
        for j in range(4):
            ref, row_in = find(blocks, turn, j, row)
            i = k * 4 + j
            copies.append(
                pltpu.make_async_copy(
                    ref.at[pl.ds(row_in, 32)], held.at[pl.ds(i * 32, 32)], sems.at[i]
                )
            )
    for copy in copies:
        copy.start()
    inner[...] = jnp.zeros(inner.shape, f32)
    for copy in copies:
        copy.wait()
    for j in range(4):
        chip = ids[0] ^ j
        for side in range(2):
            total = jnp.zeros((8, HALF), f32)
            for k in range(4):
                row = (k * 4 + j) * 32 + side * 16
                piece = held[row : row + 16, :HALF].astype(f32)
                total = total + piece[:8, :]
                at = ((ids[2] - k + QUARTERS) & (QUARTERS - 1)) * 2 + (chip >> 1)
                lane = pl.ds(pl.multiple_of((chip & 1) * BLOCK + side * HALF, HALF), HALF)
                here = lax.broadcasted_iota(jnp.int32, (8, HALF), 0) == at
                inner[:, lane] += jnp.where(here, piece[8:9, :], 0.0)
            lane = pl.multiple_of(chip * BLOCK + side * HALF, HALF)
            six[:, pl.ds(lane, HALF)] = total


def attend_kernel(ids, docs, t0, t1, t2, t3, own, other, bias, q, k, v, w, m0, m1, m2, m3, lse):
    core = ids[1]
    for j in range(4):
        base = (ids[0] ^ j) * BLOCK
        for source, side in ((own, core), (other, 1 - core)):
            rows = pl.ds(pl.multiple_of(base + side * HALF, HALF), HALF)
            for i in range(3):
                at = (j * 3 + i) * HALF
                w[rows, i * BLOCK : (i + 1) * BLOCK] = source[at : at + HALF, :]
    for b, t in enumerate((t0, t1, t2, t3)):
        rows = slice(b * BLOCK, (b + 1) * BLOCK)
        made = dot(t[...], w[...])
        q[rows, :] = (made[:, :BLOCK] + bias[0:1, :]).astype(bf16)
        k[rows, :] = made[:, BLOCK : 2 * BLOCK].astype(bf16)
        v[rows, :] = (made[:, 2 * BLOCK :] + bias[1:2, :]).astype(bf16)
    along = segments(ids, docs, (1, LENGTH), 1)
    down = segments(ids, docs, (LENGTH, 1), 0)
    for b, mixed in enumerate((m0, m1, m2, m3)):
        rows = slice(b * BLOCK, (b + 1) * BLOCK)
        same = down[rows] == along
        for h in range(4):
            cols = slice(h * HEAD_DIM, (h + 1) * HEAD_DIM)
            scores = dot(q[rows, cols] * bf16(0.125), k[:, cols], NT)
            scores = jnp.where(same, scores, -1e30)
            top = jnp.max(scores, -1, keepdims=True)
            expo = jnp.exp(scores - top)
            total = jnp.sum(expo, -1, keepdims=True)
            shares = (expo * (1.0 / total)).astype(bf16)
            mixed[:, cols] = dot(shares, v[:, cols]).astype(bf16)
            lse[rows, h : h + 1] = top + jnp.log(total)


def project_kernel(ids, tokens, x0, x1, x2, x3, other_a, other_b, vectors, *refs):
    blocks = refs[:15]
    wo, normed, scale, low, sems = refs[15:]
    core = ids[1]
    copies = []
    for n, k in enumerate((0, 3, 1, 2)):
        turn, row = place_wo(k)
        for j in range(4):
            ref, row_in = find(blocks, turn, j, row)
            got, at = (other_a, n * 4 + j) if n < 3 else (other_b, j)
            for i, (source, start, side) in enumerate(
                ((ref, row_in, core), (got, at * HALF, 1 - core))
            ):
                rows = pl.ds(pl.multiple_of(k * BLOCK + side * HALF, HALF), HALF)
                copies.append(
                    pltpu.make_async_copy(
                        source.at[pl.ds(start, HALF)],
                        wo.at[rows, lanes(ids, j)],
                        sems.at[(n * 4 + j) * 2 + i],
                    )
                )
    for copy in copies:
        copy.start()
    total = tokens[...].astype(f32) + vectors[0:1, :]
    for copy in copies:
        copy.wait()
    for k, x in enumerate((x0, x1, x2, x3)):
        total = total + dot(x[...], wo[k * BLOCK : (k + 1) * BLOCK, :])
    centered = total - jnp.mean(total, -1, keepdims=True)
    r = lax.rsqrt(jnp.mean(centered * centered, -1, keepdims=True) + 1e-05)
    n = centered * r
    normed[...] = n
    scale[...] = jnp.broadcast_to(r, scale.shape)
    low[...] = (n * vectors[2:3, :] + vectors[3:4, :]).astype(bf16)


def w1_of(blocks, k, j, half):
    ref, row = find(blocks, k, j, half * BLOCK)
    return ref[row : row + BLOCK, :]


def w2_of(blocks, k, j):
    ref, row = find(blocks, k, j, SPLIT[k])
    return ref[row : row + 512, :]


def part_of(rows, j):
    return rows[:, j * BLOCK : (j + 1) * BLOCK]


def arrange(ids, rows, mine, theirs):
    for j in range(4):
        rows[:BLOCK, j * BLOCK : (j + 1) * BLOCK] = mine[:, lanes(ids, j)]
        rows[BLOCK:, j * BLOCK : (j + 1) * BLOCK] = theirs[:, lanes(ids, j)]


def gelu_parts(inner):
    density = jnp.exp2(inner * inner * -0.7213475204444817) * 0.3989422804014327
    base = 1.0 + 0.2316419 * jnp.abs(inner)
    t = pl.reciprocal(base, approx=True)
    t = t * (2.0 - base * t)
    tail = 1.330274429 * t - 1.821255978
    tail = tail * t + 1.781477937
    tail = tail * t - 0.356563782
    tail = (tail * t + 0.319381530) * t * density
    phi = jnp.where(inner >= 0.0, 1.0 - tail, tail)
    return inner * phi, phi + inner * density


def forward_kernel(turns, ids, mine, theirs, bias, *refs):
    count = 5 * len(turns)
    blocks, refs = (None,) * (turns[0] * 5) + refs[:count], refs[count:]
    if turns[0] == 0:
        start = None
    else:
        start, refs = refs[:2], refs[2:]
    active, slope, out_mine, out_theirs, rows, total = refs
    arrange(ids, rows, mine, theirs)
    if start is not None:
        arrange(ids, total, *start)

    def inner_of(n, half):
        k = turns[n]
        at = ((ids[2] - k + QUARTERS) & (QUARTERS - 1)) * 2 + ids[1]
        offset = bias[pl.ds(at, 1), half * BLOCK : (half + 1) * BLOCK]
        total = dot(part_of(rows, 0), w1_of(blocks, k, 0, half)) + offset
        for j in range(1, 4):
            total = total + dot(part_of(rows, j), w1_of(blocks, k, j, half))
        return total

    steps = [(n, half) for n in range(len(turns)) for half in range(2)]
    inner = inner_of(*steps[0])
    for i, (n, half) in enumerate(steps):
        later = inner_of(*steps[i + 1]) if i + 1 < len(steps) else None
        span = slice(half * BLOCK, (half + 1) * BLOCK)
        deep = slice(n * 512, (n + 1) * 512)
        made, grown = gelu_parts(inner)
        active[deep, span] = made.astype(bf16)
        slope[deep, span] = grown.astype(bf16)
        if half == 1:
            for j in range(4):
                part = dot(active[deep, :], w2_of(blocks, turns[n], j))
                if n == 0 and start is None:
                    total[:, j * BLOCK : (j + 1) * BLOCK] = part
                else:
                    total[:, j * BLOCK : (j + 1) * BLOCK] += part
        inner = later
    for j in range(4):
        span = slice(j * BLOCK, (j + 1) * BLOCK)
        out_mine[:, lanes(ids, j)] = total[:BLOCK, span]
        out_theirs[:, lanes(ids, j)] = total[BLOCK:, span]


def second_kernel(normed, mine, got, vectors, cot, out, grad, low, sums):
    gain, shift = vectors[4:5, :], vectors[5:6, :]
    total = normed[...] * vectors[2:3, :] + vectors[3:4, :] + (mine[...] + got[...])
    total = total + vectors[1:2, :]
    centered = total - jnp.mean(total, -1, keepdims=True)
    r = lax.rsqrt(jnp.mean(centered * centered, -1, keepdims=True) + 1e-05)
    n = centered * r
    out[...] = (n * gain + shift).astype(bf16)
    up = cot[...].astype(f32)
    back = norm_back(up, n, r, gain)
    grad[...] = back
    low[...] = back.astype(bf16)
    sums[0:1, :] = jnp.sum(back, 0, keepdims=True)
    sums[1:2, :] = jnp.sum(up * n, 0, keepdims=True)
    sums[2:3, :] = jnp.sum(up, 0, keepdims=True)


def backward_kernel(ids, mine, theirs, slope0, slope1, *refs):
    blocks = refs[:20]
    back, out_mine, out_theirs, sums, rows, total = refs[20:]
    arrange(ids, rows, mine, theirs)
    sums[...] = jnp.zeros(sums.shape, f32)
    for k in range(4):
        span = slice(k * 512, (k + 1) * 512)
        made = dot(part_of(rows, 0), w2_of(blocks, k, 0), NT)
        for j in range(1, 4):
            made = made + dot(part_of(rows, j), w2_of(blocks, k, j), NT)
        grown = slope0[span, :] if k < 3 else slope1[...]
        made = (made * grown.astype(f32)).astype(bf16)
        back[span, :] = made
        at = ((ids[2] - k + QUARTERS) & (QUARTERS - 1)) * 2 + ids[1]
        sums[pl.ds(at, 1), :] = jnp.sum(made.astype(f32), 0, keepdims=True)
        for j in range(4):
            part = dot(made[:, :BLOCK], w1_of(blocks, k, j, 0), NT)
            part = part + dot(made[:, BLOCK:], w1_of(blocks, k, j, 1), NT)
            if k == 0:
                total[:, j * BLOCK : (j + 1) * BLOCK] = part
            else:
                total[:, j * BLOCK : (j + 1) * BLOCK] += part
    for j in range(4):
        span = slice(j * BLOCK, (j + 1) * BLOCK)
        out_mine[:, lanes(ids, j)] = total[:BLOCK, span]
        out_theirs[:, lanes(ids, j)] = total[BLOCK:, span].astype(bf16)


def weights_kernel(ids, active1, back1, active2, back2, mine, theirs, gmine, gtheirs, *outs):
    for j in range(4):
        at = lanes(ids, j)
        for active, back, out in ((active1, back1, outs[j]), (active2, back2, outs[4 + j])):
            left = dot(mine[:, at], back[:BLOCK, :], TN) + dot(theirs[:, at], back[BLOCK:, :], TN)
            out[:BLOCK, :] = left[:, :BLOCK].astype(bf16)
            out[BLOCK:512, :] = left[:, BLOCK:].astype(bf16)
            out[512:1024, :] = (
                dot(active[:BLOCK, :], gmine[:, at], TN)
                + dot(active[BLOCK:, :], gtheirs[:, at], TN)
            ).astype(bf16)


def first_kernel(second, mine, got, normed, scale, vectors, wo, grad, low, g0, g1, g2, g3, sums):
    hidden = second[...] + mine[...] + got[...].astype(f32)
    n = normed[...]
    back = norm_back(hidden, n, scale[:, :1], vectors[2:3, :])
    grad[...] = back
    rounded = back.astype(bf16)
    low[...] = rounded
    for k, g in enumerate((g0, g1, g2, g3)):
        g[...] = dot(rounded, wo[k * BLOCK : (k + 1) * BLOCK, :], NT).astype(bf16)
    sums[0:1, :] = jnp.sum(back, 0, keepdims=True)
    sums[1:2, :] = jnp.sum(hidden * n, 0, keepdims=True)
    sums[2:3, :] = jnp.sum(hidden, 0, keepdims=True)


def output_grad_kernel(ids, x0, x1, x2, x3, low, first, second, inner, own, send, made):
    core = ids[1]
    sums = jnp.concatenate([first[...], second[...], jnp.zeros((2, first.shape[1]), f32)], 0)
    for k, x in enumerate((x0, x1, x2, x3)):
        made[...] = dot(x[...], low[...], TN)
        for out, side in ((own, core), (send, 1 - core)):
            rows = pl.ds(pl.multiple_of(side * HALF, HALF), HALF)
            for j in range(4):
                at = j * 576 + k * 144
                out[at : at + HALF, :] = made[rows, lanes(ids, j)].astype(bf16)
    made[0:8, :] = sums
    for j in range(4):
        chip = ids[0] ^ j
        there = ((chip >> 1) == core).astype(f32)
        for k in range(4):
            at = ((ids[2] - k + QUARTERS) & (QUARTERS - 1)) * 2 + core
            row = inner[pl.ds(at, 1), :]
            row = jnp.where((chip & 1) == 0, row[:, :BLOCK], row[:, BLOCK:]) * there
            six = made[0:8, lanes(ids, j)]
            here = lax.broadcasted_iota(jnp.int32, (8, BLOCK), 0) == 6
            piece = jnp.concatenate([jnp.where(here, row, six), jnp.zeros((8, BLOCK), f32)], 0)
            at = j * 576 + k * 144 + HALF
            own[at : at + 16, :] = piece.astype(bf16)
            send[at : at + 16, :] = jnp.zeros((16, BLOCK), bf16)


def attend_back_kernel(heads, ids, docs, q, k, v, lse, g0, g1, g2, g3, out, sums, g, ktot, vtot):
    for b, part in enumerate((g0, g1, g2, g3)):
        g[b * BLOCK : (b + 1) * BLOCK, :] = part[...]
    along = segments(ids, docs, (1, LENGTH), 1)
    down = segments(ids, docs, (LENGTH, 1), 0)
    logs = jnp.transpose(lse[...])
    size = len(heads) * HEAD_DIM
    for b in range(4):
        rows = slice(b * BLOCK, (b + 1) * BLOCK)
        same = down == along[:, rows]
        for n, h in enumerate(heads):
            cols = slice(h * HEAD_DIM, (h + 1) * HEAD_DIM)
            to = slice(n * HEAD_DIM, (n + 1) * HEAD_DIM)
            scaled = q[rows, cols] * bf16(0.125)
            scores = dot(k[:, cols], scaled, NT)
            scores = jnp.where(same, scores, -1e30)
            shares = jnp.exp(scores - logs[h : h + 1, rows])
            dots = dot(v[:, cols], g[rows, cols], NT)
            product = shares * dots
            centre = jnp.sum(product, 0, keepdims=True)
            back = (product - shares * centre).astype(bf16)
            vpart = dot(shares.astype(bf16), g[rows, cols])
            kpart = dot(back, scaled)
            if b == 0:
                vtot[:, to] = vpart
                ktot[:, to] = kpart
            else:
                vtot[:, to] += vpart
                ktot[:, to] += kpart
            out[rows, to] = (dot(back, k[:, cols], TN) * 0.125).astype(bf16)
    out[:, size : 2 * size] = ktot[...].astype(bf16)
    out[:, 2 * size :] = vtot[...].astype(bf16)
    sums[0:1, :] = jnp.sum(out[:, :size].astype(f32), 0, keepdims=True)
    sums[1:2, :] = jnp.sum(out[:, 2 * size :].astype(f32), 0, keepdims=True)


def token_grad_kernel(low, high, w, wo, d0, d1, d2, d3, dqkv):
    for part, at in ((low, 0), (high, HALF)):
        for i in range(3):
            dqkv[:, i * BLOCK + at : i * BLOCK + at + HALF] = part[:, i * HALF : (i + 1) * HALF]
    for b, out in ((1, d1), (2, d2), (3, d3), (0, d0)):
        rows = slice(b * BLOCK, (b + 1) * BLOCK)
        out[:BLOCK, :] = dot(dqkv[rows, :], w[...], NT).astype(bf16)
        for i in range(3):
            at = b * 144 + i * 48
            out[BLOCK:, i * BLOCK : (i + 1) * BLOCK] = wo[at : at + 48, :]
        out[BLOCK:, 3 * BLOCK :] = jnp.zeros((48, BLOCK), bf16)


def input_grad_kernel(ids, t0, t1, t2, t3, dqkv, sums, own, send, made):
    core = ids[1]
    vectors = jnp.concatenate([sums[...], jnp.zeros((14, BLOCK), f32)], 0).astype(bf16)
    for j in range(4):
        for out in (own, send):
            out[j * 400 + 384 : (j + 1) * 400, :] = vectors
    for j in range(4):
        at = lanes(ids, j)
        total = dot(t0[:, at], dqkv[:BLOCK, :], TN)
        for b, t in ((1, t1), (2, t2), (3, t3)):
            total = total + dot(t[:, at], dqkv[b * BLOCK : (b + 1) * BLOCK, :], TN)
        made[...] = total
        for out, side in ((own, core), (send, 1 - core)):
            rows = pl.ds(pl.multiple_of(side * HALF, HALF), HALF)
            for i in range(3):
                to = j * 400 + i * HALF
                out[to : to + HALF, :] = made[rows, i * BLOCK : (i + 1) * BLOCK].astype(bf16)


def body_for(dp, tensor):
    fast = dp == 8 and tensor == 4
    ring_pairs = [(i, (i + 1) % tensor) for i in range(tensor)]

    def flip(value, bit, axis="dp", size=dp):
        return lax.ppermute(value, axis, [(i, i ^ bit) for i in range(size)])

    def ring(value):
        return lax.ppermute(value, "tensor", ring_pairs)

    def swap(value):
        return flip(value, 1)

    def sum_all(value, over_tensor=True):
        bit = dp >> 1
        while bit:
            value = value + flip(value, bit)
            bit >>= 1
        bit = 1
        while over_tensor and bit < tensor:
            value = value + flip(value, bit, "tensor", tensor)
            bit <<= 1
        return value

    def in_order(core, own, got, axis):
        return jnp.where(
            core == 0,
            jnp.concatenate([own, got], axis),
            jnp.concatenate([got, own], axis),
        )

    def after(value, *others):
        return lax.optimization_barrier((value, *others))[0]

    def assemble(ids, prepared, wq, wk, wv, w1, w2):
        pairs = [
            ((p * tensor + i), ((p ^ 1) * tensor + (i + tensor - 1) % tensor))
            for p in range(dp)
            for i in range(tensor)
        ]
        back = [(i, (i + tensor - 1) % tensor) for i in range(tensor)]
        ahead = lax.ppermute(prepared, "tensor", back)
        crossed = lax.ppermute(prepared, ("dp", "tensor"), pairs)
        made = call(
            assemble_kernel,
            "assemble",
            (ids, w1, swap(w1), w2, swap(w2), prepared, swap(prepared), ahead, crossed, wq, wk, wv),
            [SMEM] + [HBM] * 11,
            [shape((1728, BLOCK), bf16), shape((1184, BLOCK), bf16)],
            scratch=[pltpu.SemaphoreType.DMA((33,))],
        )
        return made, ahead

    def gather_any(core, z, wq, wk, wv, wo, w1, w2):
        def whole(value, dim):
            value = lax.all_gather(value, "dp", axis=dim, tiled=True)
            return value

        def quarters(value):
            value = lax.all_gather(value, "tensor", axis=0, tiled=False)
            return jnp.take(value, (z - jnp.arange(tensor)) % tensor, axis=0)

        a = quarters(lax.dynamic_slice_in_dim(whole(w1, 0), core * 512, 512, 1))
        b = quarters(lax.dynamic_slice_in_dim(whole(w2, 1), core * 512, 512, 0))
        c = quarters(lax.dynamic_slice_in_dim(whole(wo, 1), core * HALF, HALF, 0))
        qkv = jnp.stack([whole(wq, 0), whole(wk, 0), whole(wv, 0)])
        qkv = qkv.reshape(3, 4, 2, HALF, BLOCK).transpose(2, 1, 0, 3, 4).reshape(2, 1536, BLOCK)
        blocks = []
        for k in range(4):
            made = []
            for j in range(4):
                span = slice(j * BLOCK, (j + 1) * BLOCK)
                left = [a[k, span, :BLOCK], a[k, span, BLOCK:]]
                right = [b[k][:, span], c[k][:, span]]
                if k == 0:
                    left.append(jnp.zeros((384, BLOCK), bf16))
                    right += [c[3][:, span], jnp.zeros((64, BLOCK), bf16)]
                else:
                    right.append(jnp.zeros((32, BLOCK), bf16))
                made.append(jnp.concatenate(left + right, 0))
            blocks += made[:3] + [made[3][: SPLIT[k]], made[3][SPLIT[k] :]]
        return blocks, qkv[core], qkv[1 - core]

    def body(
        tokens,
        cotangent,
        doc_lengths,
        query_weight,
        key_weight,
        value_weight,
        output_weight,
        inner_weight,
        outer_weight,
        query_offset,
        value_offset,
        inner_offset,
        output_offset,
        outer_offset,
        first_gain,
        first_shift,
        second_gain,
        second_shift,
    ):
        place = lax.axis_index("dp")
        z = lax.axis_index("tensor")
        core = place & 1
        chip = (place >> 1) if fast else jnp.zeros_like(place)
        ids = jnp.stack([chip, core, z, place]).astype(jnp.int32)
        rows = tokens.shape[0]
        width = tokens.shape[1]

        six = jnp.stack(
            [output_offset, outer_offset, first_gain, first_shift, second_gain, second_shift]
        )
        two = jnp.stack([query_offset, value_offset])
        weights = (query_weight, key_weight, value_weight)
        t = [tokens]
        if fast:
            prepared = call(
                prepare_kernel,
                "prepare",
                (ids, six, two, inner_offset[None], output_weight),
                [SMEM] + [VMEM] * 4,
                [shape((BLOCK + 32, HALF), bf16)],
            )[0]
            (first, block), ahead = assemble(
                ids, prepared, *weights, inner_weight, outer_weight
            )
            t.append(ring(after(tokens, ahead)))

            def spread(k, own, by_x, by_y):
                cut = SPLIT[k]
                return flip(by_x[:cut], 4), flip(by_y[cut:], 2)

            x0, y0, z1 = flip(first, 2), flip(first, 4), ring(block)
            t.append(ring(t[1]))
            z1, x0, y0, t[2] = lax.optimization_barrier((z1, x0, y0, t[2]))
            x1, y1, z2 = flip(z1, 2), flip(z1, 4), ring(z1)
            a0, b0 = spread(0, first, x0, y0)
            t.append(ring(t[2]))
            z2, x1, y1, a0, b0, t[3] = lax.optimization_barrier((z2, x1, y1, a0, b0, t[3]))
            x2, y2, z3 = flip(z2, 2), flip(z2, 4), ring(z2)
            a1, b1 = spread(1, z1, x1, y1)
            own_in, qv_bias = call(
                pack_in_kernel,
                "pack_in",
                (first, x0, y0, a0, b0),
                [VMEM] * 5,
                [shape((1536, BLOCK), bf16), shape((2, BLOCK), f32)],
            )
            other_in = swap(own_in)
        else:
            piece = six.shape[1]
            field = jnp.arange(width) // piece == place * tensor + z
            six = jnp.where(field, jnp.tile(six.astype(f32), (1, width // piece)), 0)
            piece = two.shape[1]
            field = jnp.arange(width) // piece == z * dp + place
            two = jnp.where(field, jnp.tile(two.astype(f32), (1, width // piece)), 0)
            piece = inner_offset.shape[0]
            wide = piece * dp * tensor
            field = jnp.arange(wide) // piece == z * dp + place
            one = jnp.where(field, jnp.tile(inner_offset.astype(f32), wide // piece), 0)
            vectors = sum_all(jnp.concatenate([six, two, one.reshape(4, width)], 0))
            qv_bias = lax.dynamic_slice(vectors, (6, z * BLOCK), (2, BLOCK))
            inner_bias = vectors[8:12].reshape(8, 512)
            vectors = vectors[:8]
            blocks, own_in, other_in = gather_any(
                core, z, *weights, output_weight, inner_weight, outer_weight
            )
            for _ in range(3):
                t.append(ring(t[-1]))

        square = shape((LENGTH, BLOCK), bf16)
        tile = shape((BLOCK, BLOCK), bf16)
        q, k, v, w_in, m0, m1, m2, m3, lse = call(
            attend_kernel,
            "attend",
            (ids, doc_lengths, *t, own_in, other_in, qv_bias),
            [SMEM, SMEM] + [VMEM] * 7,
            [square] * 3
            + [shape((width, 3 * BLOCK), bf16)]
            + [tile] * 4
            + [shape((LENGTH, HALF), f32)],
        )

        def shift(value, by):
            return lax.ppermute(value, "tensor", [(i, (i - by) % tensor) for i in range(tensor)])

        if fast:
            z3, x2, y2, a1, b1, m0 = lax.optimization_barrier((z3, x2, y2, a1, b1, m0))
            x3, y3 = flip(z3, 2), flip(z3, 4)
            a2, b2 = spread(2, z2, x2, y2)
        x = [m0, shift(m3, 3), shift(m2, 2), shift(m1, 1)]

        def pack_out(turns, blocks):
            size = len(turns) * 4
            return swap(
                call(
                    functools.partial(pack_out_kernel, turns, len(blocks)),
                    "pack_out",
                    tuple(blocks),
                    [HBM] * len(blocks),
                    [shape((size * HALF, BLOCK), bf16)],
                    scratch=[pltpu.SemaphoreType.DMA((size,))],
                )[0]
            )

        if fast:
            blocks = [first, x0, y0, a0, b0, z1, x1, y1, a1, b1]
        other_a = pack_out((0, 3, 1), blocks[:10])
        if fast:
            x3, y3, a2, b2, *x = lax.optimization_barrier((x3, y3, a2, b2, *x))
            a3, b3 = spread(3, z3, x3, y3)
            blocks += [z2, x2, y2, a2, b2, z3, x3, y3, a3, b3]
            vectors, inner_bias = call(
                vectors_kernel,
                "vectors",
                (ids, *blocks[:15]),
                [SMEM] + [HBM] * 15,
                [shape((8, width), f32), shape((8, 512), f32)],
                scratch=[pltpu.VMEM((512, BLOCK), bf16), pltpu.SemaphoreType.DMA((16,))],
            )
        other_b = pack_out((2,), blocks[:15])
        wide_f = shape((rows, width), f32)
        wide_b = shape((rows, width), bf16)
        w_out, normed1, scale1, hidden_low = call(
            project_kernel,
            "project",
            (ids, tokens, *x, other_a, other_b, vectors, *blocks[:15]),
            [SMEM] + [VMEM] * 5 + [HBM] * 2 + [VMEM] + [HBM] * 15,
            [shape((width, width), bf16), wide_f, shape((rows, HALF), f32), wide_b],
            scratch=[pltpu.SemaphoreType.DMA((32,))],
        )
        hidden_other = swap(hidden_low)

        def forward(turns, *start):
            count = len(turns)
            tall = shape((count * 512, 512), bf16)
            return call(
                functools.partial(forward_kernel, turns),
                "forward",
                (ids, hidden_low, hidden_other, inner_bias)
                + tuple(blocks[turns[0] * 5 : turns[-1] * 5 + 5])
                + start,
                [SMEM] + [VMEM] * (3 + 5 * count + len(start)),
                [tall, tall, wide_f, wide_f],
                scratch=[
                    pltpu.VMEM((2 * rows, width), bf16),
                    pltpu.VMEM((2 * rows, width), f32),
                ],
            )

        active0, slope0, out_own, out_send = forward((0, 1, 2))
        active1, slope1, out_own, out_send = forward((3,), out_own, out_send)
        result, second_grad, second_low, second_sums = call(
            second_kernel,
            "second",
            (
                normed1,
                out_own,
                swap(out_send),
                vectors,
                cotangent,
            ),
            [VMEM] * 5,
            [wide_b, wide_f, wide_b, shape((3, width), f32)],
        )
        second_other = swap(second_low)
        tall = shape((2048, 512), bf16)
        back, grad_own, grad_send, inner_sums = call(
            backward_kernel,
            "backward",
            (ids, second_low, second_other, slope0, slope1, *blocks),
            [SMEM] + [VMEM] * 24,
            [tall, wide_f, wide_b, shape((8, 512), f32)],
            scratch=[
                pltpu.VMEM((2 * rows, width), bf16),
                pltpu.VMEM((2 * rows, width), f32),
            ],
        )

        def weights_of(turns, *others):
            def at(turn):
                return pl.BlockSpec((512, 512), lambda i: (turn, 0))

            def active_of(turn):
                return (active0, at(turn)) if turn < 3 else (active1, at(0))

            (a, a_at), (b, b_at) = active_of(turns[0]), active_of(turns[1])
            made = call(
                weights_kernel,
                "weights",
                (
                    ids,
                    a,
                    back,
                    b,
                    back,
                    hidden_low,
                    hidden_other,
                    second_low,
                    after(second_other, *others),
                ),
                [SMEM, a_at, at(turns[0]), b_at, at(turns[1])] + [VMEM] * 4,
                [shape((1024, BLOCK), bf16)] * 8,
                grid=(1,),
            )
            return {turns[0]: made[:4], turns[1]: made[4:]}

        grad_got = swap(grad_send)
        grads = weights_of((1, 2))
        first_grad, first_low, g0, g1, g2, g3, first_sums = call(
            first_kernel,
            "first",
            (
                second_grad,
                grad_own,
                after(grad_got, *grads[1]),
                normed1,
                scale1,
                vectors,
                w_out,
            ),
            [VMEM] * 7,
            [wide_f, wide_b] + [tile] * 4 + [shape((3, width), f32)],
        )
        g = [g0, shift(g3, 3), shift(g2, 2), shift(g1, 1)]
        grads.update(weights_of((3, 0), first_low))

        def meet(parts, turn):
            own, by_x, by_y, far = parts
            if turn % 2 == 0:
                return [own, by_x + flip(far, 4), by_y]
            return [own, by_x, by_y + flip(far, 2)]

        out_part = shape((2304, BLOCK), bf16)
        wo_own, wo_send = call(
            output_grad_kernel,
            "output_grad",
            (ids, *x, first_low, first_sums, second_sums, inner_sums),
            [SMEM] + [VMEM] * 8,
            [out_part, out_part],
            scratch=[pltpu.VMEM((BLOCK, width), f32)],
        )
        if fast:
            met = {turn: meet(grads[turn], turn) for turn in (1, 2)}
            wo_got = swap(wo_send)
            g[0] = after(g[0], met[1][2], met[2][1])

            def send(turn):
                return flip(met[turn][1], 2), flip(met[turn][2], 4)

            sent = {turn: send(turn) for turn in (1, 2)}

            def settle(turn, moving=None):
                total = (
                    met[turn][0].astype(f32)
                    + sent[turn][0].astype(f32)
                    + sent[turn][1].astype(f32)
                )
                return total if moving is None else total + moving.astype(f32)

        def attend_back(heads, g):
            size = len(heads) * HEAD_DIM
            return call(
                functools.partial(attend_back_kernel, heads),
                "attend_back",
                (ids, doc_lengths, q, k, v, lse, *g),
                [SMEM, SMEM] + [VMEM] * 8,
                [shape((LENGTH, 3 * size), bf16), shape((2, size), f32)],
                scratch=[
                    pltpu.VMEM((LENGTH, BLOCK), bf16),
                    pltpu.VMEM((LENGTH, size), f32),
                    pltpu.VMEM((LENGTH, size), f32),
                ],
            )

        if fast:
            wo_total = (wo_own.astype(f32) + wo_got.astype(f32)).astype(bf16)
            wo_parts = [wo_total[j * 576 : (j + 1) * 576] for j in range(4)]
            wo_far = flip(wo_parts[3], 4)
        dqkv_low, sums_low = attend_back((0, 1), g)
        if fast:
            gated = [*grads[3][1:3], *grads[0][1:3], *sent[1], wo_far, dqkv_low]
            gated = lax.optimization_barrier(tuple(gated))
            met[3] = meet([grads[3][0], *gated[0:2], grads[3][3]], 3)
            met[0] = meet([grads[0][0], *gated[2:4], grads[0][3]], 0)
            sent.update({turn: send(turn) for turn in (3, 0)})
            sent[1] = gated[4:6]
            total1 = settle(1).astype(bf16)
            moving1 = ring(total1)
            wo_x = flip(wo_parts[1] + gated[6], 2)
            wo_y = flip(wo_parts[2], 4)
            g[0] = after(g[0], dqkv_low, met[3][2], met[0][1], total1)
        dqkv_high, sums_high = attend_back((2, 3), g)
        head_sums = jnp.concatenate([sums_low, sums_high], 1)
        if fast:
            moving1, dqkv_high, wo_x, wo_y, *sent[2] = lax.optimization_barrier(
                (moving1, dqkv_high, wo_x, wo_y, *sent[2])
            )
            total2 = settle(2, moving1).astype(bf16)
            moving2 = ring(total2)
            wo_total = wo_parts[0].astype(f32) + wo_x.astype(f32) + wo_y.astype(f32)
            wo_total = after(wo_total.astype(bf16), total2)
        else:
            wo_total = wo_own[:576]
        moved = shape((rows + 48, width), bf16)
        d0, d1, d2, d3, dqkv = call(
            token_grad_kernel,
            "token_grad",
            (dqkv_low, dqkv_high, w_in, wo_total),
            [VMEM] * 4,
            [moved] * 4 + [shape((LENGTH, 3 * BLOCK), bf16)],
        )
        in_part = shape((1600, BLOCK), bf16)
        in_own, in_send = call(
            input_grad_kernel,
            "input_grad",
            (ids, *t, dqkv, head_sums),
            [SMEM] + [VMEM] * 6,
            [in_part, in_part],
            scratch=[pltpu.VMEM((BLOCK, 3 * BLOCK), f32)],
        )

        def add(left, right):
            return (left.astype(f32) + right.astype(f32)).astype(bf16)

        moving = ring(d1)
        if fast:
            in_got = swap(in_send)
            moving, moving2, in_got, *sent[3] = lax.optimization_barrier(
                (moving, moving2, in_got, *sent[3])
            )
            moving = ring(add(moving, d2))
            total3 = settle(3, moving2).astype(bf16)
            moving3 = ring(total3)
            in_total = add(in_own, in_got)
            in_parts = [in_total[j * 400 : (j + 1) * 400] for j in range(4)]
            in_far = flip(in_parts[3], 2)
            moving, moving3, in_far, *sent[0] = lax.optimization_barrier(
                (moving, moving3, in_far, *sent[0])
            )
            moving = ring(add(moving, d3))
            in_x = flip(in_parts[1], 2)
            in_y = flip(in_parts[2] + in_far, 4)
            mine = settle(0, moving3)
        else:
            moving = ring(add(moving, d2))
            moving = ring(add(moving, d3))
        moving = moving.astype(f32) + d0.astype(f32)
        tokens_grad = first_grad + moving[:rows]

        if fast:
            left = mine[:512].reshape(2, 2, HALF, BLOCK)
            right = mine[512:]

            def sides(side):
                a = lax.dynamic_index_in_dim(left, side, 1, False)
                b = lax.dynamic_slice_in_dim(right, side * HALF, HALF, 1)
                return a, b

            a, b = sides(1 - core)
            got = swap(
                jnp.concatenate(
                    [a[0, :, :HALF], a[0, :, HALF:], a[1, :, :HALF], a[1, :, HALF:], b], 0
                ).astype(bf16)
            ).astype(f32)
            a, b = sides(core)
            ga = jnp.concatenate([got[i * HALF : (i + 1) * HALF] for i in range(4)], 1)
            inner_grad = in_order(core, jnp.concatenate([a[0], a[1]], 1), ga, 1)
            outer_grad = in_order(core, b, got[512:], 0)

            total = jnp.concatenate(
                [moving[rows:, i * BLOCK : (i + 1) * BLOCK] for i in range(3)], 0
            )
            got = swap(lax.dynamic_slice_in_dim(total, (1 - core) * HALF, HALF, 1))
            total = lax.dynamic_slice_in_dim(total, core * HALF, HALF, 1)
            output_grad = in_order(core, total[:HALF], got[:HALF], 0)
            sums = total[HALF:] + got[HALF:]
            six = lax.dynamic_slice(sums, (0, z * 32), (6, 32))
            offset_inner = sums[6]

            total = in_parts[0].astype(f32) + in_x.astype(f32) + in_y.astype(f32)
            query_grad, key_grad, value_grad = [
                total[i * HALF : (i + 1) * HALF] for i in range(3)
            ]
            head_sums = total[384:386]
        else:
            def scatter(value, dim):
                return lax.psum_scatter(value, "dp", scatter_dimension=dim, tiled=True)

            def quarter(parts):
                found = jnp.stack(parts).astype(f32)
                found = jnp.take(found, (z - jnp.arange(tensor)) % tensor, axis=0)
                return lax.psum_scatter(found, "tensor", scatter_dimension=0, tiled=False)

            def half(value, dim):
                field = jnp.zeros_like(value)
                return jnp.where(
                    core == 0,
                    jnp.concatenate([value, field], dim),
                    jnp.concatenate([field, value], dim),
                )

            a = quarter(
                [
                    jnp.concatenate(
                        [jnp.concatenate([p[:BLOCK], p[BLOCK:512]], 1) for p in grads[turn]], 0
                    )
                    for turn in range(4)
                ]
            )
            b = quarter(
                [jnp.concatenate([p[512:1024] for p in grads[turn]], 1) for turn in range(4)]
            )
            inner_grad = scatter(half(a, 1), 0)
            outer_grad = scatter(half(b, 0), 1)

            def heads(value):
                value = value.reshape(4, 4, 144, BLOCK)[:, :, :HALF]
                return value.transpose(1, 2, 0, 3).reshape(4, HALF, width)

            mine, theirs = quarter(list(heads(wo_own))), quarter(list(heads(wo_send)))
            output_grad = scatter(in_order(core, mine, theirs, 0), 1)
            own, send = [
                p.astype(f32).reshape(4, 400, BLOCK)[:, :384].reshape(4, 3, HALF, BLOCK)
                for p in (in_own, in_send)
            ]
            both = jnp.where(core == 0, jnp.stack([own, send], 1), jnp.stack([send, own], 1))
            both = both.transpose(2, 0, 1, 3, 4).reshape(3, width, BLOCK)
            query_grad, key_grad, value_grad = [scatter(both[i], 0) for i in range(3)]

            sums = jnp.concatenate([first_sums, second_sums, inner_sums.reshape(4, width)], 0)
            sums = sum_all(sums)
            head_sums = sum_all(head_sums, False)
            piece = width // (dp * tensor)
            six = lax.dynamic_slice_in_dim(sums[:6], (place * tensor + z) * piece, piece, 1)
            piece = inner_offset.shape[0]
            offset_inner = lax.dynamic_slice_in_dim(
                sums[6:].reshape(-1), (z * dp + place) * piece, piece, 0
            )

        head_sums = lax.dynamic_slice_in_dim(head_sums, place * (BLOCK // dp), BLOCK // dp, 1)
        return (
            result,
            tokens_grad,
            query_grad,
            key_grad,
            value_grad,
            output_grad,
            inner_grad,
            outer_grad,
            head_sums[0],
            head_sums[1],
            offset_inner,
            six[0],
            six[3],
            six[1],
            six[2],
            six[4],
            six[5],
        )

    return body


def solution(mesh):
    return jax.shard_map(
        body_for(mesh.shape["dp"], mesh.shape["tensor"]),
        mesh=mesh,
        in_specs=(
            P(("dp", "tensor"), None),
            P(("dp", "tensor"), None),
            P("dp", None),
            P("dp", "tensor"),
            P("dp", "tensor"),
            P("dp", "tensor"),
            P("tensor", "dp"),
            P("dp", "tensor"),
            P("tensor", "dp"),
            P(("tensor", "dp")),
            P(("tensor", "dp")),
            P(("tensor", "dp")),
            P(("dp", "tensor")),
            P(("dp", "tensor")),
            P(("dp", "tensor")),
            P(("dp", "tensor")),
            P(("dp", "tensor")),
            P(("dp", "tensor")),
        ),
        out_specs=(
            P(("dp", "tensor"), None),
            P(("dp", "tensor"), None),
            P("dp", "tensor"),
            P("dp", "tensor"),
            P("dp", "tensor"),
            P("tensor", "dp"),
            P("dp", "tensor"),
            P("tensor", "dp"),
            P(("tensor", "dp")),
            P(("tensor", "dp")),
            P(("tensor", "dp")),
            P(("dp", "tensor")),
            P(("dp", "tensor")),
            P(("dp", "tensor")),
            P(("dp", "tensor")),
            P(("dp", "tensor")),
            P(("dp", "tensor")),
        ),
        check_vma=False,
    )
```

time: 413 us -> 313 us (0.76)
  local copies, waits for them, and re-layouts: 41.5 us -> 7.33 us
  Pallas kernels: 95 us -> 69 us
  waiting for transfers between devices: 182 us -> 157 us
  starting transfers between devices: 75.4 us -> 62.3 us
    unnamed x171 -> x91, local copies, waits for them, and re-layouts: 32.3 us -> 3.63 us
    ppermute x54 -> x48, waiting for transfers between devices: 107 us -> 79 us  [flip(): return lax.ppermute(value, axis, [(i, i ^ bit) for i in range(size)])]
    pallas_call x13 -> x20, Pallas kernels: 95 us -> 69 us  [call(): pl.pallas_call(kernel, grid=grid, name=name, out_shape=outs, in_specs=spe...]
    ppermute x54 -> x48, starting transfers between devices: 51.2 us -> 40.1 us  [flip(): return lax.ppermute(value, axis, [(i, i ^ bit) for i in range(size)])]
    ppermute x6, waiting for transfers between devices: 14.6 us -> 7.32 us  [shift(): lax.ppermute(value, 'tensor', [(i, (i - by) % tensor) for i in range(tens...]
    ppermute x15 -> x12, waiting for transfers between devices: 60.1 us -> 66.9 us  [ring(): return lax.ppermute(value, 'tensor', ring_pairs)]
    ppermute x15 -> x12, starting transfers between devices: 13.6 us -> 7.7 us  [ring(): return lax.ppermute(value, 'tensor', ring_pairs)]
    ppermute x0 -> x2, starting transfers between devices: none -> 5.59 us  [the longest x1 5.03 us: assemble(): ahead = lax.ppermute(prepared, 'tensor', back)]
  transfers between devices with their start and end apart: 75 -> 68, of which waited for: 33 -> 33; matrix products, arithmetic and copies ran while one was open for 8% -> 4% of each run, Pallas kernels for 16% -> 17%
where the time goes in v2:
time: 313 us; the launch traced here: 311 us
  waiting for transfers between devices  157 us (50%)
  Pallas kernels  69 us (22%)
  starting transfers between devices  62.3 us (20%)
  other arithmetic  13.3 us (4%)
  local copies, waits for them, and re-layouts  7.33 us (2%)
    ppermute x48, waiting for transfers between devices, flip(): return lax.ppermute(value, axis, [(i, i ^ bit) for i in range(size)])  79 us
    pallas_call x20, Pallas kernels, call(): pl.pallas_call(kernel, grid=grid, name=name, out_shape=outs, in_specs=spe...  69 us
    ppermute x12, waiting for transfers between devices, ring(): return lax.ppermute(value, 'tensor', ring_pairs)  66.9 us
    ppermute x48, starting transfers between devices, flip(): return lax.ppermute(value, axis, [(i, i ^ bit) for i in range(size)])  40.1 us
    ppermute x6, starting transfers between devices, shift(): lax.ppermute(value, 'tensor', [(i, (i - by) % tensor) for i in range(tens...  8.85 us
    ppermute x12, starting transfers between devices, ring(): return lax.ppermute(value, 'tensor', ring_pairs)  7.7 us
    ppermute x6, waiting for transfers between devices, shift(): lax.ppermute(value, 'tensor', [(i, (i - by) % tensor) for i in range(tens...  7.32 us
  transfers between devices with their start and end apart: 68, of which 33 were waited for; matrix products, arithmetic and copies ran while one was open for 4% of the time, Pallas kernels for 17%

profile of v2, /device:TPU:0, one launch (start us, length us, event | category | flops | bytes accessed | tf_op | source)
XLA Modules:
  0.0 310.6 jit_solution(10532342395271717254)
XLA Ops:
  5.0 5.0 %collective-permute-start.3 = (bf16[288,128]{1,0:T(8,128)(2,1)S(1)}, bf16[288,128]{1,0:T(8,128)(2,1)S(1)}, u32[]{:S(2)}, u32[]{:S(2)}) collective-permute-start(bf16[288,128]{1,0:T(8,128)(2,1)S(1)} %prepare.1.p), channel_id=1, source_target_pairs={{0,3},{1,0},{2,1},{3,2},{4,7},{5,4},{6,5},{7,6},{8,11},{9,8},{10,9... | collective-permute-start | bytes 221192 | tf_op jit(solution)/shard_map/ppermute | solution.py:588
  10.6 2.1 collective-permute-done.3.pb
  15.8 1.6 collective-permute-start.6
  19.2 10.6 %collective-permute-done.8.t1 = bf16[256,1024]{1,0:T(8,128)(2,1)S(1)} collective-permute-done((bf16[256,1024]{1,0:T(8,128)(2,1)S(1)}, bf16[256,1024]{1,0:T(8,128)(2,1)S(1)}, u32[]{:S(2)}, u32[]{:S(2)}) %collective-permute-start.8) | collective-permute-done | bytes 524320 | tf_op jit(solution)/shard_map/ppermute | solution.py:555
  29.8 13.0 %collective-permute-done.5.refs_5_ = bf16[1184,256]{1,0:T(8,128)(2,1)S(1)} collective-permute-done((bf16[1184,256]{1,0:T(8,128)(2,1)S(1)}, bf16[1184,256]{1,0:T(8,128)(2,1)S(1)}, u32[]{:S(2)}, u32[]{:S(2)}) %collective-permute-start.5) | collective-permute-done | bytes 606240 | tf_op jit(solution)/shard_map/ppermute | solution.py:555
  42.8 8.6 %collective-permute-done.9.t2 = bf16[256,1024]{1,0:T(8,128)(2,1)S(1)} collective-permute-done((bf16[256,1024]{1,0:T(8,128)(2,1)S(1)}, bf16[256,1024]{1,0:T(8,128)(2,1)S(1)}, u32[]{:S(2)}, u32[]{:S(2)}) %collective-permute-start.9) | collective-permute-done | bytes 524320 | tf_op jit(solution)/shard_map/ppermute | solution.py:555
  51.5 1.6 collective-permute-start.14
  56.5 7.8 %collective-permute-done.14.v3.refs_4_ = bf16[832,256]{1,0:T(8,128)(2,1)S(1)} collective-permute-done((bf16[832,256]{1,0:T(8,128)(2,1)S(1)}, bf16[832,256]{1,0:T(8,128)(2,1)S(1)}, u32[]{:S(2)}, u32[]{:S(2)}) %collective-permute-start.14) | collective-permute-done | bytes 426016 | tf_op jit(solution)/shard_map/ppermute | solution.py:552
  65.8 11.5 %collective-permute-done.13.p3.refs_3_ = bf16[896,256]{1,0:T(8,128)(2,1)S(1)} collective-permute-done((bf16[896,256]{1,0:T(8,128)(2,1)S(1)}, bf16[896,256]{1,0:T(8,128)(2,1)S(1)}, u32[]{:S(2)}, u32[]{:S(2)}) %collective-permute-start.13) | collective-permute-done | bytes 458784 | tf_op jit(solution)/shard_map/ppermute | solution.py:552
  77.3 1.6 collective-permute-done.15.t3
  83.6 13.2 %attend.1 = (bf16[1024,256]{1,0:T(8,128)(2,1)S(1)}, bf16[1024,256]{1,0:T(8,128)(2,1)S(1)}, bf16[1024,256]{1,0:T(8,128)(2,1)S(1)}, bf16[1024,768]{1,0:T(8,128)(2,...) custom-call(s32[4]{0:T(128)S(1)} %pad_add_fusion.ids, ...), custom_call_target="tpu_custom_call" | custom-call | flops 60000002048 | tf_op jit(solution)/shard_map/attend/pallas_call | solution.py:48
  96.9 4.8 %collective-permute-done.19.refs_8_ = bf16[512,256]{1,0:T(8,128)(2,1)S(1)} collective-permute-done((bf16[512,256]{1,0:T(8,128)(2,1)S(1)}, bf16[512,256]{1,0:T(8,128)(2,1)S(1)}, u32[]{:S(2)}, u32[]{:S(2)}) %collective-permute-start.19) | collective-permute-done | bytes 262176 | tf_op jit(solution)/shard_map/ppermute | solution.py:552
  102.7 2.5 collective-permute-start.27
  105.3 1.6 collective-permute-start.22
  110.9 2.6 collective-permute-done.27.x2
  115.7 3.3 %collective-permute-done.28.x3 = bf16[256,256]{1,0:T(8,128)(2,1)S(1)} collective-permute-done((bf16[256,256]{1,0:T(8,128)(2,1)S(1)}, bf16[256,256]{1,0:T(8,128)(2,1)S(1)}, u32[]{:S(2)}, u32[]{:S(2)}) %collective-permute-start.28) | collective-permute-done | bytes 131104 | tf_op jit(solution)/shard_map/ppermute | solution.py:733
  118.9 7.3 %collective-permute-done.24.refs_13_ = bf16[512,256]{1,0:T(8,128)(2,1)S(1)} collective-permute-done((bf16[512,256]{1,0:T(8,128)(2,1)S(1)}, bf16[512,256]{1,0:T(8,128)(2,1)S(1)}, u32[]{:S(2)}, u32[]{:S(2)}) %collective-permute-start.24) | collective-permute-done | bytes 262176 | tf_op jit(solution)/shard_map/ppermute | solution.py:552
  128.8 2.7 project.1
  131.7 1.6 collective-permute-start.33
  133.3 1.6 collective-permute-start.32
  134.9 6.3 %forward.2 = (bf16[1536,512]{1,0:T(8,128)(2,1)S(1)}, bf16[1536,512]{1,0:T(8,128)(2,1)S(1)}, f32[256,1024]{1,0:T(8,128)S(1)}, f32[256,1024]{1,0:T(8,128)S(1)}) custom-call(s32[4]{0:T(128)S(1)} %pad_add_fusion.ids, bf16[256,1024]{1,0:T(8,128)(2,1)S(1)} %get-tuple-element.174.mine, bf16[256,1024]{1,0:T(8,128)(2,1)S(1)} %collective-permute-done.31.theirs, ...), custom_call_target="tpu_custom_call" | custom-call | flops 32000000000 | tf_op jit(solution)/shard_map/forward/pallas_call | solution.py:48
  142.1 2.7 forward.3
  145.0 2.6 collective-permute-done.34.got
  147.6 1.7 second.1
  149.4 1.8 collective-permute-done.35.theirs.gtheirs
  151.2 5.4 %backward.1 = (bf16[2048,512]{1,0:T(8,128)(2,1)S(1)}, f32[256,1024]{1,0:T(8,128)S(1)}, bf16[256,1024]{1,0:T(8,128)(2,1)S(1)}, f32[8,512]{1,0:T(8,128)S(1)}) custom-call(s32[4]{0:T(128)S(1)} %pad_add_fusion.ids, bf16[256,1024]{1,0:T(8,128)(2,1)S(1)} %get-tuple-element.184.mine.gmine, bf16[256,1024]{1,0:T(8,128)(2,1)S(1)} %collective-permute-done.35.theirs.gtheirs, ...), custom_call_target="tpu_custom_call" | custom-call | flops 41999998976 | tf_op jit(solution)/shard_map/backward/pallas_call | solution.py:48
  156.8 3.1 weights.2
  159.9 1.6 collective-permute-start.38
  166.6 9.7 %collective-permute-done.37 = bf16[1024,256]{1,0:T(8,128)(2,1)S(1)} collective-permute-done((bf16[1024,256]{1,0:T(8,128)(2,1)S(1)}, bf16[1024,256]{1,0:T(8,128)(2,1)S(1)}, u32[]{:S(2)}, u32[]{:S(2)}) %collective-permute-start.37) | collective-permute-done | bytes 524320 | tf_op jit(solution)/shard_map/ppermute | solution.py:552
  177.2 2.1 collective-permute-start.39
  179.6 3.1 weights.3
  182.7 2.4 collective-permute-start.41
  185.5 1.6 collective-permute-start.48
  191.2 9.1 %attend_back.2 = (bf16[1024,384]{1,0:T(8,128)(2,1)S(1)}, f32[2,128]{1,0:T(2,128)S(1)}) custom-call(s32[4]{0:T(128)S(1)} %pad_add_fusion.ids, s32[1,8]{1,0:T(1,128)S(1)} %copy-done.23, bf16[1024,256]{1,0:T(8,128)(2,1)S(1)} %get-tuple-element.199.q, bf16[1024,256]{1,0:T(8,128)(2,1)S(1)} %copy-done.32, bf16[1024,256]{1,0:T(8,128)(2,1)S(1)} %copy-done.34, ...), custom_call_target="tpu_custom_call" | custom-call | flops 42800001024 | tf_op jit(solution)/shard_map/attend_back/pallas_call | solution.py:48
  202.2 6.7 %collective-permute-done.45 = bf16[576,256]{1,0:T(8,128)(2,1)S(1)} collective-permute-done((bf16[576,256]{1,0:T(8,128)(2,1)S(1)}, bf16[576,256]{1,0:T(8,128)(2,1)S(1)}, u32[]{:S(2)}, u32[]{:S(2)}) %collective-permute-start.45) | collective-permute-done | bytes 294944 | tf_op jit(solution)/shard_map/ppermute | solution.py:552
  209.1 2.4 collective-permute-start.46
  213.8 9.1 %attend_back.3 = (bf16[1024,384]{1,0:T(8,128)(2,1)S(1)}, f32[2,128]{1,0:T(2,128)S(1)}) custom-call(s32[4]{0:T(128)S(1)} %pad_add_fusion.ids, s32[1,8]{1,0:T(1,128)S(1)} %copy-done.23, bf16[1024,256]{1,0:T(8,128)(2,1)S(1)} %get-tuple-element.199.q, bf16[1024,256]{1,0:T(8,128)(2,1)S(1)} %copy-done.32, bf16[1024,256]{1,0:T(8,128)(2,1)S(1)} %copy-done.34, ...), custom_call_target="tpu_custom_call" | custom-call | flops 42800001024 | tf_op jit(solution)/shard_map/attend_back/pallas_call | solution.py:48
  224.3 1.9 token_grad.1
  226.3 3.0 input_grad.1
  229.3 2.2 collective-permute-start.53
  232.6 12.9 %collective-permute-done.57 = bf16[1024,256]{1,0:T(8,128)(2,1)S(1)} collective-permute-done((bf16[1024,256]{1,0:T(8,128)(2,1)S(1)}, bf16[1024,256]{1,0:T(8,128)(2,1)S(1)}, u32[]{:S(2)}, u32[]{:S(2)}) %collective-permute-start.57) | collective-permute-done | bytes 524320 | tf_op jit(solution)/shard_map/ppermute | solution.py:552
  247.2 11.6 %collective-permute-done.54 = bf16[1024,256]{1,0:T(8,128)(2,1)S(1)} collective-permute-done((bf16[1024,256]{1,0:T(8,128)(2,1)S(1)}, bf16[1024,256]{1,0:T(8,128)(2,1)S(1)}, u32[]{:S(2)}, u32[]{:S(2)}) %collective-permute-start.54) | collective-permute-done | bytes 524320 | tf_op jit(solution)/shard_map/ppermute | solution.py:555
  263.7 5.6 %collective-permute-done.60 = bf16[400,256]{1,0:T(8,128)(2,1)} collective-permute-done((bf16[400,256]{1,0:T(8,128)(2,1)S(1)}, bf16[400,256]{1,0:T(8,128)(2,1)}, u32[]{:S(2)}, u32[]{:S(2)}) %collective-permute-start.60) | collective-permute-done | bytes 204832 | tf_op jit(solution)/shard_map/ppermute | solution.py:552
  269.3 7.6 %collective-permute-done.59 = bf16[1024,256]{1,0:T(8,128)(2,1)} collective-permute-done((bf16[1024,256]{1,0:T(8,128)(2,1)}, bf16[1024,256]{1,0:T(8,128)(2,1)}, u32[]{:S(2)}, u32[]{:S(2)}) %collective-permute-start.59) | collective-permute-done | bytes 524320 | tf_op jit(solution)/shard_map/ppermute | solution.py:555
  276.8 12.0 %collective-permute-done.58 = bf16[304,1024]{1,0:T(8,128)(2,1)} collective-permute-done((bf16[304,1024]{1,0:T(8,128)(2,1)}, bf16[304,1024]{1,0:T(8,128)(2,1)}, u32[]{:S(2)}, u32[]{:S(2)}) %collective-permute-start.58) | collective-permute-done | bytes 622624 | tf_op jit(solution)/shard_map/ppermute | solution.py:555
  290.2 1.6 convert_add_fusion.1
  296.3 3.4 %collective-permute-done.64 = bf16[400,256]{1,0:T(8,128)(2,1)S(1)} collective-permute-done((bf16[400,256]{1,0:T(8,128)(2,1)S(1)}, bf16[400,256]{1,0:T(8,128)(2,1)S(1)}, u32[]{:S(2)}, u32[]{:S(2)}) %collective-permute-start.64) | collective-permute-done | bytes 204832 | tf_op jit(solution)/shard_map/ppermute | solution.py:552
  304.6 2.0 collective-permute-done.63
  (255 shorter events, 68.9 us)
Async XLA Ops:
  0.7 13.6 %collective-permute-start = (bf16[128,1024]{1,0:T(8,128)(2,1)}, bf16[128,1024]{1,0:T(8,128)(2,1)S(1)}, u32[]{:S(2)}, u32[]{:S(2)}) collective-permute-start(bf16[128,1024]{1,0:T(8,128)(2,1)} %w1.1), channel_id=1, source_target_pairs={{0,4},{4,0},{8,12},{12,8},{16,20},{20,16},{24,28},{28,24},{1,5},{5... | collective-permute-start | bytes 786440 | tf_op jit(solution)/shard_map/ppermute | solution.py:552
  1.2 13.1 %collective-permute-start.1 = (bf16[1024,128]{1,0:T(8,128)(2,1)}, bf16[1024,128]{1,0:T(8,128)(2,1)S(1)}, u32[]{:S(2)}, u32[]{:S(2)}) collective-permute-start(bf16[1024,128]{1,0:T(8,128)(2,1)} %w2.1), channel_id=1, source_target_pairs={{0,4},{4,0},{8,12},{12,8},{16,20},{20,16},{24,28},{28,24},{1,5},{5... | collective-permute-start | bytes 786440 | tf_op jit(solution)/shard_map/ppermute | solution.py:552
  12.7 17.1 %collective-permute-start.8 = (bf16[256,1024]{1,0:T(8,128)(2,1)S(1)}, bf16[256,1024]{1,0:T(8,128)(2,1)S(1)}, u32[]{:S(2)}, u32[]{:S(2)}) collective-permute-start(bf16[256,1024]{1,0:T(8,128)(2,1)S(1)} %copy-done.1), channel_id=1, source_target_pairs={{0,1},{1,2},{2,3},{3,0},{4,5},{5,6},{6,7},{7,4},{8,9},{9,10},{10,1... | collective-permute-start | bytes 1572872 | tf_op jit(solution)/shard_map/ppermute | solution.py:555
  15.8 35.6 %collective-permute-start.6 = (bf16[1728,256]{1,0:T(8,128)(2,1)S(1)}, bf16[1728,256]{1,0:T(8,128)(2,1)S(1)}, u32[]{:S(2)}, u32[]{:S(2)}) collective-permute-start(bf16[1728,256]{1,0:T(8,128)(2,1)S(1)} %get-tuple-element.142.p0.refs_0_), channel_id=1, source_target_pairs={{0,8},{4,12},{8,0},{12,4},{16,24},{20,28},{24,16},{28,20},{1,9},{5... | collective-permute-start | bytes 2654216 | tf_op jit(solution)/shard_map/ppermute | solution.py:552
  17.3 34.1 %collective-permute-start.7 = (bf16[1728,256]{1,0:T(8,128)(2,1)S(1)}, bf16[1728,256]{1,0:T(8,128)(2,1)S(1)}, u32[]{:S(2)}, u32[]{:S(2)}) collective-permute-start(bf16[1728,256]{1,0:T(8,128)(2,1)S(1)} %get-tuple-element.142.p0.refs_0_), channel_id=1, source_target_pairs={{0,16},{4,20},{8,24},{12,28},{16,0},{20,4},{24,8},{28,12},{1,17},{... | collective-permute-start | bytes 2654216 | tf_op jit(solution)/shard_map/ppermute | solution.py:552
  18.8 23.9 %collective-permute-start.5 = (bf16[1184,256]{1,0:T(8,128)(2,1)S(1)}, bf16[1184,256]{1,0:T(8,128)(2,1)S(1)}, u32[]{:S(2)}, u32[]{:S(2)}) collective-permute-start(bf16[1184,256]{1,0:T(8,128)(2,1)S(1)} %get-tuple-element.141), channel_id=1, source_target_pairs={{0,1},{1,2},{2,3},{3,0},{4,5},{5,6},{6,7},{7,4},{8,9},{9,10},{10,1... | collective-permute-start | bytes 1818632 | tf_op jit(solution)/shard_map/ppermute | solution.py:555
  29.8 21.6 %collective-permute-start.9 = (bf16[256,1024]{1,0:T(8,128)(2,1)S(1)}, bf16[256,1024]{1,0:T(8,128)(2,1)S(1)}, u32[]{:S(2)}, u32[]{:S(2)}) collective-permute-start(bf16[256,1024]{1,0:T(8,128)(2,1)S(1)} %collective-permute-done.8.t1), channel_id=1, source_target_pairs={{0,1},{1,2},{2,3},{3,0},{4,5},{5,6},{6,7},{7,4},{8,9},{9,10},{10,1... | collective-permute-start | bytes 1572872 | tf_op jit(solution)/shard_map/ppermute | solution.py:555
  51.5 12.8 %collective-permute-start.14 = (bf16[832,256]{1,0:T(8,128)(2,1)S(1)}, bf16[832,256]{1,0:T(8,128)(2,1)S(1)}, u32[]{:S(2)}, u32[]{:S(2)}) collective-permute-start(bf16[832,256]{1,0:T(8,128)(2,1)S(1)} %slice.157), channel_id=1, source_target_pairs={{0,8},{4,12},{8,0},{12,4},{16,24},{20,28},{24,16},{28,20},{1,9},{5... | collective-permute-start | bytes 1277960 | tf_op jit(solution)/shard_map/ppermute | solution.py:552
  53.0 25.8 %collective-permute-start.10 = (bf16[1184,256]{1,0:T(8,128)(2,1)S(1)}, bf16[1184,256]{1,0:T(8,128)(2,1)S(1)}, u32[]{:S(2)}, u32[]{:S(2)}) collective-permute-start(bf16[1184,256]{1,0:T(8,128)(2,1)S(1)} %collective-permute-done.5.refs_5_), channel_id=1, source_target_pairs={{0,1},{1,2},{2,3},{3,0},{4,5},{5,6},{6,7},{7,4},{8,9},{9,10},{10,1... | collective-permute-start | bytes 1818632 | tf_op jit(solution)/shard_map/ppermute | solution.py:555
  53.0 25.8 %collective-permute-start.11 = (bf16[1184,256]{1,0:T(8,128)(2,1)S(1)}, bf16[1184,256]{1,0:T(8,128)(2,1)S(1)}, u32[]{:S(2)}, u32[]{:S(2)}) collective-permute-start(bf16[1184,256]{1,0:T(8,128)(2,1)S(1)} %collective-permute-done.5.refs_5_), channel_id=1, source_target_pairs={{0,8},{4,12},{8,0},{12,4},{16,24},{20,28},{24,16},{28,20},{1,9},{5... | collective-permute-start | bytes 1818632 | tf_op jit(solution)/shard_map/ppermute | solution.py:552
  53.5 25.3 %collective-permute-start.12 = (bf16[1184,256]{1,0:T(8,128)(2,1)S(1)}, bf16[1184,256]{1,0:T(8,128)(2,1)S(1)}, u32[]{:S(2)}, u32[]{:S(2)}) collective-permute-start(bf16[1184,256]{1,0:T(8,128)(2,1)S(1)} %collective-permute-done.5.refs_5_), channel_id=1, source_target_pairs={{0,16},{4,20},{8,24},{12,28},{16,0},{20,4},{24,8},{28,12},{1,17},{... | collective-permute-start | bytes 1818632 | tf_op jit(solution)/shard_map/ppermute | solution.py:552
  55.1 23.8 %collective-permute-start.15 = (bf16[256,1024]{1,0:T(8,128)(2,1)S(1)}, bf16[256,1024]{1,0:T(8,128)(2,1)S(1)}, u32[]{:S(2)}, u32[]{:S(2)}) collective-permute-start(bf16[256,1024]{1,0:T(8,128)(2,1)S(1)} %collective-permute-done.9.t2), channel_id=1, source_target_pairs={{0,1},{1,2},{2,3},{3,0},{4,5},{5,6},{6,7},{7,4},{8,9},{9,10},{10,1... | collective-permute-start | bytes 1572872 | tf_op jit(solution)/shard_map/ppermute | solution.py:555
  64.3 13.0 %collective-permute-start.13 = (bf16[896,256]{1,0:T(8,128)(2,1)S(1)}, bf16[896,256]{1,0:T(8,128)(2,1)S(1)}, u32[]{:S(2)}, u32[]{:S(2)}) collective-permute-start(bf16[896,256]{1,0:T(8,128)(2,1)S(1)} %slice.156), channel_id=1, source_target_pairs={{0,16},{4,20},{8,24},{12,28},{16,0},{20,4},{24,8},{28,12},{1,17},{... | collective-permute-start | bytes 1376264 | tf_op jit(solution)/shard_map/ppermute | solution.py:552
  79.0 26.3 %collective-permute-start.16 = (bf16[1184,256]{1,0:T(8,128)(2,1)S(1)}, bf16[1184,256]{1,0:T(8,128)(2,1)S(1)}, u32[]{:S(2)}, u32[]{:S(2)}) collective-permute-start(bf16[1184,256]{1,0:T(8,128)(2,1)S(1)} %collective-permute-done.10.refs_10_), channel_id=1, source_target_pairs={{0,1},{1,2},{2,3},{3,0},{4,5},{5,6},{6,7},{7,4},{8,9},{9,10},{10,1... | collective-permute-start | bytes 1818632 | tf_op jit(solution)/shard_map/ppermute | solution.py:555
  79.3 26.0 %collective-permute-start.17 = (bf16[1184,256]{1,0:T(8,128)(2,1)S(1)}, bf16[1184,256]{1,0:T(8,128)(2,1)S(1)}, u32[]{:S(2)}, u32[]{:S(2)}) collective-permute-start(bf16[1184,256]{1,0:T(8,128)(2,1)S(1)} %collective-permute-done.10.refs_10_), channel_id=1, source_target_pairs={{0,8},{4,12},{8,0},{12,4},{16,24},{20,28},{24,16},{28,20},{1,9},{5... | collective-permute-start | bytes 1818632 | tf_op jit(solution)/shard_map/ppermute | solution.py:552
  80.6 24.7 %collective-permute-start.18 = (bf16[1184,256]{1,0:T(8,128)(2,1)S(1)}, bf16[1184,256]{1,0:T(8,128)(2,1)S(1)}, u32[]{:S(2)}, u32[]{:S(2)}) collective-permute-start(bf16[1184,256]{1,0:T(8,128)(2,1)S(1)} %collective-permute-done.10.refs_10_), channel_id=1, source_target_pairs={{0,16},{4,20},{8,24},{12,28},{16,0},{20,4},{24,8},{28,12},{1,17},{... | collective-permute-start | bytes 1818632 | tf_op jit(solution)/shard_map/ppermute | solution.py:552
  82.1 20.6 %collective-permute-start.20 = (bf16[672,256]{1,0:T(8,128)(2,1)S(1)}, bf16[672,256]{1,0:T(8,128)(2,1)S(1)}, u32[]{:S(2)}, u32[]{:S(2)}) collective-permute-start(bf16[672,256]{1,0:T(8,128)(2,1)S(1)} %slice.159), channel_id=1, source_target_pairs={{0,8},{4,12},{8,0},{12,4},{16,24},{20,28},{24,16},{28,20},{1,9},{5... | collective-permute-start | bytes 1032200 | tf_op jit(solution)/shard_map/ppermute | solution.py:552
  83.0 18.6 %collective-permute-start.19 = (bf16[512,256]{1,0:T(8,128)(2,1)S(1)}, bf16[512,256]{1,0:T(8,128)(2,1)S(1)}, u32[]{:S(2)}, u32[]{:S(2)}) collective-permute-start(bf16[512,256]{1,0:T(8,128)(2,1)S(1)} %slice.158), channel_id=1, source_target_pairs={{0,16},{4,20},{8,24},{12,28},{16,0},{20,4},{24,8},{28,12},{1,17},{... | collective-permute-start | bytes 786440 | tf_op jit(solution)/shard_map/ppermute | solution.py:552
  102.7 10.8 %collective-permute-start.27 = (bf16[256,256]{1,0:T(8,128)(2,1)S(1)}, bf16[256,256]{1,0:T(8,128)(2,1)S(1)}, u32[]{:S(2)}, u32[]{:S(2)}) collective-permute-start(bf16[256,256]{1,0:T(8,128)(2,1)S(1)} %get-tuple-element.162), channel_id=1, source_target_pairs={{0,2},{1,3},{2,0},{3,1},{4,6},{5,7},{6,4},{7,5},{8,10},{9,11},{10,... | collective-permute-start | bytes 393224 | tf_op jit(solution)/shard_map/ppermute | solution.py:733
  105.3 21.5 %collective-permute-start.22 = (bf16[1184,256]{1,0:T(8,128)(2,1)S(1)}, bf16[1184,256]{1,0:T(8,128)(2,1)S(1)}, u32[]{:S(2)}, u32[]{:S(2)}) collective-permute-start(bf16[1184,256]{1,0:T(8,128)(2,1)S(1)} %collective-permute-done.16.refs_0_.refs_15_), channel_id=1, source_target_pairs={{0,8},{4,12},{8,0},{12,4},{16,24},{20,28},{24,16},{28,20},{1,9},{5... | collective-permute-start | bytes 1818632 | tf_op jit(solution)/shard_map/ppermute | solution.py:552
  106.9 19.9 %collective-permute-start.23 = (bf16[1184,256]{1,0:T(8,128)(2,1)S(1)}, bf16[1184,256]{1,0:T(8,128)(2,1)S(1)}, u32[]{:S(2)}, u32[]{:S(2)}) collective-permute-start(bf16[1184,256]{1,0:T(8,128)(2,1)S(1)} %collective-permute-done.16.refs_0_.refs_15_), channel_id=1, source_target_pairs={{0,16},{4,20},{8,24},{12,28},{16,0},{20,4},{24,8},{28,12},{1,17},{... | collective-permute-start | bytes 1818632 | tf_op jit(solution)/shard_map/ppermute | solution.py:552
  108.4 18.4 %collective-permute-start.25 = (bf16[672,256]{1,0:T(8,128)(2,1)S(1)}, bf16[672,256]{1,0:T(8,128)(2,1)S(1)}, u32[]{:S(2)}, u32[]{:S(2)}) collective-permute-start(bf16[672,256]{1,0:T(8,128)(2,1)S(1)} %slice.161), channel_id=1, source_target_pairs={{0,8},{4,12},{8,0},{12,4},{16,24},{20,28},{24,16},{28,20},{1,9},{5... | collective-permute-start | bytes 1032200 | tf_op jit(solution)/shard_map/ppermute | solution.py:552
  109.4 16.8 %collective-permute-start.24 = (bf16[512,256]{1,0:T(8,128)(2,1)S(1)}, bf16[512,256]{1,0:T(8,128)(2,1)S(1)}, u32[]{:S(2)}, u32[]{:S(2)}) collective-permute-start(bf16[512,256]{1,0:T(8,128)(2,1)S(1)} %slice.160), channel_id=1, source_target_pairs={{0,16},{4,20},{8,24},{12,28},{16,0},{20,4},{24,8},{28,12},{1,17},{... | collective-permute-start | bytes 786440 | tf_op jit(solution)/shard_map/ppermute | solution.py:552
  118.9 9.4 %collective-permute-start.29 = (bf16[1536,256]{1,0:T(8,128)(2,1)S(1)}, bf16[1536,256]{1,0:T(8,128)(2,1)S(1)}, u32[]{:S(2)}, u32[]{:S(2)}) collective-permute-start(bf16[1536,256]{1,0:T(8,128)(2,1)S(1)} %pack_out.2), channel_id=1, source_target_pairs={{0,4},{4,0},{8,12},{12,8},{16,20},{20,16},{24,28},{28,24},{1,5},{5... | collective-permute-start | bytes 2359304 | tf_op jit(solution)/shard_map/ppermute | solution.py:552
  131.7 10.4 %collective-permute-start.33 = (bf16[672,256]{1,0:T(8,128)(2,1)S(1)}, bf16[672,256]{1,0:T(8,128)(2,1)S(1)}, u32[]{:S(2)}, u32[]{:S(2)}) collective-permute-start(bf16[672,256]{1,0:T(8,128)(2,1)S(1)} %slice.163), channel_id=1, source_target_pairs={{0,8},{4,12},{8,0},{12,4},{16,24},{20,28},{24,16},{28,20},{1,9},{5... | collective-permute-start | bytes 1032200 | tf_op jit(solution)/shard_map/ppermute | solution.py:552
  159.9 17.1 %collective-permute-start.38 = (bf16[1024,256]{1,0:T(8,128)(2,1)S(1)}, bf16[1024,256]{1,0:T(8,128)(2,1)S(1)}, u32[]{:S(2)}, u32[]{:S(2)}) collective-permute-start(bf16[1024,256]{1,0:T(8,128)(2,1)S(1)} %get-tuple-element.205), channel_id=1, source_target_pairs={{0,16},{4,20},{8,24},{12,28},{16,0},{20,4},{24,8},{28,12},{1,17},{... | collective-permute-start | bytes 1572872 | tf_op jit(solution)/shard_map/ppermute | solution.py:552
  161.5 14.8 %collective-permute-start.37 = (bf16[1024,256]{1,0:T(8,128)(2,1)S(1)}, bf16[1024,256]{1,0:T(8,128)(2,1)S(1)}, u32[]{:S(2)}, u32[]{:S(2)}) collective-permute-start(bf16[1024,256]{1,0:T(8,128)(2,1)S(1)} %get-tuple-element.194), channel_id=1, source_target_pairs={{0,8},{4,12},{8,0},{12,4},{16,24},{20,28},{24,16},{28,20},{1,9},{5... | collective-permute-start | bytes 1572872 | tf_op jit(solution)/shard_map/ppermute | solution.py:552
  163.0 37.4 %collective-permute-start.42 = (bf16[1024,256]{1,0:T(8,128)(2,1)S(1)}, bf16[1024,256]{1,0:T(8,128)(2,1)S(1)}, u32[]{:S(2)}, u32[]{:S(2)}) collective-permute-start(bf16[1024,256]{1,0:T(8,128)(2,1)S(1)} %get-tuple-element.192), channel_id=1, source_target_pairs={{0,8},{4,12},{8,0},{12,4},{16,24},{20,28},{24,16},{28,20},{1,9},{5... | collective-permute-start | bytes 1572872 | tf_op jit(solution)/shard_map/ppermute | solution.py:552
  166.5 16.2 %collective-permute-start.44 = (bf16[2304,256]{1,0:T(8,128)(2,1)S(1)}, bf16[2304,256]{1,0:T(8,128)(2,1)S(1)}, u32[]{:S(2)}, u32[]{:S(2)}) collective-permute-start(bf16[2304,256]{1,0:T(8,128)(2,1)S(1)} %get-tuple-element.222), channel_id=1, source_target_pairs={{0,4},{4,0},{8,12},{12,8},{16,20},{20,16},{24,28},{28,24},{1,5},{5... | collective-permute-start | bytes 3538952 | tf_op jit(solution)/shard_map/ppermute | solution.py:552
  176.4 24.5 %collective-permute-start.43 = (bf16[1024,256]{1,0:T(8,128)(2,1)S(1)}, bf16[1024,256]{1,0:T(8,128)(2,1)S(1)}, u32[]{:S(2)}, u32[]{:S(2)}) collective-permute-start(bf16[1024,256]{1,0:T(8,128)(2,1)S(1)} %add.106), channel_id=1, source_target_pairs={{0,16},{4,20},{8,24},{12,28},{16,0},{20,4},{24,8},{28,12},{1,17},{... | collective-permute-start | bytes 1572872 | tf_op jit(solution)/shard_map/ppermute | solution.py:552
  185.5 26.0 %collective-permute-start.48 = (bf16[1024,256]{1,0:T(8,128)(2,1)S(1)}, bf16[1024,256]{1,0:T(8,128)(2,1)S(1)}, u32[]{:S(2)}, u32[]{:S(2)}) collective-permute-start(bf16[1024,256]{1,0:T(8,128)(2,1)S(1)} %get-tuple-element.228), channel_id=1, source_target_pairs={{0,16},{4,20},{8,24},{12,28},{16,0},{20,4},{24,8},{28,12},{1,17},{... | collective-permute-start | bytes 1572872 | tf_op jit(solution)/shard_map/ppermute | solution.py:552
  188.2 24.3 %collective-permute-start.47 = (bf16[1024,256]{1,0:T(8,128)(2,1)S(1)}, bf16[1024,256]{1,0:T(8,128)(2,1)S(1)}, u32[]{:S(2)}, u32[]{:S(2)}) collective-permute-start(bf16[1024,256]{1,0:T(8,128)(2,1)S(1)} %get-tuple-element.226), channel_id=1, source_target_pairs={{0,8},{4,12},{8,0},{12,4},{16,24},{20,28},{24,16},{28,20},{1,9},{5... | collective-permute-start | bytes 1572872 | tf_op jit(solution)/shard_map/ppermute | solution.py:552
  189.7 19.2 %collective-permute-start.45 = (bf16[576,256]{1,0:T(8,128)(2,1)S(1)}, bf16[576,256]{1,0:T(8,128)(2,1)S(1)}, u32[]{:S(2)}, u32[]{:S(2)}) collective-permute-start(bf16[576,256]{1,0:T(8,128)(2,1)S(1)} %slice.206), channel_id=1, source_target_pairs={{0,16},{4,20},{8,24},{12,28},{16,0},{20,4},{24,8},{28,12},{1,17},{... | collective-permute-start | bytes 884744 | tf_op jit(solution)/shard_map/ppermute | solution.py:552
  200.4 22.6 %collective-permute-start.52 = (bf16[1024,256]{1,0:T(8,128)(2,1)S(1)}, bf16[1024,256]{1,0:T(8,128)(2,1)S(1)}, u32[]{:S(2)}, u32[]{:S(2)}) collective-permute-start(bf16[1024,256]{1,0:T(8,128)(2,1)S(1)} %get-tuple-element.232), channel_id=1, source_target_pairs={{0,16},{4,20},{8,24},{12,28},{16,0},{20,4},{24,8},{28,12},{1,17},{... | collective-permute-start | bytes 1572872 | tf_op jit(solution)/shard_map/ppermute | solution.py:552
  201.0 22.0 %collective-permute-start.51 = (bf16[1024,256]{1,0:T(8,128)(2,1)S(1)}, bf16[1024,256]{1,0:T(8,128)(2,1)S(1)}, u32[]{:S(2)}, u32[]{:S(2)}) collective-permute-start(bf16[1024,256]{1,0:T(8,128)(2,1)S(1)} %add.107), channel_id=1, source_target_pairs={{0,8},{4,12},{8,0},{12,4},{16,24},{20,28},{24,16},{28,20},{1,9},{5... | collective-permute-start | bytes 1572872 | tf_op jit(solution)/shard_map/ppermute | solution.py:552
  209.1 14.7 %collective-permute-start.46 = (bf16[1024,256]{1,0:T(8,128)(2,1)S(1)}, bf16[1024,256]{1,0:T(8,128)(2,1)S(1)}, u32[]{:S(2)}, u32[]{:S(2)}) collective-permute-start(bf16[1024,256]{1,0:T(8,128)(2,1)S(1)} %add_convert_fusion.6), channel_id=1, source_target_pairs={{0,1},{1,2},{2,3},{3,0},{4,5},{5,6},{6,7},{7,4},{8,9},{9,10},{10,1... | collective-permute-start | bytes 1572872 | tf_op jit(solution)/shard_map/ppermute | solution.py:555
  212.7 10.3 %collective-permute-start.49 = (bf16[576,256]{1,0:T(8,128)(2,1)S(1)}, bf16[576,256]{1,0:T(8,128)(2,1)S(1)}, u32[]{:S(2)}, u32[]{:S(2)}) collective-permute-start(bf16[576,256]{1,0:T(8,128)(2,1)S(1)} %get-tuple-element.269), channel_id=1, source_target_pairs={{0,8},{4,12},{8,0},{12,4},{16,24},{20,28},{24,16},{28,20},{1,9},{5... | collective-permute-start | bytes 884744 | tf_op jit(solution)/shard_map/ppermute | solution.py:552
  213.3 10.5 %collective-permute-start.50 = (bf16[576,256]{1,0:T(8,128)(2,1)S(1)}, bf16[576,256]{1,0:T(8,128)(2,1)S(1)}, u32[]{:S(2)}, u32[]{:S(2)}) collective-permute-start(bf16[576,256]{1,0:T(8,128)(2,1)S(1)} %get-tuple-element.268), channel_id=1, source_target_pairs={{0,16},{4,20},{8,24},{12,28},{16,0},{20,4},{24,8},{28,12},{1,17},{... | collective-permute-start | bytes 884744 | tf_op jit(solution)/shard_map/ppermute | solution.py:552
  229.2 29.6 %collective-permute-start.55 = (bf16[1600,256]{1,0:T(8,128)(2,1)S(1)}, bf16[1600,256]{1,0:T(8,128)(2,1)S(1)}, u32[]{:S(2)}, u32[]{:S(2)}) collective-permute-start(bf16[1600,256]{1,0:T(8,128)(2,1)S(1)} %get-tuple-element.246), channel_id=1, source_target_pairs={{0,4},{4,0},{8,12},{12,8},{16,20},{20,16},{24,28},{28,24},{1,5},{5... | collective-permute-start | bytes 2457608 | tf_op jit(solution)/shard_map/ppermute | solution.py:552
  229.3 29.5 %collective-permute-start.53 = (bf16[304,1024]{1,0:T(8,128)(2,1)S(1)}, bf16[304,1024]{1,0:T(8,128)(2,1)S(1)}, u32[]{:S(2)}, u32[]{:S(2)}) collective-permute-start(bf16[304,1024]{1,0:T(8,128)(2,1)S(1)} %get-tuple-element.242), channel_id=1, source_target_pairs={{0,1},{1,2},{2,3},{3,0},{4,5},{5,6},{6,7},{7,4},{8,9},{9,10},{10,1... | collective-permute-start | bytes 1867784 | tf_op jit(solution)/shard_map/ppermute | solution.py:555
  231.5 14.0 %collective-permute-start.57 = (bf16[1024,256]{1,0:T(8,128)(2,1)S(1)}, bf16[1024,256]{1,0:T(8,128)(2,1)S(1)}, u32[]{:S(2)}, u32[]{:S(2)}) collective-permute-start(bf16[1024,256]{1,0:T(8,128)(2,1)S(1)} %add.111), channel_id=1, source_target_pairs={{0,16},{4,20},{8,24},{12,28},{16,0},{20,4},{24,8},{28,12},{1,17},{... | collective-permute-start | bytes 1572872 | tf_op jit(solution)/shard_map/ppermute | solution.py:552
  231.9 14.0 %collective-permute-start.56 = (bf16[1024,256]{1,0:T(8,128)(2,1)S(1)}, bf16[1024,256]{1,0:T(8,128)(2,1)S(1)}, u32[]{:S(2)}, u32[]{:S(2)}) collective-permute-start(bf16[1024,256]{1,0:T(8,128)(2,1)S(1)} %get-tuple-element.247), channel_id=1, source_target_pairs={{0,8},{4,12},{8,0},{12,4},{16,24},{20,28},{24,16},{28,20},{1,9},{5... | collective-permute-start | bytes 1572872 | tf_op jit(solution)/shard_map/ppermute | solution.py:552
  232.5 26.3 %collective-permute-start.54 = (bf16[1024,256]{1,0:T(8,128)(2,1)S(1)}, bf16[1024,256]{1,0:T(8,128)(2,1)S(1)}, u32[]{:S(2)}, u32[]{:S(2)}) collective-permute-start(bf16[1024,256]{1,0:T(8,128)(2,1)S(1)} %add_convert_fusion.5), channel_id=1, source_target_pairs={{0,1},{1,2},{2,3},{3,0},{4,5},{5,6},{6,7},{7,4},{8,9},{9,10},{10,1... | collective-permute-start | bytes 1572872 | tf_op jit(solution)/shard_map/ppermute | solution.py:555
  245.5 18.2 %collective-permute-start.61 = (bf16[1024,256]{1,0:T(8,128)(2,1)}, bf16[1024,256]{1,0:T(8,128)(2,1)}, u32[]{:S(2)}, u32[]{:S(2)}) collective-permute-start(bf16[1024,256]{1,0:T(8,128)(2,1)} %add.112), channel_id=1, source_target_pairs={{0,8},{4,12},{8,0},{12,4},{16,24},{20,28},{24,16},{28,20},{1,9},{5... | collective-permute-start | bytes 1572872 | tf_op jit(solution)/shard_map/ppermute | solution.py:552
  246.0 17.7 %collective-permute-start.62 = (bf16[1024,256]{1,0:T(8,128)(2,1)S(1)}, bf16[1024,256]{1,0:T(8,128)(2,1)}, u32[]{:S(2)}, u32[]{:S(2)}) collective-permute-start(bf16[1024,256]{1,0:T(8,128)(2,1)S(1)} %get-tuple-element.256), channel_id=1, source_target_pairs={{0,16},{4,20},{8,24},{12,28},{16,0},{20,4},{24,8},{28,12},{1,17},{... | collective-permute-start | bytes 1572872 | tf_op jit(solution)/shard_map/ppermute | solution.py:552
  259.9 17.0 %collective-permute-start.59 = (bf16[1024,256]{1,0:T(8,128)(2,1)}, bf16[1024,256]{1,0:T(8,128)(2,1)}, u32[]{:S(2)}, u32[]{:S(2)}) collective-permute-start(bf16[1024,256]{1,0:T(8,128)(2,1)} %add_convert_fusion.4), channel_id=1, source_target_pairs={{0,1},{1,2},{2,3},{3,0},{4,5},{5,6},{6,7},{7,4},{8,9},{9,10},{10,1... | collective-permute-start | bytes 1572872 | tf_op jit(solution)/shard_map/ppermute | solution.py:555
  261.3 27.6 %collective-permute-start.58 = (bf16[304,1024]{1,0:T(8,128)(2,1)}, bf16[304,1024]{1,0:T(8,128)(2,1)}, u32[]{:S(2)}, u32[]{:S(2)}) collective-permute-start(bf16[304,1024]{1,0:T(8,128)(2,1)} %add_convert_fusion.3), channel_id=1, source_target_pairs={{0,1},{1,2},{2,3},{3,0},{4,5},{5,6},{6,7},{7,4},{8,9},{9,10},{10,1... | collective-permute-start | bytes 1867784 | tf_op jit(solution)/shard_map/ppermute | solution.py:555
  290.1 16.5 %collective-permute-start.63 = (bf16[304,1024]{1,0:T(8,128)(2,1)S(1)}, bf16[304,1024]{1,0:T(8,128)(2,1)S(1)}, u32[]{:S(2)}, u32[]{:S(2)}) collective-permute-start(bf16[304,1024]{1,0:T(8,128)(2,1)S(1)} %add_convert_fusion.2), channel_id=1, source_target_pairs={{0,1},{1,2},{2,3},{3,0},{4,5},{5,6},{6,7},{7,4},{8,9},{9,10},{10,1... | collective-permute-start | bytes 1867784 | tf_op jit(solution)/shard_map/ppermute | solution.py:555
  (59 other events, 503.1 us)
